TPU v7x, 128 devices: a whole 4x4x4 slice. The times are simulated.
128 devices in a mesh: section: 2 (over core), group: 4 (over z), replica: 16 (over x, y).
Axes of the slice: x: 4, y: 4, z: 4, core: 2. Of those that a mesh axis runs over, the one named last changes fastest.
Arguments:
- tokens: bfloat16 [2, 16, 256, 896], P(None, 'replica', 'group'), may hold values from -6 to 6
- cotangent: bfloat16 [2, 16, 256, 896], P(None, 'replica', 'group'), may hold values from -6 to 6
- doc_lengths: int32 [2, 16, 5], P(None, 'replica'), may hold values from 1 to 193, 256 in all within a row
- w_qkv: bfloat16 [2, 896, 1152], P('section', 'group'), may hold values from -0.1875 to 0.1875
- b_qkv: bfloat16 [2, 1152], P('section', 'group'), may hold values from -3 to 3
- w_out: bfloat16 [2, 896, 896], P('section', 'group'), may hold values from -0.5 to 0.5
- w_gate: bfloat16 [2, 896, 4864], P('section', 'group'), may hold values from -0.1875 to 0.1875
- w_up: bfloat16 [2, 896, 4864], P('section', 'group'), may hold values from -0.1875 to 0.1875
- w_down: bfloat16 [2, 4864, 896], P('section', 'group'), may hold values from -0.15625 to 0.15625
- norm_attn: bfloat16 [2, 896], P('section', 'group'), may hold values from 0.5 to 1.5
- norm_ffn: bfloat16 [2, 896], P('section', 'group'), may hold values from 0.5 to 1.5
Outputs:
- acts: bfloat16 [2, 2, 16, 256, 896], P('section', None, 'replica', 'group')
- input_grads: float32 [2, 2, 16, 256, 896], P('section', None, 'replica', 'group')
- grad_w_qkv: float32 [2, 896, 1152], P('section', 'group')
- grad_b_qkv: float32 [2, 1152], P('section', 'group')
- grad_w_out: float32 [2, 896, 896], P('section', 'group')
- grad_w_gate: float32 [2, 896, 4864], P('section', 'group')
- grad_w_up: float32 [2, 896, 4864], P('section', 'group')
- grad_w_down: float32 [2, 4864, 896], P('section', 'group')
- grad_norm_attn: float32 [2, 896], P('section', 'group')
- grad_norm_ffn: float32 [2, 896], P('section', 'group')
Inputs may be any that keep to these rules, and one draw needn't show every extreme that they name: `doc_lengths`: each row's 5 lengths sum to 256; in every row one document has exactly 193 tokens.
All inputs are finite; a program needn't handle non-finite values.
Results may differ from a plain program's by a relative error of at most 0.025.
Values may be sent and summed in bfloat16 or wider, within the bound.
A program may use at most 192 MiB of HBM per device.

v0:
```python
import jax
import jax.numpy as jnp
from jax import lax
from jax.sharding import PartitionSpec as P

HEADS = 14
KV_HEADS = 2
HEAD_DIM = 64


eps = 1e-06
rope_base = 1000000.0


def shifted(value, axis, steps):
    count = lax.axis_size(axis)
    leading, last = (max(0, -steps), min(count, count - steps))
    return lax.ppermute(value, axis, [(source, source + steps) for source in range(leading, last)])


def rms_scale(values):
    return lax.rsqrt(jnp.mean(values * values, axis=-1, keepdims=True) + eps)


def rotate_half(values):
    half_len = values.shape[-1] // 2
    return jnp.concatenate([-values[..., half_len:], values[..., :half_len]], axis=-1)


def norm_back(grad_norm, values, scale_rows, gain_vec):
    scaled = grad_norm * gain_vec
    row_inner = jnp.mean(scaled * values, axis=-1, keepdims=True)
    grad_in = scale_rows * (scaled - values * scale_rows * scale_rows * row_inner)
    grad_gain = jnp.sum(grad_norm * values * scale_rows, axis=0)
    return (grad_in, grad_gain)


def doc_tables(doc_lens, span_len, row_len, group_at):
    doc_ends = jnp.cumsum(doc_lens)
    doc_starts = doc_ends - doc_lens
    row_spots = jnp.arange(row_len, dtype=jnp.int32)
    segment = jnp.sum((doc_ends[None, :] <= row_spots[:, None]).astype(jnp.int32), axis=1)
    doc_pick = segment[:, None] == jnp.arange(doc_lens.shape[0], dtype=jnp.int32)[None, :]
    doc_begin = jnp.sum(jnp.where(doc_pick, doc_starts[None, :], 0), axis=1)
    first_row = group_at * span_len
    own_segment = lax.dynamic_slice_in_dim(segment, first_row, span_len)
    own_spots = lax.dynamic_slice_in_dim(row_spots, first_row, span_len)
    own_begin = lax.dynamic_slice_in_dim(doc_begin, first_row, span_len)
    allowed = (own_segment[:, None] == segment[None, :]) & (
        row_spots[None, :] <= own_spots[:, None]
    )
    inv_freqs = rope_base ** (-jnp.arange(0, HEAD_DIM, 2, dtype=jnp.float32) / HEAD_DIM)
    angles = (own_spots - own_begin).astype(jnp.float32)[:, None] * inv_freqs[None, :]
    angles = jnp.concatenate([angles, angles], axis=1)
    return (allowed, jnp.cos(angles)[:, None, :], jnp.sin(angles)[:, None, :])


def split_kv(all_kv):
    row_len = all_kv.shape[0]
    kv_width = KV_HEADS * HEAD_DIM
    key_rows = all_kv[:, :kv_width].reshape(row_len, KV_HEADS, HEAD_DIM)
    value_rows = all_kv[:, kv_width:].reshape(row_len, KV_HEADS, HEAD_DIM)
    return (key_rows, value_rows)


def score_block(query_rot, key_rows, allowed):
    grouped = query_rot.reshape(query_rot.shape[0], KV_HEADS, HEADS // KV_HEADS, HEAD_DIM)
    scores = jnp.einsum(
        "ikgd,jkd->kgij", grouped, key_rows, preferred_element_type=jnp.float32
    ) * HEAD_DIM ** (-0.5)
    return jnp.where(allowed[None, None], scores, -jnp.inf)


def layer_forward(entering, weights, allowed, cosine, sine_table):
    w_qkv, b_qkv, w_out, w_gate, w_up, w_down, gain_attn, gain_ffn = weights
    span_len = entering.shape[0]
    q_width = HEADS * HEAD_DIM
    kv_width = KV_HEADS * HEAD_DIM
    values = entering.astype(jnp.float32)
    scale_one = rms_scale(values)
    normed_one = (values * scale_one * gain_attn.astype(jnp.float32)).astype(jnp.bfloat16)
    mixed_qkv = jnp.dot(normed_one, w_qkv, preferred_element_type=jnp.float32) + b_qkv.astype(
        jnp.float32
    )
    query_pre = mixed_qkv[:, :q_width].reshape(span_len, HEADS, HEAD_DIM)
    key_pre = mixed_qkv[:, q_width : q_width + kv_width].reshape(span_len, KV_HEADS, HEAD_DIM)
    query_rot = (query_pre * cosine + rotate_half(query_pre) * sine_table).astype(jnp.bfloat16)
    key_rot = (key_pre * cosine + rotate_half(key_pre) * sine_table).astype(jnp.bfloat16)
    local_kv = jnp.concatenate(
        [
            key_rot.reshape(span_len, kv_width),
            mixed_qkv[:, q_width + kv_width :].astype(jnp.bfloat16),
        ],
        axis=1,
    )
    all_kv = lax.all_gather(local_kv, "group", axis=0, tiled=True)
    key_rows, value_rows = split_kv(all_kv)
    scores = score_block(query_rot, key_rows, allowed)
    row_top = jnp.max(scores, axis=-1, keepdims=True)
    log_total = row_top + jnp.log(jnp.sum(jnp.exp(scores - row_top), axis=-1, keepdims=True))
    attn_probs = jnp.exp(scores - log_total).astype(jnp.bfloat16)
    context = jnp.einsum(
        "kgij,jkd->ikgd", attn_probs, value_rows, preferred_element_type=jnp.float32
    )
    context = context.reshape(span_len, q_width).astype(jnp.bfloat16)
    hidden = values + jnp.dot(context, w_out, preferred_element_type=jnp.float32)
    scale_two = rms_scale(hidden)
    normed_two = (hidden * scale_two * gain_ffn.astype(jnp.float32)).astype(jnp.bfloat16)
    gate_proj = jnp.dot(normed_two, w_gate, preferred_element_type=jnp.float32)
    up_proj = jnp.dot(normed_two, w_up, preferred_element_type=jnp.float32)
    activated = (jax.nn.silu(gate_proj) * up_proj).astype(jnp.bfloat16)
    output = hidden + jnp.dot(activated, w_down, preferred_element_type=jnp.float32)
    kept_state = (
        values,
        scale_one,
        normed_one,
        query_rot,
        all_kv,
        log_total,
        context,
        hidden,
        scale_two,
        normed_two,
        gate_proj,
        up_proj,
        activated,
    )
    return (output.astype(jnp.bfloat16), kept_state)


def layer_backward(grad_out, kept_state, weights, allowed, cosine, sine_table):
    (
        values,
        scale_one,
        normed_one,
        query_rot,
        all_kv,
        log_total,
        context,
        hidden,
        scale_two,
        normed_two,
        gate_proj,
        up_proj,
        activated,
    ) = kept_state
    w_qkv, b_qkv, w_out, w_gate, w_up, w_down, gain_attn, gain_ffn = weights
    span_len = grad_out.shape[0]
    row_len = all_kv.shape[0]
    q_width = HEADS * HEAD_DIM
    kv_width = KV_HEADS * HEAD_DIM
    grad_mlp = grad_out.astype(jnp.bfloat16)
    grad_act = jnp.einsum("id,fd->if", grad_mlp, w_down, preferred_element_type=jnp.float32)
    sigma_gate = jax.nn.sigmoid(gate_proj)
    silu_gate = gate_proj * sigma_gate
    grad_gate = (grad_act * up_proj * sigma_gate * (1.0 + gate_proj * (1.0 - sigma_gate))).astype(
        jnp.bfloat16
    )
    grad_up = (grad_act * silu_gate).astype(jnp.bfloat16)
    grad_norm_two = jnp.einsum("if,df->id", grad_gate, w_gate, preferred_element_type=jnp.float32)
    grad_norm_two = grad_norm_two + jnp.einsum(
        "if,df->id", grad_up, w_up, preferred_element_type=jnp.float32
    )
    back_two, grad_gain_ffn = norm_back(
        grad_norm_two, hidden, scale_two, gain_ffn.astype(jnp.float32)
    )
    grad_hidden = grad_out + back_two
    grad_attn = grad_hidden.astype(jnp.bfloat16)
    grad_context = jnp.einsum(
        "id,ed->ie", grad_attn, w_out, preferred_element_type=jnp.float32
    ).astype(jnp.bfloat16)
    grad_context = grad_context.reshape(span_len, KV_HEADS, HEADS // KV_HEADS, HEAD_DIM)
    key_rows, value_rows = split_kv(all_kv)
    grouped = query_rot.reshape(span_len, KV_HEADS, HEADS // KV_HEADS, HEAD_DIM)
    attn_probs = jnp.exp(score_block(query_rot, key_rows, allowed) - log_total)
    grad_probs = jnp.einsum(
        "ikgd,jkd->kgij", grad_context, value_rows, preferred_element_type=jnp.float32
    )
    row_inner = jnp.sum(attn_probs * grad_probs, axis=-1, keepdims=True)
    grad_scores = (attn_probs * (grad_probs - row_inner)).astype(jnp.bfloat16)
    score_scale = HEAD_DIM ** (-0.5)
    grad_query = jnp.einsum(
        "kgij,jkd->ikgd", grad_scores, key_rows, preferred_element_type=jnp.float32
    )
    grad_query = grad_query.reshape(span_len, HEADS, HEAD_DIM) * score_scale
    grad_key_all = (
        jnp.einsum("kgij,ikgd->jkd", grad_scores, grouped, preferred_element_type=jnp.float32)
        * score_scale
    )
    grad_value_all = jnp.einsum(
        "kgij,ikgd->jkd",
        attn_probs.astype(jnp.bfloat16),
        grad_context,
        preferred_element_type=jnp.float32,
    )
    grad_kv_all = jnp.concatenate(
        [grad_key_all.reshape(row_len, kv_width), grad_value_all.reshape(row_len, kv_width)], axis=1
    )
    grad_kv = lax.psum_scatter(
        grad_kv_all.astype(jnp.bfloat16), "group", scatter_dimension=0, tiled=True
    ).astype(jnp.float32)
    grad_key = grad_kv[:, :kv_width].reshape(span_len, KV_HEADS, HEAD_DIM)
    query_back = grad_query * cosine - rotate_half(grad_query * sine_table)
    key_back = grad_key * cosine - rotate_half(grad_key * sine_table)
    grad_mixed = jnp.concatenate(
        [
            query_back.reshape(span_len, q_width),
            key_back.reshape(span_len, kv_width),
            grad_kv[:, kv_width:],
        ],
        axis=1,
    ).astype(jnp.bfloat16)
    grad_bias = jnp.sum(grad_mixed.astype(jnp.float32), axis=0)
    grad_norm_one = jnp.einsum("ie,de->id", grad_mixed, w_qkv, preferred_element_type=jnp.float32)
    back_one, grad_gain_attn = norm_back(
        grad_norm_one, values, scale_one, gain_attn.astype(jnp.float32)
    )
    grad_in = grad_hidden + back_one
    pieces = (
        grad_mixed,
        grad_attn,
        grad_gate,
        grad_up,
        grad_mlp,
        grad_bias,
        grad_gain_attn,
        grad_gain_ffn,
    )
    return (grad_in, pieces)


def flat_rows(stacked_part):
    return stacked_part.reshape(-1, stacked_part.shape[-1])


def outer_sum(left, right):
    return jnp.einsum("id,ie->de", left, right, preferred_element_type=jnp.float32)


def on_device(
    tokens, cotangent, doc_lengths, w_qkv, b_qkv, w_out, w_gate, w_up, w_down, norm_attn, norm_ffn
):
    section_at = lax.axis_index("section")
    group_at = lax.axis_index("group")
    micro_count = tokens.shape[0]
    span_len = tokens.shape[2]
    width = tokens.shape[3]
    group_count = lax.axis_size("group")
    row_len = span_len * group_count
    gathered = (
        lax.all_gather(w_qkv, "group", axis=1, tiled=True),
        lax.all_gather(b_qkv, "group", axis=1, tiled=True),
        lax.all_gather(w_out, "group", axis=1, tiled=True),
        lax.all_gather(w_gate, "group", axis=1, tiled=True),
        lax.all_gather(w_up, "group", axis=1, tiled=True),
        lax.all_gather(w_down, "group", axis=1, tiled=True),
        lax.all_gather(norm_attn, "group", axis=1, tiled=True),
        lax.all_gather(norm_ffn, "group", axis=1, tiled=True),
    )
    weights = tuple((member[0] for member in gathered))
    tables = [
        doc_tables(doc_lengths[batch_idx, 0], span_len, row_len, group_at)
        for batch_idx in range(micro_count)
    ]
    allowed_all = jnp.stack([table_set[0] for table_set in tables])
    cosine_all = jnp.stack([table_set[1] for table_set in tables])
    sine_all = jnp.stack([table_set[2] for table_set in tables])
    previous = jnp.zeros((span_len, width), jnp.bfloat16)
    section_outs = []
    kept_list = []
    for tick_at in range(micro_count + 1):
        arrived = shifted(previous, "section", 1) if tick_at > 0 else previous
        own_rows = tokens[min(tick_at, micro_count - 1), 0]
        entering = jnp.where(section_at == 0, own_rows, arrived)
        batch_at = jnp.clip(tick_at - section_at, 0, micro_count - 1)
        previous, kept_state = layer_forward(
            entering, weights, allowed_all[batch_at], cosine_all[batch_at], sine_all[batch_at]
        )
        section_outs.append(previous)
        kept_list.append(kept_state)
    stacked = jax.tree.map(lambda *members: jnp.stack(members), *kept_list)
    grad_prev = jnp.zeros((span_len, width), jnp.bfloat16)
    grad_list = []
    piece_list = []
    for tick_at in range(micro_count + 1):
        arrived = shifted(grad_prev, "section", -1) if tick_at > 0 else grad_prev
        own_grad = cotangent[min(tick_at, micro_count - 1), 0]
        incoming = jnp.where(section_at == 1, own_grad, arrived).astype(jnp.float32)
        batch_at = jnp.clip(tick_at + section_at - 1, 0, micro_count - 1)
        fwd_tick = jnp.clip(tick_at + 2 * section_at - 1, 0, micro_count)
        kept_state = jax.tree.map(lambda member: member[fwd_tick], stacked)
        grad_in, pieces = layer_backward(
            incoming,
            kept_state,
            weights,
            allowed_all[batch_at],
            cosine_all[batch_at],
            sine_all[batch_at],
        )
        grad_prev = grad_in.astype(jnp.bfloat16)
        grad_list.append(jnp.where(section_at == 1, grad_prev.astype(jnp.float32), grad_in))
        piece_list.append(pieces)
    stacked_pieces = jax.tree.map(lambda *members: jnp.stack(members), *piece_list)
    kept_valid = jax.tree.map(
        lambda member: lax.dynamic_slice_in_dim(member, section_at, micro_count, 0), stacked
    )
    piece_valid = jax.tree.map(
        lambda member: lax.dynamic_slice_in_dim(member, 1 - section_at, micro_count, 0),
        stacked_pieces,
    )
    normed_one, context, normed_two, activated = (
        kept_valid[2],
        kept_valid[6],
        kept_valid[9],
        kept_valid[12],
    )
    (
        grad_mixed,
        grad_attn,
        grad_gate,
        grad_up,
        grad_mlp,
        grad_bias,
        grad_gain_attn,
        grad_gain_ffn,
    ) = piece_valid
    gain_attn_sum = jnp.sum(grad_gain_attn, axis=0)[None]
    gain_ffn_sum = jnp.sum(grad_gain_ffn, axis=0)[None]
    grad_w_qkv = outer_sum(flat_rows(normed_one), flat_rows(grad_mixed))
    grad_w_out = outer_sum(flat_rows(context), flat_rows(grad_attn))
    grad_w_gate = outer_sum(flat_rows(normed_two), flat_rows(grad_gate))
    grad_w_up = outer_sum(flat_rows(normed_two), flat_rows(grad_up))
    grad_w_down = outer_sum(flat_rows(activated), flat_rows(grad_mlp))
    grad_terms = (
        grad_w_qkv[None],
        jnp.sum(grad_bias, axis=0)[None],
        grad_w_out[None],
        grad_w_gate[None],
        grad_w_up[None],
        grad_w_down[None],
        gain_attn_sum,
        gain_ffn_sum,
    )
    owned_rows = (
        lax.psum_scatter(
            grad_terms[0].astype(jnp.bfloat16), "group", scatter_dimension=1, tiled=True
        ).astype(jnp.float32),
        lax.psum_scatter(
            grad_terms[1].astype(jnp.bfloat16), "group", scatter_dimension=1, tiled=True
        ).astype(jnp.float32),
        lax.psum_scatter(
            grad_terms[2].astype(jnp.bfloat16), "group", scatter_dimension=1, tiled=True
        ).astype(jnp.float32),
        lax.psum_scatter(
            grad_terms[3].astype(jnp.bfloat16), "group", scatter_dimension=1, tiled=True
        ).astype(jnp.float32),
        lax.psum_scatter(
            grad_terms[4].astype(jnp.bfloat16), "group", scatter_dimension=1, tiled=True
        ).astype(jnp.float32),
        lax.psum_scatter(
            grad_terms[5].astype(jnp.bfloat16), "group", scatter_dimension=1, tiled=True
        ).astype(jnp.float32),
        lax.psum_scatter(
            grad_terms[6].astype(jnp.bfloat16), "group", scatter_dimension=1, tiled=True
        ).astype(jnp.float32),
        lax.psum_scatter(
            grad_terms[7].astype(jnp.bfloat16), "group", scatter_dimension=1, tiled=True
        ).astype(jnp.float32),
    )
    totals = (
        lax.psum(owned_rows[0].astype(jnp.bfloat16), "replica").astype(jnp.float32),
        lax.psum(owned_rows[1].astype(jnp.bfloat16), "replica").astype(jnp.float32),
        lax.psum(owned_rows[2].astype(jnp.bfloat16), "replica").astype(jnp.float32),
        lax.psum(owned_rows[3].astype(jnp.bfloat16), "replica").astype(jnp.float32),
        lax.psum(owned_rows[4].astype(jnp.bfloat16), "replica").astype(jnp.float32),
        lax.psum(owned_rows[5].astype(jnp.bfloat16), "replica").astype(jnp.float32),
        lax.psum(owned_rows[6].astype(jnp.bfloat16), "replica").astype(jnp.float32),
        lax.psum(owned_rows[7].astype(jnp.bfloat16), "replica").astype(jnp.float32),
    )
    acts = lax.dynamic_slice_in_dim(jnp.stack(section_outs), section_at, micro_count, 0)
    input_grads = lax.dynamic_slice_in_dim(jnp.stack(grad_list), 1 - section_at, micro_count, 0)
    return (
        acts[None, :, None],
        input_grads[None, :, None],
        totals[0],
        totals[1],
        totals[2],
        totals[3],
        totals[4],
        totals[5],
        totals[6],
        totals[7],
    )


def solution(mesh):
    return jax.shard_map(
        on_device,
        mesh=mesh,
        in_specs=(
            P(None, "replica", "group", None),
            P(None, "replica", "group", None),
            P(None, "replica", None),
            P("section", "group", None),
            P("section", "group"),
            P("section", "group", None),
            P("section", "group", None),
            P("section", "group", None),
            P("section", "group", None),
            P("section", "group"),
            P("section", "group"),
        ),
        out_specs=(
            P("section", None, "replica", "group", None),
            P("section", None, "replica", "group", None),
            P("section", "group", None),
            P("section", "group"),
            P("section", "group", None),
            P("section", "group", None),
            P("section", "group", None),
            P("section", "group", None),
            P("section", "group"),
            P("section", "group"),
        ),
        check_vma=False,
    )
```

profile of v0, /device:TPU:0, one launch (start us, length us, event | category | flops | bytes accessed | tf_op | source)
XLA Modules:
  0.0 1147.8 jit_solution(3509440849576723521)
XLA Ops:
  14.0 11.9 %all-reduce.5 = (bf16[1152]{0:T(1024)(128)(2,1)S(1)}, bf16[896]{0:T(1024)(128)(2,1)S(1)}, bf16[896]{0:T(1024)(128)(2,1)S(1)}) all-reduce(bf16[1152]{0:T(1024)(128)(2,1)S(1)} %dynamic-update-slice.1, bf16[896]{0:T(1024)(128)(2,1)S(1)} %dynamic-update-slice, ...), channel_id=1, replica_groups=mesh['section'=2,'group'=4,'replica'=16] {'group'}, use_global_device_ids=true, to_apply=%add.1 | all-reduce | flops 2944 | bytes 11776
  35.9 7.1 all-gather.6.cloned.1.call-done
  46.9 12.1 %all_gather.36 = bf16[256,256]{1,0:T(8,128)(2,1)S(1)} all-gather(bf16[64,256]{1,0:T(8,128)(2,1)S(1)} %pad_maximum_fusion.23), channel_id=1, replica_groups=mesh['section'=2,'group'=4,'replica'=16] {'group'}, dimensions={0}, use_global_device_ids=true | all-gather | bytes 163840 | tf_op jit(solution)/shard_map/all_gather | solution.py:96
  62.9 8.8 all-gather.8.cloned.1.call-done
  74.2 85.0 %all-gather.10.cloned.1.call-done = bf16[1,896,4864]{2,1,0:T(8,128)(2,1)} async-done(((bf16[1,224,4864]{2,1,0:T(8,128)(2,1)}), bf16[1,896,4864]{2,1,0:T(8,128)(2,1)}) %all-gather.10.cloned.1.call-update) | async-done | bytes 8716304 | tf_op jit(solution)/shard_map/all_gather | solution.py:254
  164.1 83.6 %all-gather.12.cloned.1.call-done = bf16[1,896,4864]{2,1,0:T(8,128)(2,1)} async-done(((bf16[1,224,4864]{2,1,0:T(8,128)(2,1)}), bf16[1,896,4864]{2,1,0:T(8,128)(2,1)}) %all-gather.12.cloned.1.call-update) | async-done | bytes 8716304 | tf_op jit(solution)/shard_map/all_gather | solution.py:255
  247.7 5.9 multiply_convert_fusion.2
  253.7 82.6 %all-gather.14.cloned.1.call-done = bf16[1,4864,896]{2,1,0:T(8,128)(2,1)} async-done(((bf16[1,1216,896]{2,1,0:T(8,128)(2,1)}), bf16[1,4864,896]{2,1,0:T(8,128)(2,1)}) %all-gather.14.cloned.1.call-update) | async-done | bytes 8716304 | tf_op jit(solution)/shard_map/all_gather | solution.py:256
  336.3 5.2 fusion.149
  354.1 12.1 %all_gather.42 = bf16[256,256]{1,0:T(8,128)(2,1)S(1)} all-gather(bf16[64,256]{1,0:T(8,128)(2,1)S(1)} %pad_maximum_fusion.24), channel_id=1, replica_groups=mesh['section'=2,'group'=4,'replica'=16] {'group'}, dimensions={0}, use_global_device_ids=true | all-gather | bytes 163840 | tf_op jit(solution)/shard_map/all_gather | solution.py:96
  406.8 12.4 %all_gather.43 = bf16[256,256]{1,0:T(8,128)(2,1)S(1)} all-gather(bf16[64,256]{1,0:T(8,128)(2,1)S(1)} %pad_maximum_fusion.25), channel_id=1, replica_groups=mesh['section'=2,'group'=4,'replica'=16] {'group'}, dimensions={0}, use_global_device_ids=true | all-gather | bytes 163840 | tf_op jit(solution)/shard_map/all_gather | solution.py:96
  453.9 8.6 fusion.112
  481.4 14.2 %reduce-scatter.18.cloned.1.call-done = bf16[64,256]{1,0:T(8,128)(2,1)} async-done(((bf16[256,256]{1,0:T(8,128)(2,1)}), bf16[64,256]{1,0:T(8,128)(2,1)}) %reduce-scatter.18.cloned.1.call-update) | async-done | bytes 32784 | tf_op jit(solution)/shard_map/reduce_scatter | solution.py:199
  506.5 7.0 fusion.103
  513.6 6.7 fusion.14
  534.2 15.2 %reduce-scatter.20.cloned.1.call-done = bf16[64,256]{1,0:T(8,128)(2,1)} async-done(((bf16[256,256]{1,0:T(8,128)(2,1)}), bf16[64,256]{1,0:T(8,128)(2,1)}) %reduce-scatter.20.cloned.1.call-update) | async-done | bytes 32784 | tf_op jit(solution)/shard_map/reduce_scatter | solution.py:199
  559.7 7.0 fusion.94
  566.8 6.7 fusion.12
  597.1 7.2 reduce-scatter.22.cloned.1.call-done
  611.3 7.1 fusion.38
  620.6 6.9 fusion.37
  628.8 7.1 fusion.36
  641.1 24.2 %reduce-scatter.24.cloned.1.call-done = bf16[1,224,1152]{2,1,0:T(8,128)(2,1)} async-done(((bf16[1,896,1152]{2,1,0:T(8,128)(2,1)}), bf16[1,224,1152]{2,1,0:T(8,128)(2,1)}) %reduce-scatter.24.cloned.1.call-update) | async-done | bytes 516112 | tf_op jit(solution)/shard_map/reduce_scatter | solution.py:345
  665.3 85.5 %reduce-scatter.32.cloned.1.call-done = bf16[1,1216,896]{2,1,0:T(8,128)(2,1)} async-done(((bf16[1,4864,896]{2,1,0:T(8,128)(2,1)}), bf16[1,1216,896]{2,1,0:T(8,128)(2,1)}) %reduce-scatter.32.cloned.1.call-update) | async-done | bytes 2179088 | tf_op jit(solution)/shard_map/reduce_scatter | solution.py:360
  750.7 85.5 %reduce-scatter.30.cloned.1.call-done = bf16[1,224,4864]{2,1,0:T(8,128)(2,1)} async-done(((bf16[1,896,4864]{2,1,0:T(8,128)(2,1)}), bf16[1,224,4864]{2,1,0:T(8,128)(2,1)}) %reduce-scatter.30.cloned.1.call-update) | async-done | bytes 2179088 | tf_op jit(solution)/shard_map/reduce_scatter | solution.py:357
  836.2 85.5 %reduce-scatter.28.cloned.1.call-done = bf16[1,224,4864]{2,1,0:T(8,128)(2,1)} async-done(((bf16[1,896,4864]{2,1,0:T(8,128)(2,1)}), bf16[1,224,4864]{2,1,0:T(8,128)(2,1)}) %reduce-scatter.28.cloned.1.call-update) | async-done | bytes 2179088 | tf_op jit(solution)/shard_map/reduce_scatter | solution.py:354
  922.8 5.1 fusion.164
  928.8 16.3 %reduce-scatter.38.cloned.1.call-done = bf16[224,1]{1,0:T(8,128)(2,1)} async-done(((bf16[896,1]{1,0:T(8,128)(2,1)}), bf16[224,1]{1,0:T(8,128)(2,1)}) %reduce-scatter.38.cloned.1.call-update) | async-done | bytes 464
  946.9 21.3 %reduce-scatter.36.cloned.1.call-done = bf16[224,1]{1,0:T(8,128)(2,1)} async-done(((bf16[896,1]{1,0:T(8,128)(2,1)}), bf16[224,1]{1,0:T(8,128)(2,1)}) %reduce-scatter.36.cloned.1.call-update) | async-done | bytes 464
  969.1 22.7 %reduce-scatter.34.cloned.1.call-done = bf16[288,1]{1,0:T(8,128)(2,1)} async-done(((bf16[1152,1]{1,0:T(8,128)(2,1)}), bf16[288,1]{1,0:T(8,128)(2,1)}) %reduce-scatter.34.cloned.1.call-update) | async-done | bytes 592
  992.8 41.7 %all-reduce.3 = (bf16[1,288]{1,0:T(2,128)(2,1)S(1)}, bf16[1,224]{1,0:T(2,128)(2,1)S(1)}, bf16[1,224]{1,0:T(2,128)(2,1)S(1)}) all-reduce(bf16[1,288]{1,0:T(2,128)(2,1)S(1)} %copy.310, bf16[1,224]{1,0:T(2,128)(2,1)S(1)} %copy.312, bf16[1,224]{1,0:T(2,128)(2,1)S(1)} %copy.314), channel_id=1, replica_groups=mesh['section'=2,'group'=4,'replica'=16] {'replica'}, use_global_device_ids=true, to_apply=%region_37.38 | all-reduce | flops 736 | bytes 2944 | tf_op jit(solution)/shard_map/psum | solution.py:372
  1036.2 93.1 %all-reduce.8.cloned.1.call-done = (bf16[1,224,1152]{2,1,0:T(8,128)(2,1)}, bf16[1,224,896]{2,1,0:T(8,128)(2,1)}, bf16[1,224,4864]{2,1,0:T(8,128)(2,1)}, bf16[1,2...) async-done(((bf16[1,224,1152]{2,1,0:T(8,128)(2,1)}, bf16[1,224,896]{2,1,0:T(8,128)(2,1)}, bf16[1,224,4864]{2,1,0:T(8,128)(2,1)}, bf16[1,224,4864]{2,1,0:T(8,128)(2,1)}, ...) | async-done | bytes 7454736 | tf_op jit(solution)/shard_map/psum | solution.py:371
  (776 shorter events, 227.7 us)
Async XLA Ops:
  7.2 35.8 %all-gather.6.cloned.1.call-start = ((), (), s32[]{:S(2)}) async-start(), calls=%async_computation.11 | async-start | bytes 2580480 | tf_op jit(solution)/shard_map/all_gather | solution.py:251
  7.9 63.8 %all-gather.8.cloned.1.call-start = ((), (), s32[]{:S(2)}) async-start(), calls=%async_computation.12 | async-start | bytes 2007040 | tf_op jit(solution)/shard_map/all_gather | solution.py:253
  8.7 150.6 %all-gather.10.cloned.1.call-start = ((), (), s32[]{:S(2)}) async-start(), calls=%async_computation.13 | async-start | bytes 10895360 | tf_op jit(solution)/shard_map/all_gather | solution.py:254
  9.4 238.3 %all-gather.12.cloned.1.call-start = ((), (), s32[]{:S(2)}) async-start(), calls=%async_computation.14 | async-start | bytes 10895360 | tf_op jit(solution)/shard_map/all_gather | solution.py:255
  10.0 326.2 %all-gather.14.cloned.1.call-start = ((), (), s32[]{:S(2)}) async-start(), calls=%async_computation.15 | async-start | bytes 10895360 | tf_op jit(solution)/shard_map/all_gather | solution.py:256
  10.6 484.9 %reduce-scatter.18.cloned.1.call-start = ((), (), s32[]{:S(2)}) async-start(), calls=%async_computation.16 | async-start | bytes 163840 | tf_op jit(solution)/shard_map/reduce_scatter | solution.py:199
  62.9 96.4 %copy-start.62 = (bf16[2,64,7,64]{3,1,2,0:T(8,128)(2,1)}, bf16[2,64,7,64]{3,1,2,0:T(8,128)(2,1)S(1)}, u32[]{:S(2)}) copy-start(bf16[2,64,7,64]{3,1,2,0:T(8,128)(2,1)S(1)} %convolution_convert_fusion.2) | copy-start | bytes 344068
  73.7 262.6 %copy-start.9 = (f32[64,896]{1,0:T(8,128)}, f32[64,896]{1,0:T(8,128)S(1)}, u32[]{:S(2)}) copy-start(f32[64,896]{1,0:T(8,128)S(1)} %get-tuple-element.175) | copy-start | bytes 688132
  74.2 173.5 %copy-start.154 = (f32[64]{0:T(128)}, f32[64]{0:T(128)S(1)}, u32[]{:S(2)}) copy-start(f32[64]{0:T(128)S(1)} %get-tuple-element.163) | copy-start | bytes 772
  253.6 82.6 %copy-start.20 = (bf16[64,4864]{1,0:T(8,128)(2,1)}, bf16[64,4864]{1,0:T(8,128)(2,1)S(1)}, u32[]{:S(2)}) copy-start(bf16[64,4864]{1,0:T(8,128)(2,1)S(1)} %get-tuple-element.176) | copy-start | bytes 1867780
  341.5 3.0 collective-permute-start
  394.7 2.4 collective-permute-start.1
  444.2 25.7 %copy-start.15 = (f32[3,64,896]{2,1,0:T(8,128)}, f32[3,64,896]{2,1,0:T(8,128)S(1)}, u32[]{:S(2)}) copy-start(f32[3,64,896]{2,1,0:T(8,128)S(1)} %pad_maximum_fusion.3) | copy-start | bytes 2064388
  475.2 74.2 %reduce-scatter.20.cloned.1.call-start = ((), (), s32[]{:S(2)}) async-start(), calls=%async_computation.17 | async-start | bytes 163840 | tf_op jit(solution)/shard_map/reduce_scatter | solution.py:199
  476.9 24.6 %copy-start.12 = (f32[3,64,896]{2,1,0:T(8,128)}, f32[3,64,896]{2,1,0:T(8,128)S(1)}, u32[]{:S(2)}) copy-start(f32[3,64,896]{2,1,0:T(8,128)S(1)} %pad_maximum_fusion.4) | copy-start | bytes 2064388
  502.4 3.2 collective-permute-start.2
  528.8 75.5 %reduce-scatter.22.cloned.1.call-start = ((), (), s32[]{:S(2)}) async-start(), calls=%async_computation.18 | async-start | bytes 163840 | tf_op jit(solution)/shard_map/reduce_scatter | solution.py:199
  529.4 20.8 %copy-start.130 = (f32[64,64]{1,0:T(8,128)S(1)}, f32[64,64]{1,0:T(8,128)}, u32[]{:S(2)}) copy-start(f32[64,64]{1,0:T(8,128)} %get-tuple-element.112) | copy-start | bytes 49156
  530.4 21.0 %copy-start.123 = (f32[64,128]{1,0:T(8,128)S(1)}, f32[64,128]{1,0:T(8,128)}, u32[]{:S(2)}) copy-start(f32[64,128]{1,0:T(8,128)} %mul.1188) | copy-start | bytes 98308
  530.4 21.8 %copy-start.13 = (f32[3,64,896]{2,1,0:T(8,128)S(1)}, f32[3,64,896]{2,1,0:T(8,128)}, u32[]{:S(2)}) copy-start(f32[3,64,896]{2,1,0:T(8,128)} %copy-done.12) | copy-start | bytes 2064388
  530.4 21.8 %copy-start.164 = (f32[64]{0:T(128)S(1)}, f32[64]{0:T(128)}, u32[]{:S(2)}) copy-start(f32[64]{0:T(128)} %get-tuple-element.147) | copy-start | bytes 772
  555.4 3.4 collective-permute-start.3
  583.9 57.2 %reduce-scatter.26.cloned.1.call-start = ((), (), s32[]{:S(2)}) async-start(), calls=%async_computation.20 | async-start | bytes 2007040 | tf_op jit(solution)/shard_map/reduce_scatter | solution.py:351
  588.2 77.0 %reduce-scatter.24.cloned.1.call-start = ((), (), s32[]{:S(2)}) async-start(), calls=%async_computation.19 | async-start | bytes 2580480 | tf_op jit(solution)/shard_map/reduce_scatter | solution.py:345
  610.0 140.7 %reduce-scatter.32.cloned.1.call-start = ((), (), s32[]{:S(2)}) async-start(), calls=%async_computation.23 | async-start | bytes 10895360 | tf_op jit(solution)/shard_map/reduce_scatter | solution.py:360
  618.5 217.7 %reduce-scatter.30.cloned.1.call-start = ((), (), s32[]{:S(2)}) async-start(), calls=%async_computation.22 | async-start | bytes 10895360 | tf_op jit(solution)/shard_map/reduce_scatter | solution.py:357
  627.5 294.2 %reduce-scatter.28.cloned.1.call-start = ((), (), s32[]{:S(2)}) async-start(), calls=%async_computation.21 | async-start | bytes 10895360 | tf_op jit(solution)/shard_map/reduce_scatter | solution.py:354
  636.0 309.0 %reduce-scatter.38.cloned.1.call-start = ((), (), s32[]{:S(2)}) async-start(), calls=%async_computation.26 | async-start | bytes 286720
  638.0 330.3 %reduce-scatter.36.cloned.1.call-start = ((), (), s32[]{:S(2)}) async-start(), calls=%async_computation.25 | async-start | bytes 286720
  639.9 351.9 %reduce-scatter.34.cloned.1.call-start = ((), (), s32[]{:S(2)}) async-start(), calls=%async_computation.24 | async-start | bytes 368640
  641.0 488.3 %all-reduce.8.cloned.1.call-start = ((), (), s32[]{:S(2)}) async-start(), calls=%async_computation.27 | async-start | bytes 14909440 | tf_op jit(solution)/shard_map/psum | solution.py:371
  922.8 23.2 %copy-start.64 = (f32[64,896]{1,0:T(8,128)S(1)}, f32[64,896]{1,0:T(8,128)}, u32[]{:S(2)}) copy-start(f32[64,896]{1,0:T(8,128)} %copy-done.63) | copy-start | bytes 688132
  (188 other events, 854.4 us)
Sparse Core Ops, SparseCore 0:
  9.7 33.2 all-gather.5
  44.6 27.0 all-gather.7
  73.4 85.8 all-gather.9
  160.8 86.9 all-gather.11
  249.2 86.9 all-gather.13
  475.3 20.2 reduce-scatter.17
  528.9 20.4 reduce-scatter.19
  584.0 20.2 reduce-scatter.21
  607.4 25.6 reduce-scatter.25
  636.1 29.1 reduce-scatter.23
  667.8 82.9 reduce-scatter.31
  753.2 82.9 reduce-scatter.29
  838.7 82.9 reduce-scatter.27
  924.6 20.3 reduce-scatter.37
  947.8 20.3 reduce-scatter.35
  971.2 20.5 reduce-scatter.33
  996.3 132.9 all-reduce.7
where the time goes:
time: 1160 us; the launch traced here: 1150 us
  waiting for transfers between devices  743 us (64%)
  matrix products  138 us (12%)
  blocking collectives  90.2 us (8%)
  local copies, waits for them, and re-layouts  83.1 us (7%)
  other arithmetic  67.7 us (6%)
  between operations  18.9 us (2%)
    psum x1, waiting for transfers between devices, on_device(): lax.psum(owned_rows[0].astype(jnp.bfloat16), 'replica').astype(jnp.float32)  93.1 us
    reduce_scatter x1, waiting for transfers between devices, on_device(): lax.psum_scatter(grad_terms[5].astype(jnp.bfloat16), 'group', scatter_dim...  85.5 us
    reduce_scatter x1, waiting for transfers between devices, on_device(): lax.psum_scatter(grad_terms[4].astype(jnp.bfloat16), 'group', scatter_dim...  85.5 us
    reduce_scatter x1, waiting for transfers between devices, on_device(): lax.psum_scatter(grad_terms[3].astype(jnp.bfloat16), 'group', scatter_dim...  85.5 us
    all_gather x1, waiting for transfers between devices, on_device(): lax.all_gather(w_gate, 'group', axis=1, tiled=True)  85 us
    all_gather x1, waiting for transfers between devices, on_device(): lax.all_gather(w_up, 'group', axis=1, tiled=True)  83.6 us
    all_gather x1, waiting for transfers between devices, on_device(): lax.all_gather(w_down, 'group', axis=1, tiled=True)  82.6 us
    unnamed x20, waiting for transfers between devices  63.6 us
  transfers between devices with their start and end apart: 21, of which 18 were waited for; matrix products, arithmetic and copies ran while one was open for 9% of the time, Pallas kernels for 0%

commit v1 on v0

v1 whole, which is shorter than its diff:
```python
import jax
import jax.numpy as jnp
import numpy as np
from jax import lax
from jax.sharding import PartitionSpec as P

HEADS = 14
KV_HEADS = 2
HEAD_DIM = 64
GROUPS = HEADS // KV_HEADS
D = 896
FF = 4864
QKV = 1152
SPAN = 64
ROW = 256
REPL = 16
ZDEV = 4
OWN = D // ZDEV
CHUNK = OWN // REPL
BLOCK = FF // ZDEV
WIN = 1280
STARTS = [128 * ((19 * z) // 2) for z in range(ZDEV)]
SHIFTS = [BLOCK * z - STARTS[z] for z in range(ZDEV)]
KV_WIDTH = KV_HEADS * HEAD_DIM

eps = 1e-06
rope_base = 1000000.0
f32 = jnp.float32
bf16 = jnp.bfloat16

PERM = np.zeros((D, REPL, ZDEV, 16), np.float32)
for z_at in range(ZDEV):
    for r_at in range(REPL):
        for i_at in range(CHUNK):
            PERM[z_at * OWN + r_at * CHUNK + i_at, r_at, z_at, i_at] = 1.0
PERM = PERM.reshape(D, REPL * ZDEV * 16)


def rms_scale(values):
    return lax.rsqrt(jnp.mean(values * values, axis=-1, keepdims=True) + eps)


def rotate_half(values):
    half_len = values.shape[-1] // 2
    return jnp.concatenate([-values[..., half_len:], values[..., :half_len]], axis=-1)


def norm_back(grad_norm, values, scale_rows, gain_vec):
    scaled = grad_norm * gain_vec
    row_inner = jnp.mean(scaled * values, axis=-1, keepdims=True)
    grad_in = scale_rows * (scaled - values * scale_rows * scale_rows * row_inner)
    grad_gain = jnp.sum(grad_norm * values * scale_rows, axis=0)
    return (grad_in, grad_gain)


def doc_tables(doc_lens, group_at):
    doc_ends = jnp.cumsum(doc_lens)
    doc_starts = doc_ends - doc_lens
    row_spots = jnp.arange(ROW, dtype=jnp.int32)
    segment = jnp.sum((doc_ends[None, :] <= row_spots[:, None]).astype(jnp.int32), axis=1)
    doc_pick = segment[:, None] == jnp.arange(doc_lens.shape[0], dtype=jnp.int32)[None, :]
    doc_begin = jnp.sum(jnp.where(doc_pick, doc_starts[None, :], 0), axis=1)
    first_row = group_at * SPAN
    own_segment = lax.dynamic_slice_in_dim(segment, first_row, SPAN)
    own_spots = lax.dynamic_slice_in_dim(row_spots, first_row, SPAN)
    own_begin = lax.dynamic_slice_in_dim(doc_begin, first_row, SPAN)
    allowed = (own_segment[:, None] == segment[None, :]) & (
        row_spots[None, :] <= own_spots[:, None]
    )
    inv_freqs = rope_base ** (-jnp.arange(0, HEAD_DIM, 2, dtype=f32) / HEAD_DIM)
    angles = (own_spots - own_begin).astype(f32)[:, None] * inv_freqs[None, :]
    angles = jnp.concatenate([angles, angles], axis=1)
    return (allowed, jnp.cos(angles)[:, None, :], jnp.sin(angles)[:, None, :])


def split_kv(all_kv):
    key_rows = all_kv[:, :KV_WIDTH].reshape(ROW, KV_HEADS, HEAD_DIM)
    value_rows = all_kv[:, KV_WIDTH:].reshape(ROW, KV_HEADS, HEAD_DIM)
    return (key_rows, value_rows)


def score_block(query_rot, key_rows, allowed):
    grouped = query_rot.reshape(SPAN, KV_HEADS, GROUPS, HEAD_DIM)
    scores = (
        jnp.einsum("ikgd,jkd->kgij", grouped, key_rows, preferred_element_type=f32)
        * HEAD_DIM ** (-0.5)
    )
    return jnp.where(allowed[None, None], scores, -jnp.inf)


def dot(left, right):
    return jnp.dot(left, right, preferred_element_type=f32)


def dot_t(left, right):
    return jnp.einsum("id,ed->ie", left, right, preferred_element_type=f32)


def layer_forward(entering, weights, tables):
    w_qo, w_gu, w_down, b_qkv, gain_attn, gain_ffn = weights
    allowed, cosine, sine_table = tables
    values = entering.astype(f32)
    scale_one = rms_scale(values)
    normed_one = (values * scale_one * gain_attn).astype(bf16)
    mixed_qkv = dot(normed_one, w_qo[:, :QKV]) + b_qkv
    query_pre = mixed_qkv[:, :D].reshape(SPAN, HEADS, HEAD_DIM)
    key_pre = mixed_qkv[:, D : D + KV_WIDTH].reshape(SPAN, KV_HEADS, HEAD_DIM)
    query_rot = (query_pre * cosine + rotate_half(query_pre) * sine_table).astype(bf16)
    key_rot = (key_pre * cosine + rotate_half(key_pre) * sine_table).astype(bf16)
    local_kv = jnp.concatenate(
        [key_rot.reshape(SPAN, KV_WIDTH), mixed_qkv[:, D + KV_WIDTH :].astype(bf16)], axis=1
    )
    all_kv = lax.all_gather(local_kv, "group", axis=0, tiled=True)
    key_rows, value_rows = split_kv(all_kv)
    scores = score_block(query_rot, key_rows, allowed)
    row_top = jnp.max(scores, axis=-1, keepdims=True)
    log_total = row_top + jnp.log(jnp.sum(jnp.exp(scores - row_top), axis=-1, keepdims=True))
    attn_probs = jnp.exp(scores - log_total).astype(bf16)
    context = jnp.einsum("kgij,jkd->ikgd", attn_probs, value_rows, preferred_element_type=f32)
    context = context.reshape(SPAN, D).astype(bf16)
    hidden = values + dot(context, w_qo[:, QKV:])
    scale_two = rms_scale(hidden)
    normed_two = (hidden * scale_two * gain_ffn).astype(bf16)
    normed_all = lax.all_gather(normed_two, "group", axis=0, tiled=True)
    gate_up = dot(normed_all, w_gu)
    gate_proj, up_proj = gate_up[:, :WIN], gate_up[:, WIN:]
    activated = (jax.nn.silu(gate_proj) * up_proj).astype(bf16)
    partial = dot(activated, w_down).astype(bf16)
    mlp = lax.psum_scatter(partial, "group", scatter_dimension=0, tiled=True).astype(f32)
    output = (hidden + mlp).astype(bf16)
    kept = (values, scale_one, normed_one, query_rot, all_kv, log_total, context, hidden)
    kept = kept + (scale_two, normed_all, gate_up, activated)
    return (output, kept)


def layer_backward(grad_out, kept, weights, tables):
    values, scale_one, normed_one, query_rot, all_kv, log_total, context, hidden = kept[:8]
    scale_two, normed_all, gate_up, activated = kept[8:]
    w_qo, w_gu, w_down, b_qkv, gain_attn, gain_ffn = weights
    allowed, cosine, sine_table = tables
    gate_proj, up_proj = gate_up[:, :WIN], gate_up[:, WIN:]
    grad_mlp = grad_out.astype(bf16)
    grad_mlp_all = lax.all_gather(grad_mlp, "group", axis=0, tiled=True)
    grad_act = dot_t(grad_mlp_all, w_down)
    sigma_gate = jax.nn.sigmoid(gate_proj)
    silu_gate = gate_proj * sigma_gate
    grad_gate = grad_act * up_proj * sigma_gate * (1.0 + gate_proj * (1.0 - sigma_gate))
    grad_up = grad_act * silu_gate
    grad_gu = jnp.concatenate([grad_gate.astype(bf16), grad_up.astype(bf16)], axis=1)
    partial = dot_t(grad_gu, w_gu).astype(bf16)
    grad_norm_two = lax.psum_scatter(
        partial, "group", scatter_dimension=0, tiled=True
    ).astype(f32)
    back_two, grad_gain_ffn = norm_back(grad_norm_two, hidden, scale_two, gain_ffn)
    grad_hidden = grad_out + back_two
    grad_attn = grad_hidden.astype(bf16)
    grad_context = dot_t(grad_attn, w_qo[:, QKV:]).astype(bf16)
    grad_context = grad_context.reshape(SPAN, KV_HEADS, GROUPS, HEAD_DIM)
    key_rows, value_rows = split_kv(all_kv)
    grouped = query_rot.reshape(SPAN, KV_HEADS, GROUPS, HEAD_DIM)
    attn_probs = jnp.exp(score_block(query_rot, key_rows, allowed) - log_total)
    grad_probs = jnp.einsum("ikgd,jkd->kgij", grad_context, value_rows, preferred_element_type=f32)
    row_inner = jnp.sum(attn_probs * grad_probs, axis=-1, keepdims=True)
    grad_scores = (attn_probs * (grad_probs - row_inner)).astype(bf16)
    score_scale = HEAD_DIM ** (-0.5)
    grad_query = jnp.einsum("kgij,jkd->ikgd", grad_scores, key_rows, preferred_element_type=f32)
    grad_query = grad_query.reshape(SPAN, HEADS, HEAD_DIM) * score_scale
    grad_key_all = (
        jnp.einsum("kgij,ikgd->jkd", grad_scores, grouped, preferred_element_type=f32)
        * score_scale
    )
    grad_value_all = jnp.einsum(
        "kgij,ikgd->jkd", attn_probs.astype(bf16), grad_context, preferred_element_type=f32
    )
    grad_kv_all = jnp.concatenate(
        [grad_key_all.reshape(ROW, KV_WIDTH), grad_value_all.reshape(ROW, KV_WIDTH)], axis=1
    )
    grad_kv = lax.psum_scatter(
        grad_kv_all.astype(bf16), "group", scatter_dimension=0, tiled=True
    ).astype(f32)
    grad_key = grad_kv[:, :KV_WIDTH].reshape(SPAN, KV_HEADS, HEAD_DIM)
    query_back = grad_query * cosine - rotate_half(grad_query * sine_table)
    key_back = grad_key * cosine - rotate_half(grad_key * sine_table)
    grad_mixed = jnp.concatenate(
        [query_back.reshape(SPAN, D), key_back.reshape(SPAN, KV_WIDTH), grad_kv[:, KV_WIDTH:]],
        axis=1,
    ).astype(bf16)
    grad_bias = jnp.sum(grad_mixed.astype(f32), axis=0)
    grad_norm_one = dot_t(grad_mixed, w_qo[:, :QKV])
    back_one, grad_gain_attn = norm_back(grad_norm_one, values, scale_one, gain_attn)
    grad_in = grad_hidden + back_one
    pieces = (
        jnp.concatenate([normed_one, grad_mixed, context, grad_attn], axis=1),
        jnp.concatenate([normed_all, grad_gu, activated, grad_mlp_all], axis=1),
        jnp.concatenate([grad_gain_attn, grad_gain_ffn, grad_bias])[None],
    )
    return (grad_in, pieces)


def gather_weights(w_qkv, b_qkv, w_out, w_gate, w_up, w_down, norm_attn, norm_ffn):
    group_at = lax.axis_index("group")
    replica_at = lax.axis_index("replica")

    def own_rows(block):
        return lax.dynamic_slice_in_dim(block, replica_at * CHUNK, CHUNK, 0)

    vectors = jnp.concatenate([norm_attn, norm_ffn, b_qkv])
    joint = jnp.concatenate([own_rows(w_qkv), own_rows(w_out)], axis=1)
    extra = jnp.zeros((2, joint.shape[1]), bf16)
    extra = lax.dynamic_update_slice(extra, vectors[None], (0, 0))
    joint = jnp.concatenate([joint, extra], axis=0)
    joint = lax.all_gather(joint, ("group", "replica"), axis=0, tiled=False)
    joint = joint.reshape(ZDEV, REPL, 16, joint.shape[-1])
    w_qo = joint[:, :, :CHUNK].reshape(D, QKV + D)
    vectors = joint[:, 0, CHUNK, : vectors.shape[0]]
    gain_attn = vectors[:, :OWN].reshape(D)
    gain_ffn = vectors[:, OWN : 2 * OWN].reshape(D)
    bias = vectors[:, 2 * OWN :].reshape(QKV)
    gate_rows, up_rows = own_rows(w_gate), own_rows(w_up)
    pieces = jnp.stack(
        [
            jnp.concatenate([gate_rows[:, s : s + WIN], up_rows[:, s : s + WIN]], axis=1)
            for s in STARTS
        ]
    )
    pieces = jnp.pad(pieces, ((0, 0), (0, 2), (0, 0)))
    pieces = lax.all_to_all(pieces, "group", split_axis=0, concat_axis=0, tiled=True)
    w_gu = lax.all_gather(pieces, "replica", axis=0, tiled=False)
    w_gu = jnp.transpose(w_gu[:, :, :CHUNK], (1, 0, 2, 3)).reshape(D, 2 * WIN)
    padded_down = lax.dynamic_update_slice(
        jnp.zeros((WIN, D), bf16), w_down, ((group_at % 2) * 64, 0)
    )
    return (w_qo, w_gu, padded_down, jnp.concatenate([bias, gain_attn, gain_ffn])[None])


def swap(value):
    return lax.ppermute(value, "section", [(0, 1), (1, 0)])


def weight_grads(token_pieces, row_pieces, vector_sum):
    perm = jnp.asarray(PERM, bf16)
    group_at = lax.axis_index("group")
    normed_one, grad_mixed, context, grad_attn = (
        token_pieces[:, :D],
        token_pieces[:, D : D + QKV],
        token_pieces[:, D + QKV : 2 * D + QKV],
        token_pieces[:, 2 * D + QKV :],
    )
    normed_all, grad_gu, activated, grad_mlp = (
        row_pieces[:, :D],
        row_pieces[:, D : D + 2 * WIN],
        row_pieces[:, D + 2 * WIN : D + 3 * WIN],
        row_pieces[:, D + 3 * WIN :],
    )

    def outer(left, right):
        return jnp.einsum("id,ie->de", left, right, preferred_element_type=f32).astype(bf16)

    left_one = dot(normed_one, perm).astype(bf16)
    left_out = dot(context, perm).astype(bf16)
    left_two = dot(normed_all, perm).astype(bf16)
    vec = vector_sum[0]
    rows = jnp.stack(
        [vec[:D].reshape(ZDEV, REPL, CHUNK), vec[D : 2 * D].reshape(ZDEV, REPL, CHUNK)], axis=2
    ).reshape(ZDEV, REPL, 2 * CHUNK)
    rows = jnp.concatenate([rows, vec[2 * D :].reshape(ZDEV, REPL, QKV // 64)], axis=2)
    rows = jnp.pad(rows, ((0, 0), (0, 0), (0, QKV - rows.shape[-1])))
    rows = jnp.transpose(rows, (1, 0, 2)).astype(bf16)
    spot = jnp.arange(16)[None, None, :, None] == CHUNK
    part_qkv = outer(left_one, grad_mixed).reshape(REPL, ZDEV, 16, QKV)
    part_qkv = jnp.where(spot, rows[:, :, None, :], part_qkv)
    part_out = outer(left_out, grad_attn).reshape(REPL, ZDEV, 16, D)
    part_gu = outer(left_two, grad_gu).reshape(REPL, ZDEV, 16, 2 * WIN)
    part_down = outer(activated, grad_mlp).reshape(REPL, WIN // REPL, D)

    def scatter(part):
        return lax.psum_scatter(part, "replica", scatter_dimension=0, tiled=False)

    part_qkv, part_out, part_gu, part_down = map(scatter, (part_qkv, part_out, part_gu, part_down))
    mixed = jnp.concatenate([part_qkv, part_out, part_gu], axis=-1)
    mixed = lax.all_to_all(mixed, "group", split_axis=0, concat_axis=0, tiled=True)
    joint = jnp.sum(mixed[:, :, : QKV + D].astype(f32), axis=0).astype(bf16)
    gate = jnp.concatenate(
        [mixed[z, :, QKV + D + SHIFTS[z] :][:, :BLOCK] for z in range(ZDEV)], axis=-1
    )
    up = jnp.concatenate(
        [mixed[z, :, QKV + D + WIN + SHIFTS[z] :][:, :BLOCK] for z in range(ZDEV)], axis=-1
    )
    final = jnp.concatenate([joint, gate, up], axis=-1)
    final = lax.all_gather(final, "replica", axis=0, tiled=False)
    final_down = lax.all_gather(part_down, "replica", axis=0, tiled=True)
    grad_down = lax.dynamic_slice_in_dim(final_down, (group_at % 2) * 64, BLOCK, 0)
    body = final[:, :CHUNK].reshape(OWN, final.shape[-1]).astype(f32)
    tail = final[:, CHUNK, :128].astype(f32)
    grad_gain_attn = tail[:, :CHUNK].reshape(OWN)
    grad_gain_ffn = tail[:, CHUNK : 2 * CHUNK].reshape(OWN)
    grad_bias = tail[:, 2 * CHUNK : 2 * CHUNK + QKV // 64].reshape(QKV // 4)
    return (
        body[:, :QKV],
        grad_bias,
        body[:, QKV : QKV + D],
        body[:, QKV + D : QKV + D + FF],
        body[:, QKV + D + FF :],
        grad_down.astype(f32),
        grad_gain_attn,
        grad_gain_ffn,
    )


def on_device(
    tokens, cotangent, doc_lengths, w_qkv, b_qkv, w_out, w_gate, w_up, w_down, norm_attn, norm_ffn
):
    section_at = lax.axis_index("section")
    group_at = lax.axis_index("group")
    first = section_at == 0
    own_set = gather_weights(
        w_qkv[0], b_qkv[0], w_out[0], w_gate[0], w_up[0], w_down[0], norm_attn[0], norm_ffn[0]
    )
    other_set = tuple(map(swap, own_set))

    def unpack(members):
        w_qo, w_gu, padded_down, vectors = members
        vectors = vectors[0].astype(f32)
        return (
            w_qo,
            w_gu,
            padded_down,
            vectors[:QKV],
            vectors[QKV : QKV + D],
            vectors[QKV + D :],
        )

    layer_sets = [
        unpack([jnp.where(first, a, b) for a, b in zip(own_set, other_set)]),
        unpack([jnp.where(first, b, a) for a, b in zip(own_set, other_set)]),
    ]
    own_tokens = lax.dynamic_index_in_dim(tokens, section_at, 0, keepdims=False)[0]
    own_cotangent = lax.dynamic_index_in_dim(cotangent, section_at, 0, keepdims=False)[0]
    lengths = lax.dynamic_index_in_dim(doc_lengths, section_at, 0, keepdims=False)[0]
    tables = doc_tables(lengths, group_at)
    out_first, kept_first = layer_forward(own_tokens, layer_sets[0], tables)
    out_second, kept_second = layer_forward(out_first, layer_sets[1], tables)
    grad_second, pieces_second = layer_backward(
        own_cotangent.astype(f32), kept_second, layer_sets[1], tables
    )
    grad_second = grad_second.astype(bf16)
    grad_first, pieces_first = layer_backward(
        grad_second.astype(f32), kept_first, layer_sets[0], tables
    )
    sent = [jnp.where(first, b, a) for a, b in zip(pieces_first, pieces_second)]
    kept = [jnp.where(first, a, b) for a, b in zip(pieces_first, pieces_second)]
    got = [swap(member) for member in sent]
    token_pieces = jnp.concatenate([kept[0], got[0]], axis=0)
    row_pieces = jnp.concatenate([kept[1], got[1]], axis=0)
    grads = weight_grads(token_pieces, row_pieces, kept[2] + got[2])

    def placed(lead, second):
        mine = jnp.where(first, lead, second)
        theirs = swap(jnp.where(first, second, lead))
        return jnp.stack([jnp.where(first, mine, theirs), jnp.where(first, theirs, mine)])

    acts = placed(out_first, out_second)
    input_grads = placed(grad_first, grad_second.astype(f32))
    return (acts[None, :, None], input_grads[None, :, None]) + tuple(g[None] for g in grads)


def solution(mesh):
    rows = P("section", "group", None)
    vector = P("section", "group")
    spans = P("section", None, "replica", "group", None)
    return jax.shard_map(
        on_device,
        mesh=mesh,
        in_specs=(
            P(None, "replica", "group", None),
            P(None, "replica", "group", None),
            P(None, "replica", None),
            rows,
            vector,
            rows,
            rows,
            rows,
            rows,
            vector,
            vector,
        ),
        out_specs=(spans, spans, rows, vector, rows, rows, rows, rows, vector, vector),
        check_vma=False,
    )
```

time: 1160 us -> 893 us (0.77)
  waiting for transfers between devices: 743 us -> 540 us
  matrix products: 138 us -> 70.1 us
  blocking collectives: 90.2 us -> 104 us
    reduce_scatter x8 -> x6, waiting for transfers between devices: 317 us -> 70.2 us  [the longest x2 28.4 us: layer_backward(): lax.psum_scatter(grad_kv_all.astype(bf16), 'group', scatter_dimension=0,...]
    unnamed x20 -> x18, waiting for transfers between devices: 63.6 us -> 282 us
    psum x1 -> x0, waiting for transfers between devices: 93.1 us -> none  [on_device(): lax.psum(owned_rows[0].astype(jnp.bfloat16), 'replica').astype(jnp.float32)]
    all_gather x5 -> x4, waiting for transfers between devices: 267 us -> 184 us  [the longest x1 58.1 us: weight_grads(): final = lax.all_gather(final, 'replica', axis=0, tiled=False)]
    dot_general x44 -> x24, matrix products: 133 us -> 67.3 us  [the longest x8 25.3 us: dot_t(): return jnp.einsum('id,ed->ie', left, right, preferred_element_type=f32)]
    all_gather x0 -> x4, blocking collectives: none -> 53.2 us  [the longest x2 26.7 us: layer_backward(): grad_mlp_all = lax.all_gather(grad_mlp, 'group', axis=0, tiled=True)]
    psum x1 -> x0, blocking collectives: 41.7 us -> none  [on_device(): lax.psum(owned_rows[1].astype(jnp.bfloat16), 'replica').astype(jnp.float32)]
    all_to_all x0 -> x2, blocking collectives: none -> 26.3 us  [the longest x1 13.5 us: weight_grads(): lax.all_to_all(mixed, 'group', split_axis=0, concat_axis=0, tiled=True)]
  transfers between devices with their start and end apart: 21 -> 23, of which waited for: 18 -> 19; matrix products, arithmetic and copies ran while one was open for 9% -> 15% of each run, Pallas kernels for 0% -> 0%
where the time goes in v1:
time: 893 us; the launch traced here: 882 us
  waiting for transfers between devices  540 us (60%)
  blocking collectives  104 us (12%)
  local copies, waits for them, and re-layouts  78 us (9%)
  other arithmetic  70.2 us (8%)
  matrix products  70.1 us (8%)
  between operations  15.9 us (2%)
    unnamed x18, waiting for transfers between devices  282 us
    all_gather x1, waiting for transfers between devices, weight_grads(): final = lax.all_gather(final, 'replica', axis=0, tiled=False)  58.1 us
    all_gather x1, waiting for transfers between devices, gather_weights(): joint = lax.all_gather(joint, ('group', 'replica'), axis=0, tiled=False)  54.1 us
    all_gather x1, waiting for transfers between devices, gather_weights(): w_gu = lax.all_gather(pieces, 'replica', axis=0, tiled=False)  43.4 us
    reduce_scatter x2, waiting for transfers between devices, layer_backward(): lax.psum_scatter(grad_kv_all.astype(bf16), 'group', scatter_dimension=0,...  28.4 us
    all_gather x1, waiting for transfers between devices, weight_grads(): final_down = lax.all_gather(part_down, 'replica', axis=0, tiled=True)  28 us
    all_gather x2, blocking collectives, layer_backward(): grad_mlp_all = lax.all_gather(grad_mlp, 'group', axis=0, tiled=True)  26.7 us
    all_gather x2, blocking collectives, layer_forward(): normed_all = lax.all_gather(normed_two, 'group', axis=0, tiled=True)  26.4 us
  transfers between devices with their start and end apart: 23, of which 19 were waited for; matrix products, arithmetic and copies ran while one was open for 15% of the time, Pallas kernels for 0%

profile of v1, /device:TPU:0, one launch (start us, length us, event | category | flops | bytes accessed | tf_op | source)
XLA Modules:
  0.0 881.5 jit_solution(13666392841938025716)
XLA Ops:
  13.3 12.8 %all_to_all.10 = bf16[4,16,2560]{2,1,0:T(8,128)(2,1)} all-to-all(bf16[4,16,2560]{2,1,0:T(8,128)(2,1)S(1)} %fusion.79), channel_id=1, replica_groups=mesh['section'=2,'group'=4,'replica'=16] {'group'}, dimensions={0} | all-to-all | bytes 655360 | tf_op jit(solution)/shard_map/all_to_all | solution.py:227
  29.5 54.1 %all-gather.10.cloned.1.call-done = bf16[1024,2048]{1,0:T(8,128)(2,1)} async-done(((bf16[16,2048]{1,0:T(8,128)(2,1)}), bf16[1024,2048]{1,0:T(8,128)(2,1)}) %all-gather.10.cloned.1.call-update) | async-done | bytes 4194320 | tf_op jit(solution)/shard_map/all_gather | solution.py:212
  83.5 6.0 reshape.577
  96.1 43.4 %all-gather.12.cloned.1.call-done = bf16[64,16,2560]{2,1,0:T(8,128)(2,1)} async-done(((bf16[4,16,2560]{2,1,0:T(8,128)(2,1)}), bf16[64,16,2560]{2,1,0:T(8,128)(2,1)}) %all-gather.12.cloned.1.call-update) | async-done | bytes 5242896 | tf_op jit(solution)/shard_map/all_gather | solution.py:228
  145.2 7.4 reshape.585
  152.7 5.5 broadcast_select_fusion.2
  163.2 12.5 %all_gather.41 = bf16[256,256]{1,0:T(8,128)(2,1)S(1)} all-gather(bf16[64,256]{1,0:T(8,128)(2,1)S(1)} %pad_maximum_fusion.22), channel_id=1, replica_groups=mesh['section'=2,'group'=4,'replica'=16] {'group'}, dimensions={0}, use_global_device_ids=true | all-gather | bytes 163840 | tf_op jit(solution)/shard_map/all_gather | solution.py:113
  179.5 13.2 %all_gather.42 = bf16[256,896]{1,0:T(8,128)(2,1)S(1)} all-gather(bf16[64,896]{1,0:T(8,128)(2,1)S(1)} %multiply_convert_fusion.9), channel_id=1, replica_groups=mesh['section'=2,'group'=4,'replica'=16] {'group'}, dimensions={0}, use_global_device_ids=true | all-gather | bytes 573440 | tf_op jit(solution)/shard_map/all_gather | solution.py:124
  202.6 14.1 %all-gather.2 = bf16[1,1,256,896]{3,2,1,0:T(8,128)(2,1)} all-gather(bf16[1,1,64,896]{3,2,1,0:T(8,128)(2,1)S(1)} %constant_dynamic-slice_fusion), channel_id=4, replica_groups=mesh['section'=2,'group'=4,'replica'=16] {'group'}, dimensions={2}, use_global_device_ids=true | all-gather | bytes 573440 | tf_op jit(solution)/shard_map/all_gather | solution.py:143
  217.6 4.5 reduce-scatter.19.cloned.1.call-done
  230.5 12.0 %all_gather.45 = bf16[256,256]{1,0:T(8,128)(2,1)S(1)} all-gather(bf16[64,256]{1,0:T(8,128)(2,1)S(1)} %pad_maximum_fusion.23), channel_id=1, replica_groups=mesh['section'=2,'group'=4,'replica'=16] {'group'}, dimensions={0}, use_global_device_ids=true | all-gather | bytes 163840 | tf_op jit(solution)/shard_map/all_gather | solution.py:113
  246.0 13.2 %all_gather.46 = bf16[256,896]{1,0:T(8,128)(2,1)S(1)} all-gather(bf16[64,896]{1,0:T(8,128)(2,1)S(1)} %multiply_convert_fusion.8), channel_id=1, replica_groups=mesh['section'=2,'group'=4,'replica'=16] {'group'}, dimensions={0}, use_global_device_ids=true | all-gather | bytes 573440 | tf_op jit(solution)/shard_map/all_gather | solution.py:124
  269.4 4.6 fusion.34
  281.4 12.6 %reduce-scatter.23.cloned.1.call-done = bf16[64,896]{1,0:T(8,128)(2,1)} async-done(((bf16[256,896]{1,0:T(8,128)(2,1)}), bf16[64,896]{1,0:T(8,128)(2,1)}) %reduce-scatter.23.cloned.1.call-update) | async-done | bytes 114704 | tf_op jit(solution)/shard_map/reduce_scatter | solution.py:151
  306.6 11.2 %reduce-scatter.21.cloned.1.call-done = bf16[64,896]{1,0:T(8,128)(2,1)} async-done(((bf16[256,896]{1,0:T(8,128)(2,1)}), bf16[64,896]{1,0:T(8,128)(2,1)}) %reduce-scatter.21.cloned.1.call-update) | async-done | bytes 114704 | tf_op jit(solution)/shard_map/reduce_scatter | solution.py:129
  322.0 18.4 %reduce-scatter.25.cloned.1.call-done = bf16[64,256]{1,0:T(8,128)(2,1)} async-done(((bf16[256,256]{1,0:T(8,128)(2,1)}), bf16[64,256]{1,0:T(8,128)(2,1)}) %reduce-scatter.25.cloned.1.call-update) | async-done | bytes 32784 | tf_op jit(solution)/shard_map/reduce_scatter | solution.py:178
  347.7 12.7 %all_gather.48 = bf16[256,896]{1,0:T(8,128)(2,1)S(1)} all-gather(bf16[64,896]{1,0:T(8,128)(2,1)S(1)} %fusion.103), channel_id=1, replica_groups=mesh['section'=2,'group'=4,'replica'=16] {'group'}, dimensions={0}, use_global_device_ids=true | all-gather | bytes 573440 | tf_op jit(solution)/shard_map/all_gather | solution.py:143
  370.2 5.7 broadcast_select_fusion.4
  377.7 13.5 %reduce-scatter.27.cloned.1.call-done = bf16[64,896]{1,0:T(8,128)(2,1)} async-done(((bf16[256,896]{1,0:T(8,128)(2,1)}), bf16[64,896]{1,0:T(8,128)(2,1)}) %reduce-scatter.27.cloned.1.call-update) | async-done | bytes 114704 | tf_op jit(solution)/shard_map/reduce_scatter | solution.py:151
  399.3 4.6 convolution_convert_fusion.2
  409.0 10.0 %reduce-scatter.29.cloned.1.call-done = bf16[64,256]{1,0:T(8,128)(2,1)} async-done(((bf16[256,256]{1,0:T(8,128)(2,1)}), bf16[64,256]{1,0:T(8,128)(2,1)}) %reduce-scatter.29.cloned.1.call-update) | async-done | bytes 32784 | tf_op jit(solution)/shard_map/reduce_scatter | solution.py:178
  442.4 8.8 convolution_convert_fusion
  451.2 46.2 %reduce-scatter.37.cloned.1.call-done = bf16[1,80,896]{2,1,0:T(8,128)(2,1)} async-done(((bf16[16,80,896]{2,1,0:T(8,128)(2,1)}), bf16[1,80,896]{2,1,0:T(8,128)(2,1)}) %reduce-scatter.37.cloned.1.call-update) | async-done | bytes 143376
  497.5 76.3 %reduce-scatter.33.cloned.1.call-done = bf16[1,4,16,896]{3,2,1,0:T(8,128)(2,1)} async-done(((bf16[16,4,16,896]{3,2,1,0:T(8,128)(2,1)}), bf16[1,4,16,896]{3,2,1,0:T(8,128)(2,1)}) %reduce-scatter.33.cloned.1.call-update) | async-done | bytes 114704
  573.8 78.1 %reduce-scatter.31.cloned.1.call-done = bf16[1,4,16,1152]{3,2,1,0:T(8,128)(2,1)} async-done(((bf16[16,4,16,1152]{3,2,1,0:T(8,128)(2,1)}), bf16[1,4,16,1152]{3,2,1,0:T(8,128)(2,1)}) %reduce-scatter.31.cloned.1.call-update) | async-done | bytes 147472
  651.9 81.4 %reduce-scatter.35.cloned.1.call-done = bf16[1,4,16,2560]{3,2,1,0:T(8,128)(2,1)} async-done(((bf16[16,4,16,2560]{3,2,1,0:T(8,128)(2,1)}), bf16[1,4,16,2560]{3,2,1,0:T(8,128)(2,1)}) %reduce-scatter.35.cloned.1.call-update) | async-done | bytes 327696
  734.5 13.5 %all_to_all.11 = bf16[4,16,4608]{2,1,0:T(8,128)(2,1)S(1)} all-to-all(bf16[4,16,4608]{2,1,0:T(8,128)(2,1)S(1)} %pad_maximum_fusion.2), channel_id=1, replica_groups=mesh['section'=2,'group'=4,'replica'=16] {'group'}, dimensions={0} | all-to-all | bytes 1179648 | tf_op jit(solution)/shard_map/all_to_all | solution.py:281
  752.3 28.0 %all-gather.16.cloned.1.call-done = bf16[1,1280,896]{2,1,0:T(8,128)(2,1)} async-done(((bf16[1,80,896]{2,1,0:T(8,128)(2,1)}), bf16[1,1280,896]{2,1,0:T(8,128)(2,1)}) %all-gather.16.cloned.1.call-update) | async-done | bytes 2293776 | tf_op jit(solution)/shard_map/all_gather | solution.py:291
  784.3 58.1 %all-gather.14.cloned.1.call-done = bf16[256,11776]{1,0:T(8,128)(2,1)} async-done(((bf16[16,11776]{1,0:T(8,128)(2,1)}), bf16[256,11776]{1,0:T(8,128)(2,1)}) %all-gather.14.cloned.1.call-update) | async-done | bytes 6029328 | tf_op jit(solution)/shard_map/all_gather | solution.py:290
  842.4 8.5 slice_convert_fusion
  850.9 8.8 reshape.610
  859.6 7.7 slice_bitcast_fusion.1
  (425 shorter events, 158.4 us)
Async XLA Ops:
  7.2 76.3 %all-gather.10.cloned.1.call-start = ((), (), s32[]{:S(2)}) async-start(), calls=%async_computation.18 | async-start | bytes 4259840 | tf_op jit(solution)/shard_map/all_gather | solution.py:212
  11.9 127.6 %all-gather.12.cloned.1.call-start = ((), (), s32[]{:S(2)}) async-start(), calls=%async_computation.19 | async-start | bytes 5570560 | tf_op jit(solution)/shard_map/all_gather | solution.py:228
  26.1 195.9 %reduce-scatter.19.cloned.1.call-start = ((), (), s32[]{:S(2)}) async-start(), calls=%async_computation.12 | async-start | bytes 573440 | tf_op jit(solution)/shard_map/reduce_scatter | solution.py:129
  29.3 167.4 %collective-permute-start.3 = (bf16[1280,896]{1,0:T(8,128)(2,1)}, bf16[1280,896]{1,0:T(8,128)(2,1)}, u32[]{:S(2)}, u32[]{:S(2)}) collective-permute-start(bf16[1280,896]{1,0:T(8,128)(2,1)} %bitcast_dynamic-update-slice_fusion), channel_id=1, source_target_pairs={{0,64},{64,0},{1,65},{65,1},{2,66},{66,2},{3,67},{67,3},{4,68},{68... | collective-permute-start | bytes 6881288 | tf_op jit(solution)/shard_map/ppermute | solution.py:237
  89.6 63.1 %collective-permute-start.1 = (bf16[896,2048]{1,0:T(8,128)(2,1)}, bf16[896,2048]{1,0:T(8,128)(2,1)}, u32[]{:S(2)}, u32[]{:S(2)}) collective-permute-start(bf16[896,2048]{1,0:T(8,128)(2,1)} %reshape.577), channel_id=1, source_target_pairs={{0,64},{64,0},{1,65},{65,1},{2,66},{66,2},{3,67},{67,3},{4,68},{68... | collective-permute-start | bytes 11010056 | tf_op jit(solution)/shard_map/ppermute | solution.py:237
  90.1 68.1 %copy-start.53 = (f32[64]{0:T(128)}, f32[64]{0:T(128)S(1)}, u32[]{:S(2)}) copy-start(f32[64]{0:T(128)S(1)} %add_rsqrt_fusion.3) | copy-start | bytes 772
  91.5 4.5 collective-permute-start
  96.0 62.1 %copy-start.45 = (f32[896]{0:T(1024)}, f32[896]{0:T(1024)S(1)}, u32[]{:S(2)}) copy-start(f32[896]{0:T(1024)S(1)} %get-tuple-element.83) | copy-start | bytes 10756
  152.6 40.1 %collective-permute-start.2 = (bf16[896,2560]{1,0:T(8,128)(2,1)}, bf16[896,2560]{1,0:T(8,128)(2,1)}, u32[]{:S(2)}, u32[]{:S(2)}) collective-permute-start(bf16[896,2560]{1,0:T(8,128)(2,1)} %reshape.585), channel_id=1, source_target_pairs={{0,64},{64,0},{1,65},{65,1},{2,66},{66,2},{3,67},{67,3},{4,68},{68... | collective-permute-start | bytes 13762568 | tf_op jit(solution)/shard_map/ppermute | solution.py:237
  201.7 92.4 %reduce-scatter.23.cloned.1.call-start = ((), (), s32[]{:S(2)}) async-start(), calls=%async_computation.14 | async-start | bytes 573440 | tf_op jit(solution)/shard_map/reduce_scatter | solution.py:151
  223.1 124.5 %copy-start.11 = (bf16[64,896]{1,0:T(8,128)(2,1)}, bf16[64,896]{1,0:T(8,128)(2,1)S(1)}, u32[]{:S(2)}) copy-start(bf16[64,896]{1,0:T(8,128)(2,1)S(1)} %get-tuple-element.107) | copy-start | bytes 344068
  274.0 43.8 %reduce-scatter.21.cloned.1.call-start = ((), (), s32[]{:S(2)}) async-start(), calls=%async_computation.13 | async-start | bytes 573440 | tf_op jit(solution)/shard_map/reduce_scatter | solution.py:129
  281.2 59.2 %reduce-scatter.25.cloned.1.call-start = ((), (), s32[]{:S(2)}) async-start(), calls=%async_computation.15 | async-start | bytes 163840 | tf_op jit(solution)/shard_map/reduce_scatter | solution.py:178
  306.6 84.6 %reduce-scatter.27.cloned.1.call-start = ((), (), s32[]{:S(2)}) async-start(), calls=%async_computation.16 | async-start | bytes 573440 | tf_op jit(solution)/shard_map/reduce_scatter | solution.py:151
  322.0 25.7 %copy-start.30 = (bf16[64,896]{1,0:T(8,128)(2,1)}, bf16[64,896]{1,0:T(8,128)(2,1)S(1)}, u32[]{:S(2)}) copy-start(bf16[64,896]{1,0:T(8,128)(2,1)S(1)} %get-tuple-element.91) | copy-start | bytes 344068
  344.5 23.2 %slice-start.2 = ((s8[4587520]{0:T(1024)(128)(4,1)}), s8[4194304]{0:T(1024)(128)(4,1)S(1)}, s32[]{:S(2)}) async-start(s8[4587520]{0:T(1024)(128)(4,1)} %bitcast.236), calls=%async_computation.28 | async-start | bytes 8388608
  370.2 21.0 %copy-start.52 = (f32[64]{0:T(128)S(1)}, f32[64]{0:T(128)}, u32[]{:S(2)}) copy-start(f32[64]{0:T(128)} %copy-done.51) | copy-start | bytes 772
  370.2 48.8 %reduce-scatter.29.cloned.1.call-start = ((), (), s32[]{:S(2)}) async-start(), calls=%async_computation.17 | async-start | bytes 163840 | tf_op jit(solution)/shard_map/reduce_scatter | solution.py:178
  376.0 23.4 %collective-permute-start.8 = (bf16[256,5632]{1,0:T(8,128)(2,1)}, bf16[256,5632]{1,0:T(8,128)(2,1)}, u32[]{:S(2)}, u32[]{:S(2)}) collective-permute-start(bf16[256,5632]{1,0:T(8,128)(2,1)} %get-tuple-element.114), channel_id=1, source_target_pairs={{0,64},{64,0},{1,65},{65,1},{2,66},{66,2},{3,67},{67,3},{4,68},{68... | collective-permute-start | bytes 8650760 | tf_op jit(solution)/shard_map/ppermute | solution.py:237
  393.8 29.8 %copy-start.9 = (f32[64,896]{1,0:T(8,128)}, f32[64,896]{1,0:T(8,128)S(1)}, u32[]{:S(2)}) copy-start(f32[64,896]{1,0:T(8,128)S(1)} %convert_add_fusion) | copy-start | bytes 688132
  398.6 98.8 %reduce-scatter.37.cloned.1.call-start = ((), (), s32[]{:S(2)}) async-start(), calls=%async_computation.25 | async-start | bytes 2437120
  403.9 169.9 %reduce-scatter.33.cloned.1.call-start = ((), (), s32[]{:S(2)}) async-start(), calls=%async_computation.23 | async-start | bytes 1949696
  407.0 20.2 %copy-start.49 = (f32[896]{0:T(1024)S(1)}, f32[896]{0:T(1024)}, u32[]{:S(2)}) copy-start(f32[896]{0:T(1024)} %get-tuple-element.74) | copy-start | bytes 10756
  407.0 20.4 %copy-start.4 = (bf16[896,1024]{1,0:T(8,128)(2,1)S(1)}, bf16[896,1024]{1,0:T(8,128)(2,1)}, u32[]{:S(2)}) copy-start(bf16[896,1024]{1,0:T(8,128)(2,1)} %constant.100.clone) | copy-start | bytes 5505028
  425.5 1.9 collective-permute-start.7
  429.9 222.0 %reduce-scatter.31.cloned.1.call-start = ((), (), s32[]{:S(2)}) async-start(), calls=%async_computation.22 | async-start | bytes 2506752
  433.2 1.3 collective-permute-start.6
  442.3 290.9 %reduce-scatter.35.cloned.1.call-start = ((), (), s32[]{:S(2)}) async-start(), calls=%async_computation.24 | async-start | bytes 5570560
  451.2 329.2 %all-gather.16.cloned.1.call-start = ((), (), s32[]{:S(2)}) async-start(), calls=%async_computation.21 | async-start | bytes 2437120 | tf_op jit(solution)/shard_map/all_gather | solution.py:291
  497.5 344.9 %all-gather.14.cloned.1.call-start = ((), (), s32[]{:S(2)}) async-start(), calls=%async_computation.20 | async-start | bytes 6406144 | tf_op jit(solution)/shard_map/all_gather | solution.py:290
  749.2 1.4 collective-permute-start.4
  749.5 2.0 collective-permute-start.5
  (56 other events, 450.5 us)
Sparse Core Ops, SparseCore 0:
  12.0 71.4 all-gather.9
  85.7 53.7 all-gather.11
  201.8 20.1 reduce-scatter.18
  274.1 19.8 reduce-scatter.22
  296.9 20.9 reduce-scatter.20
  320.1 20.2 reduce-scatter.24
  370.2 20.9 reduce-scatter.26
  398.7 20.1 reduce-scatter.28
  422.4 75.0 reduce-scatter.36
  500.5 73.2 reduce-scatter.32
  577.7 74.1 reduce-scatter.30
  655.1 78.0 reduce-scatter.34
  735.4 44.8 all-gather.15
  783.0 59.3 all-gather.13

commit v2 on v1

--- a/solution.py
+++ b/solution.py
@@ -1,7 +1,8 @@
 import jax
 import jax.numpy as jnp
-import numpy as np
 from jax import lax
+from jax.experimental import pallas as pl
+from jax.experimental.pallas import tpu as pltpu
 from jax.sharding import PartitionSpec as P
 
 HEADS = 14
@@ -27,14 +28,6 @@
 rope_base = 1000000.0
 f32 = jnp.float32
 bf16 = jnp.bfloat16
-
-PERM = np.zeros((D, REPL, ZDEV, 16), np.float32)
-for z_at in range(ZDEV):
-    for r_at in range(REPL):
-        for i_at in range(CHUNK):
-            PERM[z_at * OWN + r_at * CHUNK + i_at, r_at, z_at, i_at] = 1.0
-PERM = PERM.reshape(D, REPL * ZDEV * 16)
-
 
 def rms_scale(values):
     return lax.rsqrt(jnp.mean(values * values, axis=-1, keepdims=True) + eps)
@@ -237,73 +230,455 @@
     return lax.ppermute(value, "section", [(0, 1), (1, 0)])
 
 
+MESH = pl.DeviceIdType.MESH
+TILES_R = OWN // 16
+COLS = 15232
+PART_A = (0, 7680)
+PART_B = (7680, 12928)
+PART_C = (12928, 15232)
+DOWN_AT = 4 * 2 * WIN
+QO_AT = PART_C[0]
+VEC_AT = QO_AT + QKV + D
+RING = 4
+
+
+def halves(start, stop):
+    middle = start + ((stop - start) // 128 + 1) // 2 * 128
+    return ((start, middle), (middle, stop))
+
+
+def ring_spot(spot, steps):
+    return lax.rem(spot + steps + RING, RING)
+
+
+class Links:
+    def __init__(self, send_sems, recv_sems):
+        self.send_sems, self.recv_sems, self.used, self.started = send_sems, recv_sems, 0, []
+
+    def take(self, count):
+        first = self.used
+        self.used += count
+        return first
+
+    def copy(self, source, target, sem_at, device):
+        return pltpu.make_async_remote_copy(
+            src_ref=source,
+            dst_ref=target,
+            send_sem=self.send_sems.at[sem_at],
+            recv_sem=self.recv_sems.at[sem_at],
+            device_id=device,
+            device_id_type=MESH,
+        )
+
+    def send(self, source, target, sem_at, device):
+        copy = self.copy(source, target, sem_at, device)
+        copy.start()
+        self.started.append(copy)
+
+    def arrived(self, target, sem_at, device):
+        self.copy(target, target, sem_at, device).wait_recv()
+
+    def finish(self):
+        for copy in self.started:
+            copy.wait_send()
+        self.started = []
+
+
+class RingSum:
+    def __init__(self, links, spot, device_at, block, first, second, left, right, add):
+        self.links, self.spot, self.block, self.add = links, spot, block, add
+        self.right, self.left = device_at(ring_spot(spot, 1)), device_at(ring_spot(spot, -1))
+        self.first, self.second, self.from_left, self.from_right = first, second, left, right
+        self.sem = links.take(6)
+
+    def start(self):
+        send, sem, spot = self.links.send, self.sem, self.spot
+        far = ring_spot(spot, 2)
+        send(self.block(far, 0), self.first, sem, self.right)
+        send(self.block(far, 1), self.second, sem + 1, self.left)
+        send(self.block(ring_spot(spot, 1), 1), self.from_left(1), sem + 2, self.right)
+        send(self.block(ring_spot(spot, -1), 0), self.from_right(0), sem + 3, self.left)
+
+    def middle(self):
+        links, sem, spot = self.links, self.sem, self.spot
+        links.arrived(self.first, sem, self.right)
+        onward = self.block(ring_spot(spot, 1), 0)
+        self.add(onward, onward, self.first)
+        links.send(onward, self.from_left(0), sem + 4, self.right)
+        links.arrived(self.second, sem + 1, self.left)
+        onward = self.block(ring_spot(spot, -1), 1)
+        self.add(onward, onward, self.second)
+        links.send(onward, self.from_right(1), sem + 5, self.left)
+
+    def end(self, result):
+        links, sem, spot = self.links, self.sem, self.spot
+        links.arrived(self.from_left(1), sem + 2, self.right)
+        links.arrived(self.from_right(0), sem + 3, self.left)
+        links.arrived(self.from_left(0), sem + 4, self.right)
+        links.arrived(self.from_right(1), sem + 5, self.left)
+        for half in (0, 1):
+            self.add(
+                result(half), self.block(spot, half), self.from_left(half), self.from_right(half)
+            )
+
+
+class RingShare:
+    def __init__(self, links, spot, device_at, block):
+        self.links, self.spot, self.block = links, spot, block
+        self.right, self.left = device_at(ring_spot(spot, 1)), device_at(ring_spot(spot, -1))
+        self.sem = links.take(6)
+
+    def start(self):
+        send, sem = self.links.send, self.sem
+        low, high = self.block(self.spot, 0), self.block(self.spot, 1)
+        send(low, low, sem, self.right)
+        send(high, high, sem + 2, self.left)
+        send(high, high, sem + 1, self.right)
+        send(low, low, sem + 3, self.left)
+
+    def middle(self):
+        links, sem, spot = self.links, self.sem, self.spot
+        low = self.block(ring_spot(spot, -1), 0)
+        links.arrived(low, sem, self.right)
+        links.send(low, low, sem + 4, self.right)
+        high = self.block(ring_spot(spot, 1), 1)
+        links.arrived(high, sem + 2, self.left)
+        links.send(high, high, sem + 5, self.left)
+
+    def end(self):
+        links, sem, spot = self.links, self.sem, self.spot
+        links.arrived(self.block(ring_spot(spot, -1), 1), sem + 1, self.right)
+        links.arrived(self.block(ring_spot(spot, 1), 0), sem + 3, self.left)
+        links.arrived(self.block(ring_spot(spot, 2), 0), sem + 4, self.right)
+        links.arrived(self.block(ring_spot(spot, 2), 1), sem + 5, self.left)
+
+
+def add_into(target, *sources):
+    if len(target.shape) == 3:
+        for at in range(target.shape[0]):
+            add_into(target.at[at], *[source.at[at] for source in sources])
+        return
+    total = sources[0][...].astype(f32)
+    for source in sources[1:]:
+        total = total + source[...].astype(f32)
+    target[...] = total.astype(target.dtype)
+
+
+def greet(replica_spots, group_spots):
+    barrier = pltpu.get_barrier_semaphore()
+    for spot in replica_spots:
+        pl.semaphore_signal(barrier, inc=1, device_id={"replica": spot}, device_id_type=MESH)
+    for spot in group_spots:
+        pl.semaphore_signal(barrier, inc=1, device_id={"group": spot}, device_id_type=MESH)
+    pl.semaphore_wait(barrier, len(replica_spots) + len(group_spots))
+
+
+def grads_kernel(
+    n2t, dgu, act, dmlp, left_rows, right_rows, vec,
+    shared, part, own, zbuf, left_all, right_all, vec_all,
+    a_first, a_second, a_left, a_right, a_sum, a_first2, a_second2, a_left2, a_right2,
+    b_first, b_second, b_left, b_right, b_sum, b_first2, b_second2, b_left2, b_right2,
+    c_first, c_second, c_left, c_right, c_sum, c_first2, c_second2, c_left2, c_right2,
+    send_sems, recv_sems,
+):
+    group_at = lax.axis_index("group")
+    replica_at = lax.axis_index("replica")
+    x_at, y_at = replica_at // RING, lax.rem(replica_at, RING)
+    links = Links(send_sems, recv_sems)
+
+    def along_x(spot):
+        return {"replica": spot * RING + y_at}
+
+    def along_y(spot):
+        return {"replica": x_at * RING + spot}
+
+    peers = [ring_spot(group_at, step) for step in (1, 2, 3)]
+    greet(
+        [
+            ring_spot(x_at, 1) * RING + y_at,
+            ring_spot(x_at, -1) * RING + y_at,
+            x_at * RING + ring_spot(y_at, 1),
+            x_at * RING + ring_spot(y_at, -1),
+        ],
+        peers,
+    )
+    tok_sem = links.take(9)
+    for step, peer in enumerate(peers):
+        for at, (source, target) in enumerate(
+            [
+                (left_rows.at[peer], left_all.at[group_at]),
+                (right_rows, right_all.at[group_at]),
+                (vec, vec_all.at[group_at]),
+            ]
+        ):
+            links.send(source, target, tok_sem + 3 * step + at, {"group": peer})
+    left_all[group_at] = left_rows[group_at]
+    right_all[group_at] = right_rows[...]
+    vec_all[group_at] = vec[...]
+
+    def gate_up(tile, carry):
+        at = pl.multiple_of(tile * 256, 256)
+        block = jnp.dot(n2t[...], dgu[:, pl.ds(at, 256)], preferred_element_type=f32).astype(bf16)
+        block = block.reshape(ZDEV, TILES_R, 16, 256)
+        for z in range(ZDEV):
+            where = pl.multiple_of(tile * 256 + z * 2 * WIN, 128)
+            for r in range(TILES_R):
+                part[r // RING, r % RING, :, pl.ds(where, 256)] = block[z, r]
+        return carry
+
+    lax.fori_loop(0, 2 * WIN // 256, gate_up, 0)
+    shift = lax.rem(group_at, 2) * 64
+    for quarter in range(4):
+        rows = pl.ds(pl.multiple_of(shift + 304 * quarter, 16), 304)
+        block = jnp.dot(act[rows, :], dmlp[...], preferred_element_type=f32).astype(bf16)
+        block = block.reshape(19, 16, D)
+        for inner in range(19):
+            tile = 19 * quarter + inner
+            if tile < 3 * TILES_R:
+                r, at = tile // 3, DOWN_AT + D * (tile % 3)
+            else:
+                r, at = TILES_R + (tile - 3 * TILES_R) // 17, D * ((tile - 3 * TILES_R) % 17)
+            part[r // RING, r % RING, :, at : at + D] = block[inner]
+
+    def summers(cols, x_first, bufs):
+        first, second, left, right, total, first2, second2, left2, right2 = bufs
+        start, stop = cols
+
+        def big(spot, half):
+            span = pl.ds(2 * half, 2)
+            if x_first:
+                return part.at[spot, span, :, start:stop]
+            return part.at[span, spot, :, start:stop]
+
+        cuts = halves(0, stop - start)
+
+        def small(spot, half):
+            return total.at[spot, :, cuts[half][0] : cuts[half][1]]
+
+        def pair(buf):
+            return lambda half: buf.at[pl.ds(2 * half, 2)]
+
+        def cut(buf):
+            return lambda half: buf.at[:, cuts[half][0] : cuts[half][1]]
+
+        one = (x_at, along_x) if x_first else (y_at, along_y)
+        two = (y_at, along_y) if x_first else (x_at, along_x)
+        stage_one = RingSum(
+            links, *one, big, first, second, pair(left), pair(right), add_into
+        )
+        stage_two = RingSum(
+            links, *two, small, first2, second2, cut(left2), cut(right2), add_into
+        )
+
+        def result(half):
+            return own.at[:, start + cuts[half][0] : start + cuts[half][1]]
+
+        return stage_one, stage_two, pair(total), result
+
+    a_one, a_two, a_mid, a_result = summers(
+        PART_A, True,
+        (a_first, a_second, a_left, a_right, a_sum, a_first2, a_second2, a_left2, a_right2),
+    )
+    b_one, b_two, b_mid, b_result = summers(
+        PART_B, False,
+        (b_first, b_second, b_left, b_right, b_sum, b_first2, b_second2, b_left2, b_right2),
+    )
+    c_one, c_two, c_mid, c_result = summers(
+        PART_C, False,
+        (c_first, c_second, c_left, c_right, c_sum, c_first2, c_second2, c_left2, c_right2),
+    )
+    a_one.start()
+    b_one.start()
+    a_one.middle()
+    b_one.middle()
+    for step, peer in enumerate(peers):
+        source = ring_spot(group_at, -1 - step)
+        for at, target in enumerate((left_all, right_all, vec_all)):
+            links.arrived(target.at[source], tok_sem + 3 * step + at, {"group": peer})
+    for width, col, row in ((QKV, 0, 0), (D, QKV, OWN)):
+        total = jnp.dot(
+            left_all[0, row : row + OWN], right_all[0, :, col : col + width],
+            preferred_element_type=f32,
+        )
+        for z in range(1, ZDEV):
+            total = total + jnp.dot(
+                left_all[z, row : row + OWN], right_all[z, :, col : col + width],
+                preferred_element_type=f32,
+            )
+        total = total.astype(bf16).reshape(TILES_R, 16, width)
+        for r in range(TILES_R):
+            part[r // RING, r % RING, :, QO_AT + col : QO_AT + col + width] = total[r]
+    part[0, 0, :, VEC_AT:COLS] = (
+        vec_all[0] + vec_all[1] + vec_all[2] + vec_all[3]
+    ).astype(bf16)
+    for r in range(1, TILES_R):
+        part[r // RING, r % RING, :, VEC_AT:COLS] = jnp.zeros((16, COLS - VEC_AT), bf16)
+    c_one.start()
+    a_one.end(a_mid)
+    a_two.start()
+    b_one.end(b_mid)
+    b_two.start()
+    c_one.middle()
+    a_two.middle()
+    b_two.middle()
+    c_one.end(c_mid)
+    c_two.start()
+    a_two.end(a_result)
+    b_two.end(b_result)
+    slot_sem = links.take(3)
+    for step, peer in enumerate(peers):
+        where = pl.multiple_of(peer * 2 * WIN, 128)
+        links.send(
+            own.at[:, pl.ds(where, 2 * WIN)], zbuf.at[group_at], slot_sem + step, {"group": peer}
+        )
+    where = pl.multiple_of(group_at * 2 * WIN, 128)
+    zbuf[group_at] = own[:, pl.ds(where, 2 * WIN)]
+    c_two.middle()
+    c_two.end(c_result)
+    for step, peer in enumerate(peers):
+        links.arrived(zbuf.at[ring_spot(group_at, -1 - step)], slot_sem + step, {"group": peer})
+
+    @pl.when(replica_at < TILES_R)
+    def _():
+        for which in (0, 1):
+            base, at = which * FF, which * WIN
+            for z in range(ZDEV):
+                low = 128 if z % 2 else 0
+                high = WIN if z % 2 else WIN - 128
+                to = base + STARTS[z]
+                shared[x_at, y_at, :, to + low : to + high] = zbuf[z, :, at + low : at + high]
+            for z in (0, 2):
+                to = base + STARTS[z + 1]
+                shared[x_at, y_at, :, to : to + 128] = (
+                    zbuf[z, :, at + WIN - 128 : at + WIN] + zbuf[z + 1, :, at : at + 128]
+                )
+        shared[x_at, y_at, :, 2 * FF : 2 * FF + 512] = jnp.zeros((16, 512), bf16)
+        shared[x_at, y_at, :, DOWN_AT:COLS] = own[:, DOWN_AT:COLS]
+
+    @pl.when(replica_at >= TILES_R)
+    def _():
+        shared[x_at, y_at] = own[...]
+
+    def sharers(cols, x_first):
+        start, stop = cols
+        cuts = halves(start, stop)
+
+        def small(spot, half):
+            low, high = cuts[half]
+            if x_first:
+                return shared.at[spot, y_at, :, low:high]
+            return shared.at[x_at, spot, :, low:high]
+
+        def big(spot, half):
+            span = pl.ds(2 * half, 2)
+            if x_first:
+                return shared.at[span, spot, :, start:stop]
+            return shared.at[spot, span, :, start:stop]
+
+        one = (x_at, along_x) if x_first else (y_at, along_y)
+        two = (y_at, along_y) if x_first else (x_at, along_x)
+        return RingShare(links, *one, small), RingShare(links, *two, big)
+
+    a_one, a_two = sharers((0, 7680), False)
+    b_one, b_two = sharers((7680, COLS), True)
+    a_one.start()
+    b_one.start()
+    a_one.middle()
+    b_one.middle()
+    a_one.end()
+    a_two.start()
+    b_one.end()
+    b_two.start()
+    a_two.middle()
+    b_two.middle()
+    a_two.end()
+    b_two.end()
+    links.finish()
+
+
+def share_grads(n2t, dgu, act, dmlp, left_rows, right_rows, vec):
+    def bufs(cols):
+        width = cols[1] - cols[0]
+        low, high = [b - a for a, b in halves(0, width)]
+        shapes = [(2, 16, width), (2, 16, width), (4, 16, width), (4, 16, width), (4, 16, width)]
+        shapes = shapes + [(16, low), (16, high), (16, width), (16, width)]
+        return [pltpu.VMEM(shape, bf16) for shape in shapes]
+
+    vmem = pl.BlockSpec(memory_space=pltpu.VMEM)
+    sems = 9 + 3 + 6 * 6 + 4 * 6
+    return pl.pallas_call(
+        grads_kernel,
+        out_shape=jax.ShapeDtypeStruct((RING, RING, 16, COLS), bf16),
+        in_specs=[vmem] * 7,
+        out_specs=vmem,
+        scratch_shapes=[
+            pltpu.VMEM((RING, RING, 16, COLS), bf16),
+            pltpu.VMEM((16, COLS), bf16),
+            pltpu.VMEM((ZDEV, 16, 2 * WIN), bf16),
+            pltpu.VMEM((ZDEV, 2 * OWN, 2 * SPAN), bf16),
+            pltpu.VMEM((ZDEV, 2 * SPAN, QKV + D), bf16),
+            pltpu.VMEM((ZDEV, 16, 256), f32),
+            *bufs(PART_A),
+            *bufs(PART_B),
+            *bufs(PART_C),
+            pltpu.SemaphoreType.DMA((sems,)),
+            pltpu.SemaphoreType.DMA((sems,)),
+        ],
+        compiler_params=pltpu.CompilerParams(
+            collective_id=1, has_side_effects=True, vmem_limit_bytes=58 * 1024 * 1024
+        ),
+        name="grads",
+    )(n2t, dgu, act, dmlp, left_rows, right_rows, vec)
+
+
 def weight_grads(token_pieces, row_pieces, vector_sum):
-    perm = jnp.asarray(PERM, bf16)
     group_at = lax.axis_index("group")
-    normed_one, grad_mixed, context, grad_attn = (
-        token_pieces[:, :D],
-        token_pieces[:, D : D + QKV],
-        token_pieces[:, D + QKV : 2 * D + QKV],
-        token_pieces[:, 2 * D + QKV :],
-    )
-    normed_all, grad_gu, activated, grad_mlp = (
-        row_pieces[:, :D],
-        row_pieces[:, D : D + 2 * WIN],
-        row_pieces[:, D + 2 * WIN : D + 3 * WIN],
-        row_pieces[:, D + 3 * WIN :],
-    )
-
-    def outer(left, right):
-        return jnp.einsum("id,ie->de", left, right, preferred_element_type=f32).astype(bf16)
-
-    left_one = dot(normed_one, perm).astype(bf16)
-    left_out = dot(context, perm).astype(bf16)
-    left_two = dot(normed_all, perm).astype(bf16)
-    vec = vector_sum[0]
-    rows = jnp.stack(
-        [vec[:D].reshape(ZDEV, REPL, CHUNK), vec[D : 2 * D].reshape(ZDEV, REPL, CHUNK)], axis=2
-    ).reshape(ZDEV, REPL, 2 * CHUNK)
-    rows = jnp.concatenate([rows, vec[2 * D :].reshape(ZDEV, REPL, QKV // 64)], axis=2)
-    rows = jnp.pad(rows, ((0, 0), (0, 0), (0, QKV - rows.shape[-1])))
-    rows = jnp.transpose(rows, (1, 0, 2)).astype(bf16)
-    spot = jnp.arange(16)[None, None, :, None] == CHUNK
-    part_qkv = outer(left_one, grad_mixed).reshape(REPL, ZDEV, 16, QKV)
-    part_qkv = jnp.where(spot, rows[:, :, None, :], part_qkv)
-    part_out = outer(left_out, grad_attn).reshape(REPL, ZDEV, 16, D)
-    part_gu = outer(left_two, grad_gu).reshape(REPL, ZDEV, 16, 2 * WIN)
-    part_down = outer(activated, grad_mlp).reshape(REPL, WIN // REPL, D)
-
-    def scatter(part):
-        return lax.psum_scatter(part, "replica", scatter_dimension=0, tiled=False)
-
-    part_qkv, part_out, part_gu, part_down = map(scatter, (part_qkv, part_out, part_gu, part_down))
-    mixed = jnp.concatenate([part_qkv, part_out, part_gu], axis=-1)
-    mixed = lax.all_to_all(mixed, "group", split_axis=0, concat_axis=0, tiled=True)
-    joint = jnp.sum(mixed[:, :, : QKV + D].astype(f32), axis=0).astype(bf16)
-    gate = jnp.concatenate(
-        [mixed[z, :, QKV + D + SHIFTS[z] :][:, :BLOCK] for z in range(ZDEV)], axis=-1
-    )
-    up = jnp.concatenate(
-        [mixed[z, :, QKV + D + WIN + SHIFTS[z] :][:, :BLOCK] for z in range(ZDEV)], axis=-1
-    )
-    final = jnp.concatenate([joint, gate, up], axis=-1)
-    final = lax.all_gather(final, "replica", axis=0, tiled=False)
-    final_down = lax.all_gather(part_down, "replica", axis=0, tiled=True)
-    grad_down = lax.dynamic_slice_in_dim(final_down, (group_at % 2) * 64, BLOCK, 0)
-    body = final[:, :CHUNK].reshape(OWN, final.shape[-1]).astype(f32)
-    tail = final[:, CHUNK, :128].astype(f32)
-    grad_gain_attn = tail[:, :CHUNK].reshape(OWN)
-    grad_gain_ffn = tail[:, CHUNK : 2 * CHUNK].reshape(OWN)
-    grad_bias = tail[:, 2 * CHUNK : 2 * CHUNK + QKV // 64].reshape(QKV // 4)
+    normed_all = row_pieces[:, :D]
+    grad_gu = row_pieces[:, D : D + 2 * WIN]
+    activated = row_pieces[:, D + 2 * WIN : D + 3 * WIN]
+    grad_mlp = row_pieces[:, D + 3 * WIN :]
+    lefts = jnp.concatenate(
+        [
+            token_pieces[:, :D].reshape(2 * SPAN, ZDEV, OWN),
+            token_pieces[:, D + QKV : 2 * D + QKV].reshape(2 * SPAN, ZDEV, OWN),
+        ],
+        axis=2,
+    )
+    rights = jnp.concatenate(
+        [token_pieces[:, D : D + QKV], token_pieces[:, 2 * D + QKV :]], axis=1
+    )
+    vec = jnp.pad(vector_sum[0], (0, 16 * 256 - vector_sum.shape[1])).reshape(16, 256)
+    shared = share_grads(
+        normed_all.T, grad_gu, activated.T, grad_mlp, jnp.transpose(lefts, (1, 2, 0)), rights, vec
+    )
+    shared = shared.reshape(REPL, 16, COLS)
+
+    def rows_of(start, width):
+        block = shared[:TILES_R, :, start : start + width]
+        return block.reshape(OWN, width).astype(f32)
+
+    lead = shared[:TILES_R, :, DOWN_AT : DOWN_AT + 3 * D].reshape(TILES_R, 16, 3, D)
+    rest = shared[TILES_R:].reshape(2, 16, 17, D)
+    grad_down = jnp.concatenate(
+        [
+            jnp.transpose(lead, (0, 2, 1, 3)).reshape(-1, D),
+            jnp.transpose(rest, (0, 2, 1, 3)).reshape(-1, D),
+        ]
+    ).astype(f32)
+    vec = shared[0, :, VEC_AT:].reshape(16 * 256).astype(f32)
+
+    def own_part(start, width):
+        return lax.dynamic_slice_in_dim(vec, start + group_at * width, width, 0)
+
     return (
-        body[:, :QKV],
-        grad_bias,
-        body[:, QKV : QKV + D],
-        body[:, QKV + D : QKV + D + FF],
-        body[:, QKV + D + FF :],
-        grad_down.astype(f32),
-        grad_gain_attn,
-        grad_gain_ffn,
+        rows_of(QO_AT, QKV),
+        own_part(2 * D, QKV // ZDEV),
+        rows_of(QO_AT + QKV, D),
+        rows_of(0, FF),
+        rows_of(FF, FF),
+        grad_down,
+        own_part(0, OWN),
+        own_part(D, OWN),
     )
 
 

time: 893 us -> 622 us (0.70)
  waiting for transfers between devices: 540 us -> 175 us
  Pallas kernels: 0 us -> 109 us
  matrix products: 70.1 us -> 53.8 us
  blocking collectives: 104 us -> 90.9 us
  local copies, waits for them, and re-layouts: 78 us -> 89.1 us
    unnamed x18 -> x8, waiting for transfers between devices: 282 us -> 0.13 us
    pallas_call x0 -> x1, Pallas kernels: none -> 109 us  [share_grads(): pl.pallas_call(grads_kernel, out_shape=jax.ShapeDtypeStruct((RING, RING,...]
    all_gather x2 -> x0, waiting for transfers between devices: 86.1 us -> none  [the longest x1 58.1 us: weight_grads(): final = lax.all_gather(final, 'replica', axis=0, tiled=False)]
    dot_general x4 -> x0, matrix products: 18.4 us -> none  [outer(): jnp.einsum('id,ie->de', left, right, preferred_element_type=f32)]
    slice x8 -> x7, local copies, waits for them, and re-layouts: 0.23 us -> 14.1 us  [the longest x3 6.02 us: rows_of(): block = shared[:TILES_R, :, start:start + width]]
    all_to_all x1 -> x0, blocking collectives: 13.5 us -> none  [weight_grads(): lax.all_to_all(mixed, 'group', split_axis=0, concat_axis=0, tiled=True)]
    broadcast_in_dim x3 -> x1, local copies, waits for them, and re-layouts: 12 us -> 0.57 us  [on_device(): g[None]]
    convert_element_type x2 -> x0, local copies, waits for them, and re-layouts: 9.48 us -> none  [the longest x1 8.76 us: weight_grads(): body = final[:, :CHUNK].reshape(OWN, final.shape[-1]).astype(f32)]
  transfers between devices with their start and end apart: 23 -> 17, of which waited for: 19 -> 11; matrix products, arithmetic and copies ran while one was open for 15% -> 20% of each run, Pallas kernels for 0% -> 0%
where the time goes in v2:
time: 622 us; the launch traced here: 611 us
  waiting for transfers between devices  175 us (28%)
  Pallas kernels  109 us (18%)
  blocking collectives  90.9 us (15%)
  local copies, waits for them, and re-layouts  89.1 us (14%)
  other arithmetic  75 us (12%)
  matrix products  53.8 us (9%)
  between operations  15.9 us (3%)
    pallas_call x1, Pallas kernels, share_grads(): pl.pallas_call(grads_kernel, out_shape=jax.ShapeDtypeStruct((RING, RING,...  109 us
    all_gather x1, waiting for transfers between devices, gather_weights(): joint = lax.all_gather(joint, ('group', 'replica'), axis=0, tiled=False)  54.1 us
    all_gather x1, waiting for transfers between devices, gather_weights(): w_gu = lax.all_gather(pieces, 'replica', axis=0, tiled=False)  43.4 us
    reduce_scatter x2, waiting for transfers between devices, layer_backward(): lax.psum_scatter(grad_kv_all.astype(bf16), 'group', scatter_dimension=0,...  31.9 us
    all_gather x2, blocking collectives, layer_backward(): grad_mlp_all = lax.all_gather(grad_mlp, 'group', axis=0, tiled=True)  27.2 us
    all_gather x2, blocking collectives, layer_forward(): normed_all = lax.all_gather(normed_two, 'group', axis=0, tiled=True)  26.4 us
    dot_general x8, matrix products, dot_t(): return jnp.einsum('id,ed->ie', left, right, preferred_element_type=f32)  25.3 us
    all_gather x2, blocking collectives, layer_forward(): all_kv = lax.all_gather(local_kv, 'group', axis=0, tiled=True)  24.5 us
  transfers between devices with their start and end apart: 17, of which 11 were waited for; matrix products, arithmetic and copies ran while one was open for 20% of the time, Pallas kernels for 0%

profile of v2, /device:TPU:0, one launch (start us, length us, event | category | flops | bytes accessed | tf_op | source)
XLA Modules:
  0.0 610.9 jit_solution(18122737494332488517)
XLA Ops:
  13.3 12.8 %all_to_all.5 = bf16[4,16,2560]{2,1,0:T(8,128)(2,1)} all-to-all(bf16[4,16,2560]{2,1,0:T(8,128)(2,1)S(1)} %fusion.79), channel_id=1, replica_groups=mesh['section'=2,'group'=4,'replica'=16] {'group'}, dimensions={0} | all-to-all | bytes 655360 | tf_op jit(solution)/shard_map/all_to_all | solution.py:220
  29.5 54.1 %all-gather.6.cloned.1.call-done = bf16[1024,2048]{1,0:T(8,128)(2,1)} async-done(((bf16[16,2048]{1,0:T(8,128)(2,1)}), bf16[1024,2048]{1,0:T(8,128)(2,1)}) %all-gather.6.cloned.1.call-update) | async-done | bytes 4194320 | tf_op jit(solution)/shard_map/all_gather | solution.py:205
  83.5 6.0 reshape.645
  93.0 3.0 collective-permute-done
  96.1 43.4 %all-gather.8.cloned.1.call-done = bf16[64,16,2560]{2,1,0:T(8,128)(2,1)} async-done(((bf16[4,16,2560]{2,1,0:T(8,128)(2,1)}), bf16[64,16,2560]{2,1,0:T(8,128)(2,1)}) %all-gather.8.cloned.1.call-update) | async-done | bytes 5242896 | tf_op jit(solution)/shard_map/all_gather | solution.py:221
  139.5 3.0 slice_bitcast_fusion
  145.2 7.4 %reshape.653 = bf16[896,2560]{1,0:T(8,128)(2,1)} reshape(bf16[4,16,14,2560]{3,2,1,0:T(8,128)(2,1)} %copy.216) | data formatting | bytes 9175040 | tf_op jit(solution)/shard_map/reshape | solution.py:222
  152.6 5.5 broadcast_select_fusion.2
  163.6 12.5 %all_gather.32 = bf16[256,256]{1,0:T(8,128)(2,1)S(1)} all-gather(bf16[64,256]{1,0:T(8,128)(2,1)S(1)} %pad_maximum_fusion.14), channel_id=1, replica_groups=mesh['section'=2,'group'=4,'replica'=16] {'group'}, dimensions={0}, use_global_device_ids=true | all-gather | bytes 163840 | tf_op jit(solution)/shard_map/all_gather | solution.py:106
  179.8 13.2 %all_gather.33 = bf16[256,896]{1,0:T(8,128)(2,1)S(1)} all-gather(bf16[64,896]{1,0:T(8,128)(2,1)S(1)} %multiply_convert_fusion.9), channel_id=1, replica_groups=mesh['section'=2,'group'=4,'replica'=16] {'group'}, dimensions={0}, use_global_device_ids=true | all-gather | bytes 573440 | tf_op jit(solution)/shard_map/all_gather | solution.py:117
  193.0 3.9 fusion.8
  198.4 3.5 convolution_convert_fusion.1
  202.2 14.4 %all-gather.2 = bf16[1,1,256,896]{3,2,1,0:T(8,128)(2,1)} all-gather(bf16[1,1,64,896]{3,2,1,0:T(8,128)(2,1)S(1)} %constant_dynamic-slice_fusion), channel_id=4, replica_groups=mesh['section'=2,'group'=4,'replica'=16] {'group'}, dimensions={2}, use_global_device_ids=true | all-gather | bytes 573440 | tf_op jit(solution)/shard_map/all_gather | solution.py:136
  228.5 12.0 %all_gather.36 = bf16[256,256]{1,0:T(8,128)(2,1)S(1)} all-gather(bf16[64,256]{1,0:T(8,128)(2,1)S(1)} %pad_maximum_fusion.15), channel_id=1, replica_groups=mesh['section'=2,'group'=4,'replica'=16] {'group'}, dimensions={0}, use_global_device_ids=true | all-gather | bytes 163840 | tf_op jit(solution)/shard_map/all_gather | solution.py:106
  244.1 13.2 %all_gather.37 = bf16[256,896]{1,0:T(8,128)(2,1)S(1)} all-gather(bf16[64,896]{1,0:T(8,128)(2,1)S(1)} %multiply_convert_fusion.8), channel_id=1, replica_groups=mesh['section'=2,'group'=4,'replica'=16] {'group'}, dimensions={0}, use_global_device_ids=true | all-gather | bytes 573440 | tf_op jit(solution)/shard_map/all_gather | solution.py:117
  257.4 4.1 fusion.10
  261.5 3.9 constant_dynamic-update-slice_fusion.7
  267.4 4.6 fusion.33
  272.1 3.1 constant_dynamic-update-slice_fusion.5
  276.8 3.5 convolution_convert_fusion
  280.8 11.7 %reduce-scatter.11.cloned.1.call-done = bf16[64,896]{1,0:T(8,128)(2,1)} async-done(((bf16[256,896]{1,0:T(8,128)(2,1)}), bf16[64,896]{1,0:T(8,128)(2,1)}) %reduce-scatter.11.cloned.1.call-update) | async-done | bytes 114704 | tf_op jit(solution)/shard_map/reduce_scatter | solution.py:144
  302.1 14.3 %reduce-scatter.9.cloned.1.call-done = bf16[64,896]{1,0:T(8,128)(2,1)} async-done(((bf16[256,896]{1,0:T(8,128)(2,1)}), bf16[64,896]{1,0:T(8,128)(2,1)}) %reduce-scatter.9.cloned.1.call-update) | async-done | bytes 114704 | tf_op jit(solution)/shard_map/reduce_scatter | solution.py:122
  320.0 19.5 %reduce-scatter.13.cloned.1.call-done = bf16[64,256]{1,0:T(8,128)(2,1)} async-done(((bf16[256,256]{1,0:T(8,128)(2,1)}), bf16[64,256]{1,0:T(8,128)(2,1)}) %reduce-scatter.13.cloned.1.call-update) | async-done | bytes 32784 | tf_op jit(solution)/shard_map/reduce_scatter | solution.py:171
  347.6 12.8 %all_gather.39 = bf16[256,896]{1,0:T(8,128)(2,1)S(1)} all-gather(bf16[64,896]{1,0:T(8,128)(2,1)S(1)} %fusion.98), channel_id=1, replica_groups=mesh['section'=2,'group'=4,'replica'=16] {'group'}, dimensions={0}, use_global_device_ids=true | all-gather | bytes 573440 | tf_op jit(solution)/shard_map/all_gather | solution.py:136
  360.4 4.1 constant_dynamic-update-slice_fusion.3
  371.3 3.8 broadcast_select_fusion.5
  376.8 12.4 %reduce-scatter.15.cloned.1.call-done = bf16[64,896]{1,0:T(8,128)(2,1)} async-done(((bf16[256,896]{1,0:T(8,128)(2,1)}), bf16[64,896]{1,0:T(8,128)(2,1)}) %reduce-scatter.15.cloned.1.call-update) | async-done | bytes 114704 | tf_op jit(solution)/shard_map/reduce_scatter | solution.py:144
  412.2 12.4 %reduce-scatter.17.cloned.1.call-done = bf16[64,256]{1,0:T(8,128)(2,1)} async-done(((bf16[256,256]{1,0:T(8,128)(2,1)}), bf16[64,256]{1,0:T(8,128)(2,1)}) %reduce-scatter.17.cloned.1.call-update) | async-done | bytes 32784 | tf_op jit(solution)/shard_map/reduce_scatter | solution.py:171
  459.3 3.0 fusion.dgu
  462.3 109.3 %grads.1 = bf16[4,4,16,15232]{3,2,1,0:T(8,128)(2,1)} custom-call(bf16[896,512]{1,0:T(8,128)(2,1)} %copy.241.n2t, bf16[512,2560]{1,0:T(8,128)(2,1)} %fusion.dgu, bf16[1280,512]{1,0:T(8,128)(2,1)} %copy.242.act, bf16[512,896]{1,0:T(8,128)(2,1)} %get-tuple-element.112.dmlp, bf16[4,448,128]{2,1,0:T(8,128)(2,1)} %maximum_bitcast_fusion.2.left_rows, ...), custom_call_target="tpu_custom_call" | custom-call | tf_op jit(solution)/shard_map/grads/pallas_call | solution.py:609
  576.1 3.9 fusion.140
  582.9 3.6 reshape.675
  (403 shorter events, 157.0 us)
Async XLA Ops:
  7.2 76.3 %all-gather.6.cloned.1.call-start = ((), (), s32[]{:S(2)}) async-start(), calls=%async_computation.13 | async-start | bytes 4259840 | tf_op jit(solution)/shard_map/all_gather | solution.py:205
  11.9 127.6 %all-gather.8.cloned.1.call-start = ((), (), s32[]{:S(2)}) async-start(), calls=%async_computation.14 | async-start | bytes 5570560 | tf_op jit(solution)/shard_map/all_gather | solution.py:221
  26.1 195.8 %reduce-scatter.7.cloned.1.call-start = ((), (), s32[]{:S(2)}) async-start(), calls=%async_computation.7 | async-start | bytes 573440 | tf_op jit(solution)/shard_map/reduce_scatter | solution.py:122
  29.3 167.7 %collective-permute-start.3 = (bf16[1280,896]{1,0:T(8,128)(2,1)}, bf16[1280,896]{1,0:T(8,128)(2,1)}, u32[]{:S(2)}, u32[]{:S(2)}) collective-permute-start(bf16[1280,896]{1,0:T(8,128)(2,1)} %bitcast_dynamic-update-slice_fusion), channel_id=1, source_target_pairs={{0,64},{64,0},{1,65},{65,1},{2,66},{66,2},{3,67},{67,3},{4,68},{68... | collective-permute-start | bytes 6881288 | tf_op jit(solution)/shard_map/ppermute | solution.py:230
  89.6 63.1 %collective-permute-start.1 = (bf16[896,2048]{1,0:T(8,128)(2,1)}, bf16[896,2048]{1,0:T(8,128)(2,1)}, u32[]{:S(2)}, u32[]{:S(2)}) collective-permute-start(bf16[896,2048]{1,0:T(8,128)(2,1)} %reshape.645), channel_id=1, source_target_pairs={{0,64},{64,0},{1,65},{65,1},{2,66},{66,2},{3,67},{67,3},{4,68},{68... | collective-permute-start | bytes 11010056 | tf_op jit(solution)/shard_map/ppermute | solution.py:230
  90.1 126.6 %copy-start.55 = (f32[64]{0:T(128)}, f32[64]{0:T(128)S(1)}, u32[]{:S(2)}) copy-start(f32[64]{0:T(128)S(1)} %add_rsqrt_fusion.3) | copy-start | bytes 772
  91.5 4.5 collective-permute-start
  96.0 120.6 %copy-start.48 = (f32[896]{0:T(1024)}, f32[896]{0:T(1024)S(1)}, u32[]{:S(2)}) copy-start(f32[896]{0:T(1024)S(1)} %get-tuple-element.81) | copy-start | bytes 10756
  152.6 40.4 %collective-permute-start.2 = (bf16[896,2560]{1,0:T(8,128)(2,1)}, bf16[896,2560]{1,0:T(8,128)(2,1)}, u32[]{:S(2)}, u32[]{:S(2)}) collective-permute-start(bf16[896,2560]{1,0:T(8,128)(2,1)} %reshape.653), channel_id=1, source_target_pairs={{0,64},{64,0},{1,65},{65,1},{2,66},{66,2},{3,67},{67,3},{4,68},{68... | collective-permute-start | bytes 13762568 | tf_op jit(solution)/shard_map/ppermute | solution.py:230
  179.7 17.2 %copy-start.53 = (f32[64]{0:T(128)}, f32[64]{0:T(128)S(1)}, u32[]{:S(2)}) copy-start(f32[64]{0:T(128)S(1)} %add_rsqrt_fusion.2) | copy-start | bytes 772
  201.9 90.7 %reduce-scatter.11.cloned.1.call-start = ((), (), s32[]{:S(2)}) async-start(), calls=%async_computation.9 | async-start | bytes 573440 | tf_op jit(solution)/shard_map/reduce_scatter | solution.py:144
  202.2 115.8 %copy-start.19 = (f32[64,896]{1,0:T(8,128)}, f32[64,896]{1,0:T(8,128)S(1)}, u32[]{:S(2)}) copy-start(f32[64,896]{1,0:T(8,128)S(1)} %mul.579) | copy-start | bytes 688132
  223.0 120.6 %copy-start.17 = (bf16[64,896]{1,0:T(8,128)(2,1)}, bf16[64,896]{1,0:T(8,128)(2,1)S(1)}, u32[]{:S(2)}) copy-start(bf16[64,896]{1,0:T(8,128)(2,1)S(1)} %get-tuple-element.105) | copy-start | bytes 344068
  272.1 44.3 %reduce-scatter.9.cloned.1.call-start = ((), (), s32[]{:S(2)}) async-start(), calls=%async_computation.8 | async-start | bytes 573440 | tf_op jit(solution)/shard_map/reduce_scatter | solution.py:122
  276.8 17.3 %copy-start.44 = (bf16[2,1,64,896]{3,2,1,0:T(8,128)(2,1)S(1)}, bf16[2,1,64,896]{3,2,1,0:T(8,128)(2,1)}, u32[]{:S(2)}) copy-start(bf16[2,1,64,896]{3,2,1,0:T(8,128)(2,1)} %param.12) | copy-start | bytes 688132
  280.4 59.1 %reduce-scatter.13.cloned.1.call-start = ((), (), s32[]{:S(2)}) async-start(), calls=%async_computation.10 | async-start | bytes 163840 | tf_op jit(solution)/shard_map/reduce_scatter | solution.py:171
  295.2 51.3 %copy-start.12 = (f32[64,896]{1,0:T(8,128)}, f32[64,896]{1,0:T(8,128)S(1)}, u32[]{:S(2)}) copy-start(f32[64,896]{1,0:T(8,128)S(1)} %fusion.103) | copy-start | bytes 688132
  300.5 15.9 %copy-start.51 = (f32[896]{0:T(1024)S(1)}, f32[896]{0:T(1024)}, u32[]{:S(2)}) copy-start(f32[896]{0:T(1024)} %copy-done.50) | copy-start | bytes 10756
  300.5 15.8 %copy-start.58 = (f32[64]{0:T(128)S(1)}, f32[64]{0:T(128)}, u32[]{:S(2)}) copy-start(f32[64]{0:T(128)} %copy-done.57) | copy-start | bytes 772
  302.0 87.2 %reduce-scatter.15.cloned.1.call-start = ((), (), s32[]{:S(2)}) async-start(), calls=%async_computation.11 | async-start | bytes 573440 | tf_op jit(solution)/shard_map/reduce_scatter | solution.py:144
  318.0 1.3 collective-permute-start.4
  318.7 27.8 %copy-start.32 = (bf16[64,896]{1,0:T(8,128)(2,1)}, bf16[64,896]{1,0:T(8,128)(2,1)S(1)}, u32[]{:S(2)}) copy-start(bf16[64,896]{1,0:T(8,128)(2,1)S(1)} %get-tuple-element.89) | copy-start | bytes 344068
  319.3 27.2 %copy-start.59 = (f32[64]{0:T(128)S(1)}, f32[64]{0:T(128)}, u32[]{:S(2)}) copy-start(f32[64]{0:T(128)} %copy-done.57) | copy-start | bytes 772
  340.8 19.6 %copy-start.7 = (f32[256,2560]{1,0:T(8,128)S(1)}, f32[256,2560]{1,0:T(8,128)}, u32[]{:S(2)}) copy-start(f32[256,2560]{1,0:T(8,128)} %copy-done.6) | copy-start | bytes 7864324
  347.6 18.2 %slice-start.2 = ((s8[4587520]{0:T(1024)(128)(4,1)}), s8[4194304]{0:T(1024)(128)(4,1)S(1)}, s32[]{:S(2)}) async-start(s8[4587520]{0:T(1024)(128)(4,1)} %bitcast.234), calls=%async_computation.17 | async-start | bytes 8388608
  368.1 56.5 %reduce-scatter.17.cloned.1.call-start = ((), (), s32[]{:S(2)}) async-start(), calls=%async_computation.12 | async-start | bytes 163840 | tf_op jit(solution)/shard_map/reduce_scatter | solution.py:171
  375.2 74.7 %collective-permute-start.6 = (bf16[256,5632]{1,0:T(8,128)(2,1)}, bf16[256,5632]{1,0:T(8,128)(2,1)}, u32[]{:S(2)}, u32[]{:S(2)}) collective-permute-start(bf16[256,5632]{1,0:T(8,128)(2,1)} %get-tuple-element.115), channel_id=1, source_target_pairs={{0,64},{64,0},{1,65},{65,1},{2,66},{66,2},{3,67},{67,3},{4,68},{68... | collective-permute-start | bytes 8650760 | tf_op jit(solution)/shard_map/ppermute | solution.py:230
  406.6 23.4 %copy-start.49 = (f32[896]{0:T(1024)S(1)}, f32[896]{0:T(1024)}, u32[]{:S(2)}) copy-start(f32[896]{0:T(1024)} %copy-done.48) | copy-start | bytes 10756
  406.6 23.4 %copy-start.56 = (f32[64]{0:T(128)S(1)}, f32[64]{0:T(128)}, u32[]{:S(2)}) copy-start(f32[64]{0:T(128)} %copy-done.55) | copy-start | bytes 772
  432.7 5.1 collective-permute-start.8
  435.7 5.1 collective-permute-start.7
  437.1 1.8 collective-permute-start.5
  (52 other events, 196.1 us)
Sparse Core Ops, SparseCore 0:
  12.0 71.4 all-gather.5
  85.7 53.7 all-gather.7
  202.0 19.8 reduce-scatter.6
  272.2 20.3 reduce-scatter.10
  295.4 20.8 reduce-scatter.8
  319.2 20.2 reduce-scatter.12
  368.2 20.9 reduce-scatter.14
  404.4 20.1 reduce-scatter.16

commit v3 on v2

--- a/solution.py
+++ b/solution.py
@@ -33,19 +33,6 @@
     return lax.rsqrt(jnp.mean(values * values, axis=-1, keepdims=True) + eps)
 
 
-def rotate_half(values):
-    half_len = values.shape[-1] // 2
-    return jnp.concatenate([-values[..., half_len:], values[..., :half_len]], axis=-1)
-
-
-def norm_back(grad_norm, values, scale_rows, gain_vec):
-    scaled = grad_norm * gain_vec
-    row_inner = jnp.mean(scaled * values, axis=-1, keepdims=True)
-    grad_in = scale_rows * (scaled - values * scale_rows * scale_rows * row_inner)
-    grad_gain = jnp.sum(grad_norm * values * scale_rows, axis=0)
-    return (grad_in, grad_gain)
-
-
 def doc_tables(doc_lens, group_at):
     doc_ends = jnp.cumsum(doc_lens)
     doc_starts = doc_ends - doc_lens
@@ -62,172 +49,12 @@
     )
     inv_freqs = rope_base ** (-jnp.arange(0, HEAD_DIM, 2, dtype=f32) / HEAD_DIM)
     angles = (own_spots - own_begin).astype(f32)[:, None] * inv_freqs[None, :]
-    angles = jnp.concatenate([angles, angles], axis=1)
-    return (allowed, jnp.cos(angles)[:, None, :], jnp.sin(angles)[:, None, :])
-
-
-def split_kv(all_kv):
-    key_rows = all_kv[:, :KV_WIDTH].reshape(ROW, KV_HEADS, HEAD_DIM)
-    value_rows = all_kv[:, KV_WIDTH:].reshape(ROW, KV_HEADS, HEAD_DIM)
-    return (key_rows, value_rows)
-
-
-def score_block(query_rot, key_rows, allowed):
-    grouped = query_rot.reshape(SPAN, KV_HEADS, GROUPS, HEAD_DIM)
-    scores = (
-        jnp.einsum("ikgd,jkd->kgij", grouped, key_rows, preferred_element_type=f32)
-        * HEAD_DIM ** (-0.5)
-    )
-    return jnp.where(allowed[None, None], scores, -jnp.inf)
-
-
-def dot(left, right):
-    return jnp.dot(left, right, preferred_element_type=f32)
-
-
-def dot_t(left, right):
-    return jnp.einsum("id,ed->ie", left, right, preferred_element_type=f32)
-
-
-def layer_forward(entering, weights, tables):
-    w_qo, w_gu, w_down, b_qkv, gain_attn, gain_ffn = weights
-    allowed, cosine, sine_table = tables
-    values = entering.astype(f32)
-    scale_one = rms_scale(values)
-    normed_one = (values * scale_one * gain_attn).astype(bf16)
-    mixed_qkv = dot(normed_one, w_qo[:, :QKV]) + b_qkv
-    query_pre = mixed_qkv[:, :D].reshape(SPAN, HEADS, HEAD_DIM)
-    key_pre = mixed_qkv[:, D : D + KV_WIDTH].reshape(SPAN, KV_HEADS, HEAD_DIM)
-    query_rot = (query_pre * cosine + rotate_half(query_pre) * sine_table).astype(bf16)
-    key_rot = (key_pre * cosine + rotate_half(key_pre) * sine_table).astype(bf16)
-    local_kv = jnp.concatenate(
-        [key_rot.reshape(SPAN, KV_WIDTH), mixed_qkv[:, D + KV_WIDTH :].astype(bf16)], axis=1
-    )
-    all_kv = lax.all_gather(local_kv, "group", axis=0, tiled=True)
-    key_rows, value_rows = split_kv(all_kv)
-    scores = score_block(query_rot, key_rows, allowed)
-    row_top = jnp.max(scores, axis=-1, keepdims=True)
-    log_total = row_top + jnp.log(jnp.sum(jnp.exp(scores - row_top), axis=-1, keepdims=True))
-    attn_probs = jnp.exp(scores - log_total).astype(bf16)
-    context = jnp.einsum("kgij,jkd->ikgd", attn_probs, value_rows, preferred_element_type=f32)
-    context = context.reshape(SPAN, D).astype(bf16)
-    hidden = values + dot(context, w_qo[:, QKV:])
-    scale_two = rms_scale(hidden)
-    normed_two = (hidden * scale_two * gain_ffn).astype(bf16)
-    normed_all = lax.all_gather(normed_two, "group", axis=0, tiled=True)
-    gate_up = dot(normed_all, w_gu)
-    gate_proj, up_proj = gate_up[:, :WIN], gate_up[:, WIN:]
-    activated = (jax.nn.silu(gate_proj) * up_proj).astype(bf16)
-    partial = dot(activated, w_down).astype(bf16)
-    mlp = lax.psum_scatter(partial, "group", scatter_dimension=0, tiled=True).astype(f32)
-    output = (hidden + mlp).astype(bf16)
-    kept = (values, scale_one, normed_one, query_rot, all_kv, log_total, context, hidden)
-    kept = kept + (scale_two, normed_all, gate_up, activated)
-    return (output, kept)
-
-
-def layer_backward(grad_out, kept, weights, tables):
-    values, scale_one, normed_one, query_rot, all_kv, log_total, context, hidden = kept[:8]
-    scale_two, normed_all, gate_up, activated = kept[8:]
-    w_qo, w_gu, w_down, b_qkv, gain_attn, gain_ffn = weights
-    allowed, cosine, sine_table = tables
-    gate_proj, up_proj = gate_up[:, :WIN], gate_up[:, WIN:]
-    grad_mlp = grad_out.astype(bf16)
-    grad_mlp_all = lax.all_gather(grad_mlp, "group", axis=0, tiled=True)
-    grad_act = dot_t(grad_mlp_all, w_down)
-    sigma_gate = jax.nn.sigmoid(gate_proj)
-    silu_gate = gate_proj * sigma_gate
-    grad_gate = grad_act * up_proj * sigma_gate * (1.0 + gate_proj * (1.0 - sigma_gate))
-    grad_up = grad_act * silu_gate
-    grad_gu = jnp.concatenate([grad_gate.astype(bf16), grad_up.astype(bf16)], axis=1)
-    partial = dot_t(grad_gu, w_gu).astype(bf16)
-    grad_norm_two = lax.psum_scatter(
-        partial, "group", scatter_dimension=0, tiled=True
-    ).astype(f32)
-    back_two, grad_gain_ffn = norm_back(grad_norm_two, hidden, scale_two, gain_ffn)
-    grad_hidden = grad_out + back_two
-    grad_attn = grad_hidden.astype(bf16)
-    grad_context = dot_t(grad_attn, w_qo[:, QKV:]).astype(bf16)
-    grad_context = grad_context.reshape(SPAN, KV_HEADS, GROUPS, HEAD_DIM)
-    key_rows, value_rows = split_kv(all_kv)
-    grouped = query_rot.reshape(SPAN, KV_HEADS, GROUPS, HEAD_DIM)
-    attn_probs = jnp.exp(score_block(query_rot, key_rows, allowed) - log_total)
-    grad_probs = jnp.einsum("ikgd,jkd->kgij", grad_context, value_rows, preferred_element_type=f32)
-    row_inner = jnp.sum(attn_probs * grad_probs, axis=-1, keepdims=True)
-    grad_scores = (attn_probs * (grad_probs - row_inner)).astype(bf16)
-    score_scale = HEAD_DIM ** (-0.5)
-    grad_query = jnp.einsum("kgij,jkd->ikgd", grad_scores, key_rows, preferred_element_type=f32)
-    grad_query = grad_query.reshape(SPAN, HEADS, HEAD_DIM) * score_scale
-    grad_key_all = (
-        jnp.einsum("kgij,ikgd->jkd", grad_scores, grouped, preferred_element_type=f32)
-        * score_scale
-    )
-    grad_value_all = jnp.einsum(
-        "kgij,ikgd->jkd", attn_probs.astype(bf16), grad_context, preferred_element_type=f32
-    )
-    grad_kv_all = jnp.concatenate(
-        [grad_key_all.reshape(ROW, KV_WIDTH), grad_value_all.reshape(ROW, KV_WIDTH)], axis=1
-    )
-    grad_kv = lax.psum_scatter(
-        grad_kv_all.astype(bf16), "group", scatter_dimension=0, tiled=True
-    ).astype(f32)
-    grad_key = grad_kv[:, :KV_WIDTH].reshape(SPAN, KV_HEADS, HEAD_DIM)
-    query_back = grad_query * cosine - rotate_half(grad_query * sine_table)
-    key_back = grad_key * cosine - rotate_half(grad_key * sine_table)
-    grad_mixed = jnp.concatenate(
-        [query_back.reshape(SPAN, D), key_back.reshape(SPAN, KV_WIDTH), grad_kv[:, KV_WIDTH:]],
-        axis=1,
-    ).astype(bf16)
-    grad_bias = jnp.sum(grad_mixed.astype(f32), axis=0)
-    grad_norm_one = dot_t(grad_mixed, w_qo[:, :QKV])
-    back_one, grad_gain_attn = norm_back(grad_norm_one, values, scale_one, gain_attn)
-    grad_in = grad_hidden + back_one
-    pieces = (
-        jnp.concatenate([normed_one, grad_mixed, context, grad_attn], axis=1),
-        jnp.concatenate([normed_all, grad_gu, activated, grad_mlp_all], axis=1),
-        jnp.concatenate([grad_gain_attn, grad_gain_ffn, grad_bias])[None],
-    )
-    return (grad_in, pieces)
-
-
-def gather_weights(w_qkv, b_qkv, w_out, w_gate, w_up, w_down, norm_attn, norm_ffn):
-    group_at = lax.axis_index("group")
-    replica_at = lax.axis_index("replica")
-
-    def own_rows(block):
-        return lax.dynamic_slice_in_dim(block, replica_at * CHUNK, CHUNK, 0)
-
-    vectors = jnp.concatenate([norm_attn, norm_ffn, b_qkv])
-    joint = jnp.concatenate([own_rows(w_qkv), own_rows(w_out)], axis=1)
-    extra = jnp.zeros((2, joint.shape[1]), bf16)
-    extra = lax.dynamic_update_slice(extra, vectors[None], (0, 0))
-    joint = jnp.concatenate([joint, extra], axis=0)
-    joint = lax.all_gather(joint, ("group", "replica"), axis=0, tiled=False)
-    joint = joint.reshape(ZDEV, REPL, 16, joint.shape[-1])
-    w_qo = joint[:, :, :CHUNK].reshape(D, QKV + D)
-    vectors = joint[:, 0, CHUNK, : vectors.shape[0]]
-    gain_attn = vectors[:, :OWN].reshape(D)
-    gain_ffn = vectors[:, OWN : 2 * OWN].reshape(D)
-    bias = vectors[:, 2 * OWN :].reshape(QKV)
-    gate_rows, up_rows = own_rows(w_gate), own_rows(w_up)
-    pieces = jnp.stack(
-        [
-            jnp.concatenate([gate_rows[:, s : s + WIN], up_rows[:, s : s + WIN]], axis=1)
-            for s in STARTS
-        ]
-    )
-    pieces = jnp.pad(pieces, ((0, 0), (0, 2), (0, 0)))
-    pieces = lax.all_to_all(pieces, "group", split_axis=0, concat_axis=0, tiled=True)
-    w_gu = lax.all_gather(pieces, "replica", axis=0, tiled=False)
-    w_gu = jnp.transpose(w_gu[:, :, :CHUNK], (1, 0, 2, 3)).reshape(D, 2 * WIN)
-    padded_down = lax.dynamic_update_slice(
-        jnp.zeros((WIN, D), bf16), w_down, ((group_at % 2) * 64, 0)
-    )
-    return (w_qo, w_gu, padded_down, jnp.concatenate([bias, gain_attn, gain_ffn])[None])
-
-
-def swap(value):
-    return lax.ppermute(value, "section", [(0, 1), (1, 0)])
+    cosine, sine = jnp.cos(angles), jnp.sin(angles)
+    blank = jnp.zeros_like(sine)
+    cosine = jnp.concatenate([cosine] * 4, axis=1)
+    sine_up = jnp.concatenate([-sine, blank] * 2, axis=1)
+    sine_down = jnp.concatenate([blank, sine] * 2, axis=1)
+    return (allowed.astype(f32), cosine, sine_up, sine_down)
 
 
 MESH = pl.DeviceIdType.MESH
@@ -323,10 +150,16 @@
 
 
 class RingShare:
-    def __init__(self, links, spot, device_at, block):
-        self.links, self.spot, self.block = links, spot, block
+    def __init__(self, links, spot, device_at, block, sibling=None):
+        self.links, self.spot, self.block, self.sibling = links, spot, block, sibling
         self.right, self.left = device_at(ring_spot(spot, 1)), device_at(ring_spot(spot, -1))
         self.sem = links.take(6)
+        self.twin = links.take(8) if sibling else 0
+
+    def pass_on(self, steps, half):
+        if self.sibling:
+            view = self.block(ring_spot(self.spot, steps), half)
+            self.links.send(view, view, self.twin + 2 * (steps % RING) + half, self.sibling)
 
     def start(self):
         send, sem = self.links.send, self.sem
@@ -335,22 +168,36 @@
         send(high, high, sem + 2, self.left)
         send(high, high, sem + 1, self.right)
         send(low, low, sem + 3, self.left)
+        self.pass_on(0, 0)
+        self.pass_on(0, 1)
 
     def middle(self):
         links, sem, spot = self.links, self.sem, self.spot
         low = self.block(ring_spot(spot, -1), 0)
         links.arrived(low, sem, self.right)
         links.send(low, low, sem + 4, self.right)
+        self.pass_on(-1, 0)
         high = self.block(ring_spot(spot, 1), 1)
         links.arrived(high, sem + 2, self.left)
         links.send(high, high, sem + 5, self.left)
+        self.pass_on(1, 1)
 
     def end(self):
         links, sem, spot = self.links, self.sem, self.spot
-        links.arrived(self.block(ring_spot(spot, -1), 1), sem + 1, self.right)
-        links.arrived(self.block(ring_spot(spot, 1), 0), sem + 3, self.left)
-        links.arrived(self.block(ring_spot(spot, 2), 0), sem + 4, self.right)
-        links.arrived(self.block(ring_spot(spot, 2), 1), sem + 5, self.left)
+        for steps, half, at, device in (
+            (-1, 1, 1, self.right),
+            (1, 0, 3, self.left),
+            (2, 0, 4, self.right),
+            (2, 1, 5, self.left),
+        ):
+            links.arrived(self.block(ring_spot(spot, steps), half), sem + at, device)
+            self.pass_on(steps, half)
+
+    def end_twin(self, twin_block):
+        for steps in range(RING):
+            for half in (0, 1):
+                view = twin_block(ring_spot(self.spot, steps), half)
+                self.links.arrived(view, self.twin + 2 * steps + half, self.sibling)
 
 
 def add_into(target, *sources):
@@ -364,18 +211,18 @@
     target[...] = total.astype(target.dtype)
 
 
-def greet(replica_spots, group_spots):
+def greet(replica_spots, group_spots, section_spots=()):
     barrier = pltpu.get_barrier_semaphore()
-    for spot in replica_spots:
-        pl.semaphore_signal(barrier, inc=1, device_id={"replica": spot}, device_id_type=MESH)
-    for spot in group_spots:
-        pl.semaphore_signal(barrier, inc=1, device_id={"group": spot}, device_id_type=MESH)
-    pl.semaphore_wait(barrier, len(replica_spots) + len(group_spots))
+    spots = {"replica": replica_spots, "group": group_spots, "section": section_spots}
+    for axis, members in spots.items():
+        for spot in members:
+            pl.semaphore_signal(barrier, inc=1, device_id={axis: spot}, device_id_type=MESH)
+    pl.semaphore_wait(barrier, sum(map(len, spots.values())))
 
 
 def grads_kernel(
-    n2t, dgu, act, dmlp, left_rows, right_rows, vec,
-    shared, part, own, zbuf, left_all, right_all, vec_all,
+    n2_rows, dgu, act_rows, dmlp, left_tokens, right_tokens, vecs,
+    shared, n2t, act, left_rows, right_rows, vec, part, own, zbuf, left_all, right_all, vec_all,
     a_first, a_second, a_left, a_right, a_sum, a_first2, a_second2, a_left2, a_right2,
     b_first, b_second, b_left, b_right, b_sum, b_first2, b_second2, b_left2, b_right2,
     c_first, c_second, c_left, c_right, c_sum, c_first2, c_second2, c_left2, c_right2,
@@ -402,6 +249,12 @@
         ],
         peers,
     )
+    right_rows[...] = right_tokens[...].reshape(2 * SPAN, QKV + D)
+    vec[...] = vecs[0] + vecs[1]
+    tall = left_tokens[...].reshape(2 * SPAN, 2 * D).T
+    for z in range(ZDEV):
+        left_rows[z, :OWN] = tall[OWN * z : OWN * (z + 1)]
+        left_rows[z, OWN:] = tall[D + OWN * z : D + OWN * (z + 1)]
     tok_sem = links.take(9)
     for step, peer in enumerate(peers):
         for at, (source, target) in enumerate(
@@ -415,6 +268,9 @@
     left_all[group_at] = left_rows[group_at]
     right_all[group_at] = right_rows[...]
     vec_all[group_at] = vec[...]
+
+    n2t[...] = n2_rows[...].T
+    act[...] = act_rows[...].T
 
     def gate_up(tile, carry):
         at = pl.multiple_of(tile * 256, 256)
@@ -596,7 +452,7 @@
     links.finish()
 
 
-def share_grads(n2t, dgu, act, dmlp, left_rows, right_rows, vec):
+def share_grads(n2, dgu, act, dmlp, lefts, rights, vecs):
     def bufs(cols):
         width = cols[1] - cols[0]
         low, high = [b - a for a, b in halves(0, width)]
@@ -612,6 +468,11 @@
         in_specs=[vmem] * 7,
         out_specs=vmem,
         scratch_shapes=[
+            pltpu.VMEM((D, 2 * ROW), bf16),
+            pltpu.VMEM((WIN, 2 * ROW), bf16),
+            pltpu.VMEM((ZDEV, 2 * OWN, 2 * SPAN), bf16),
+            pltpu.VMEM((2 * SPAN, QKV + D), bf16),
+            pltpu.VMEM((16, 256), f32),
             pltpu.VMEM((RING, RING, 16, COLS), bf16),
             pltpu.VMEM((16, COLS), bf16),
             pltpu.VMEM((ZDEV, 16, 2 * WIN), bf16),
@@ -628,28 +489,19 @@
             collective_id=1, has_side_effects=True, vmem_limit_bytes=58 * 1024 * 1024
         ),
         name="grads",
-    )(n2t, dgu, act, dmlp, left_rows, right_rows, vec)
-
-
-def weight_grads(token_pieces, row_pieces, vector_sum):
+    )(n2, dgu, act, dmlp, lefts, rights, vecs)
+
+
+def weight_grads(n2, dgu, act, dmlp, lefts, rights, vecs):
     group_at = lax.axis_index("group")
-    normed_all = row_pieces[:, :D]
-    grad_gu = row_pieces[:, D : D + 2 * WIN]
-    activated = row_pieces[:, D + 2 * WIN : D + 3 * WIN]
-    grad_mlp = row_pieces[:, D + 3 * WIN :]
-    lefts = jnp.concatenate(
-        [
-            token_pieces[:, :D].reshape(2 * SPAN, ZDEV, OWN),
-            token_pieces[:, D + QKV : 2 * D + QKV].reshape(2 * SPAN, ZDEV, OWN),
-        ],
-        axis=2,
-    )
-    rights = jnp.concatenate(
-        [token_pieces[:, D : D + QKV], token_pieces[:, 2 * D + QKV :]], axis=1
-    )
-    vec = jnp.pad(vector_sum[0], (0, 16 * 256 - vector_sum.shape[1])).reshape(16, 256)
     shared = share_grads(
-        normed_all.T, grad_gu, activated.T, grad_mlp, jnp.transpose(lefts, (1, 2, 0)), rights, vec
+        n2.reshape(2 * ROW, D),
+        dgu.reshape(2 * ROW, 2 * WIN),
+        act.reshape(2 * ROW, WIN),
+        dmlp.reshape(2 * ROW, D),
+        lefts,
+        rights,
+        vecs,
     )
     shared = shared.reshape(REPL, 16, COLS)
 
@@ -672,14 +524,590 @@
 
     return (
         rows_of(QO_AT, QKV),
-        own_part(2 * D, QKV // ZDEV),
+        own_part(0, QKV // ZDEV),
         rows_of(QO_AT + QKV, D),
         rows_of(0, FF),
         rows_of(FF, FF),
         grad_down,
-        own_part(0, OWN),
-        own_part(D, OWN),
-    )
+        own_part(QKV, OWN),
+        own_part(QKV + D, OWN),
+    )
+
+
+PAIRS = HEADS // 2
+KINDS = (((0, 1, 2, 3), 0), ((0, 1, 2), 1), ((4, 5, 6), 2), ((3, 4, 5, 6), 3))
+SCALE = HEAD_DIM ** (-0.5)
+TILE = 256
+
+
+def dot_nt(left, right):
+    return lax.dot_general(left, right, (((1,), (1,)), ((), ())), preferred_element_type=f32)
+
+
+def dot_tn(left, right):
+    return lax.dot_general(left, right, (((0,), (0,)), ((), ())), preferred_element_type=f32)
+
+
+def spread(pair):
+    low = lax.broadcasted_iota(jnp.int32, pair.shape, 1) < HEAD_DIM
+    wide = pair.astype(f32)
+    turned = pltpu.roll(wide, HEAD_DIM, 1)
+    zero = jnp.zeros_like(wide)
+    members = (
+        jnp.where(low, wide, zero),
+        jnp.where(low, zero, turned),
+        jnp.where(low, turned, zero),
+        jnp.where(low, zero, wide),
+    )
+    return [member.astype(bf16) for member in members]
+
+
+def unspread(kinds):
+    low = lax.broadcasted_iota(jnp.int32, kinds[0].shape, 1) < HEAD_DIM
+    straight = jnp.where(low, kinds[0], kinds[3])
+    crossed = jnp.where(low, kinds[2], kinds[1])
+    return straight + pltpu.roll(crossed, HEAD_DIM, 1)
+
+
+def stack_pairs(tokens, kind):
+    return jnp.concatenate(
+        [tokens[:, 2 * HEAD_DIM * p : 2 * HEAD_DIM * (p + 1)] for p in KINDS[kind][0]], axis=0
+    )
+
+
+def join_pairs(kinds):
+    found = [None] * PAIRS
+    for kind, (pairs, _) in enumerate(KINDS):
+        for at, p in enumerate(pairs):
+            part = kinds[kind][SPAN * at : SPAN * (at + 1)]
+            found[p] = part if found[p] is None else found[p] + part
+    return jnp.concatenate(found, axis=1)
+
+
+def turn(values, cosine, sine_up, sine_down, sign):
+    tiles = []
+    for at in range(values.shape[1] // 128):
+        tile = values[:, 128 * at : 128 * (at + 1)]
+        up = pltpu.roll(tile, 128 - HEAD_DIM // 2, 1)
+        down = pltpu.roll(tile, HEAD_DIM // 2, 1)
+        tiles.append(tile * cosine + sign * (up * sine_up + down * sine_down))
+    return jnp.concatenate(tiles, axis=1)
+
+
+def layers_kernel(
+    tokens, cotangent, mask, cosine, sine_up, sine_down, vectors, joint_hbm, wide_hbm, down_hbm,
+    acts, grads_in, out_n2, out_dgu, out_act, out_dmlp, out_left, out_right, out_vec,
+    joint, wide, down, xs, n1s, qs, kvs, probs, ctx, hid, n2s, gus, act, ysend, yrecv,
+    dys, dmlp, dgu, dn2, dsend, drecv, dkvsend, dkvrecv, lefts, rights, vecs, igs,
+    send_sems, recv_sems, load_sems, away_send, away_recv, stay_sems,
+):
+    section_at = lax.axis_index("section")
+    group_at = lax.axis_index("group")
+    other = 1 - section_at
+    peers = [ring_spot(group_at, step) for step in (1, 2, 3)]
+    greet([], peers, [other])
+
+    def load(layer, which):
+        source, target = [
+            (joint_hbm.at[layer], joint.at[layer]),
+            (wide_hbm.at[layer, :, pl.ds(0, TILES_R)], wide.at[layer]),
+            (down_hbm.at[layer], down.at[layer]),
+        ][which]
+        return pltpu.make_async_copy(source, target, load_sems.at[layer, which])
+
+    for layer in (0, 1):
+        for which in range(3):
+            load(layer, which).start()
+
+    def exchange(layer, which, source, target):
+        copies = []
+        for step, peer in enumerate(peers):
+            copy = pltpu.make_async_remote_copy(
+                src_ref=source(peer),
+                dst_ref=target(group_at),
+                send_sem=send_sems.at[layer, which, step],
+                recv_sem=recv_sems.at[layer, which, step],
+                device_id={"group": peer},
+                device_id_type=MESH,
+            )
+            copy.start()
+            copies.append(copy)
+
+        def finish():
+            for step, peer in enumerate(peers):
+                landed = target(ring_spot(group_at, -1 - step))
+                pltpu.make_async_remote_copy(
+                    src_ref=landed,
+                    dst_ref=landed,
+                    send_sem=send_sems.at[layer, which, step],
+                    recv_sem=recv_sems.at[layer, which, step],
+                    device_id={"group": peer},
+                    device_id_type=MESH,
+                ).wait_recv()
+            for copy in copies:
+                copy.wait_send()
+
+        return finish
+
+    def wide_cols(layer, start):
+        block = wide[layer, :, :, :, pl.ds(pl.multiple_of(start, 128), TILE)]
+        return block.reshape(D, TILE)
+
+    def gathered_sum(own, got):
+        total = own[group_at].astype(f32)
+        for step in (1, 2, 3):
+            total = total + got[ring_spot(group_at, step)].astype(f32)
+        return total
+
+    def allowed(count):
+        return jnp.concatenate([mask[...]] * count, axis=0) > 0.0
+
+    xs[0] = tokens[section_at]
+    bias_at, gain_at, gain_two_at = (0, QKV), (QKV, QKV + D), (QKV + D, QKV + 2 * D)
+
+    def forward(layer, carry):
+        x = xs[layer].astype(f32)
+        gain_one = vectors[layer, :, gain_at[0] : gain_at[1]]
+        gain_two = vectors[layer, :, gain_two_at[0] : gain_two_at[1]]
+        n1 = (x * rms_scale(x) * gain_one).astype(bf16)
+        n1s[layer] = n1
+        load(layer, 0).wait()
+        qkv = jnp.dot(n1, joint[layer, :, :QKV], preferred_element_type=f32)
+        qkv = qkv + vectors[layer, :, bias_at[0] : bias_at[1]]
+        turned = turn(
+            qkv[:, : D + KV_WIDTH], cosine[...], sine_up[...], sine_down[...], 1.0
+        ).astype(bf16)
+        qs[layer] = turned[:, :D]
+        kvs[layer, group_at] = jnp.concatenate(
+            [turned[:, D:], qkv[:, D + KV_WIDTH :].astype(bf16)], axis=1
+        )
+        exchange(
+            layer, 0, lambda peer: kvs.at[layer, group_at], lambda spot: kvs.at[layer, spot]
+        )()
+        kv = kvs[layer].reshape(ROW, 2 * KV_WIDTH)
+        keys, values = spread(kv[:, :KV_WIDTH]), spread(kv[:, KV_WIDTH:])
+        outs, row = [], 0
+        for kind, (pairs, _) in enumerate(KINDS):
+            count = SPAN * len(pairs)
+            scores = dot_nt(stack_pairs(turned, kind), keys[kind]) * SCALE
+            scores = jnp.where(allowed(len(pairs)), scores, -jnp.inf)
+            top = jnp.max(scores, axis=-1, keepdims=True)
+            raised = jnp.exp(scores - top)
+            prob = raised * (1.0 / jnp.sum(raised, axis=-1, keepdims=True))
+            probs[layer, row : row + count] = prob
+            outs.append(jnp.dot(prob.astype(bf16), values[kind], preferred_element_type=f32))
+            row += count
+        context = join_pairs(outs).astype(bf16)
+        ctx[layer] = context
+        hidden = x + jnp.dot(context, joint[layer, :, QKV:], preferred_element_type=f32)
+        hid[layer] = hidden
+        n2s[layer, group_at] = (hidden * rms_scale(hidden) * gain_two).astype(bf16)
+        done = exchange(
+            layer, 1, lambda peer: n2s.at[layer, group_at], lambda spot: n2s.at[layer, spot]
+        )
+        load(layer, 1).wait()
+        done()
+
+        def columns(tile, carry):
+            at = tile * TILE
+            n2 = n2s[layer].reshape(ROW, D)
+            gate = jnp.dot(n2, wide_cols(layer, at), preferred_element_type=f32)
+            up = jnp.dot(n2, wide_cols(layer, at + WIN), preferred_element_type=f32)
+            gus[layer, 0, :, pl.ds(pl.multiple_of(at, TILE), TILE)] = gate
+            gus[layer, 1, :, pl.ds(pl.multiple_of(at, TILE), TILE)] = up
+            act[layer, :, pl.ds(pl.multiple_of(at, TILE), TILE)] = (
+                gate * jax.nn.sigmoid(gate) * up
+            ).astype(bf16)
+            return carry
+
+        lax.fori_loop(0, WIN // TILE, columns, 0)
+        load(layer, 2).wait()
+        partial = jnp.dot(act[layer], down[layer], preferred_element_type=f32)
+        ysend[layer] = partial.astype(bf16).reshape(ZDEV, SPAN, D)
+        exchange(
+            layer, 2, lambda peer: ysend.at[layer, peer], lambda spot: yrecv.at[layer, spot]
+        )()
+        mlp = gathered_sum(ysend.at[layer], yrecv.at[layer])
+        xs[layer + 1] = (hidden + mlp).astype(bf16)
+        return carry
+
+    lax.fori_loop(0, 2, forward, 0)
+    dys[...] = cotangent[section_at].astype(f32)
+
+    def hand_over(layer):
+        return [
+            (xs.at[layer + 1], acts),
+            (igs.at[layer], grads_in),
+            (n2s.at[layer], out_n2),
+            (dgu.at[layer], out_dgu),
+            (act.at[layer], out_act),
+            (dmlp.at[layer], out_dmlp),
+            (lefts.at[layer], out_left),
+            (rights.at[layer], out_right),
+            (vecs.at[layer], out_vec),
+        ]
+
+    def staying(layer):
+        return [
+            pltpu.make_async_copy(source, target.at[section_at], stay_sems.at[at])
+            for at, (source, target) in enumerate(hand_over(layer))
+        ]
+
+    def leaving(layer, slot):
+        return [
+            pltpu.make_async_remote_copy(
+                src_ref=source,
+                dst_ref=target.at[slot],
+                send_sem=away_send.at[at],
+                recv_sem=away_recv.at[at],
+                device_id={"section": other},
+                device_id_type=MESH,
+            )
+            for at, (source, target) in enumerate(hand_over(layer))
+        ]
+
+    def backward(turn_at, carry):
+        layer = 1 - turn_at
+        gain_one = vectors[layer, :, gain_at[0] : gain_at[1]]
+        gain_two = vectors[layer, :, gain_two_at[0] : gain_two_at[1]]
+        dy = dys[...]
+        dmlp[layer, group_at] = dy.astype(bf16)
+        exchange(
+            layer, 3, lambda peer: dmlp.at[layer, group_at], lambda spot: dmlp.at[layer, spot]
+        )()
+        dn2[...] = jnp.zeros_like(dn2)
+
+        def columns(tile, carry):
+            at = pl.multiple_of(tile * TILE, TILE)
+            grad = dot_nt(dmlp[layer].reshape(ROW, D), down[layer, pl.ds(at, TILE), :])
+            gate = gus[layer, 0, :, pl.ds(at, TILE)]
+            up = gus[layer, 1, :, pl.ds(at, TILE)]
+            sigma = jax.nn.sigmoid(gate)
+            grad_gate = (grad * up * sigma * (1.0 + gate * (1.0 - sigma))).astype(bf16)
+            grad_up = (grad * gate * sigma).astype(bf16)
+            dgu[layer, :, pl.ds(at, TILE)] = grad_gate
+            dgu[layer, :, pl.ds(pl.multiple_of(at + WIN, TILE), TILE)] = grad_up
+            dn2[...] += dot_nt(grad_gate, wide_cols(layer, at)) + dot_nt(
+                grad_up, wide_cols(layer, at + WIN)
+            )
+            return carry
+
+        lax.fori_loop(0, WIN // TILE, columns, 0)
+        dsend[layer] = dn2[...].astype(bf16).reshape(ZDEV, SPAN, D)
+        exchange(
+            layer, 4, lambda peer: dsend.at[layer, peer], lambda spot: drecv.at[layer, spot]
+        )()
+        grad_two = gathered_sum(dsend.at[layer], drecv.at[layer])
+        hidden = hid[layer]
+        scale = rms_scale(hidden)
+        scaled = grad_two * gain_two
+        inner = jnp.mean(scaled * hidden, axis=-1, keepdims=True)
+        dhid = dy + scale * (scaled - hidden * (scale * scale * inner))
+        gain_two_term = jnp.sum(grad_two * hidden * scale, axis=0, keepdims=True)
+        dt = dhid.astype(bf16)
+        rights[layer, :, QKV:] = dt
+        do = dot_nt(dt, joint[layer, :, QKV:]).astype(bf16)
+        kv = kvs[layer].reshape(ROW, 2 * KV_WIDTH)
+        keys, values = spread(kv[:, :KV_WIDTH]), spread(kv[:, KV_WIDTH:])
+        queries = qs[layer]
+        dqs, dks, dvs, row = [], [], [], 0
+        for kind, (pairs, _) in enumerate(KINDS):
+            count = SPAN * len(pairs)
+            prob = probs[layer, row : row + count]
+            grad = stack_pairs(do, kind)
+            dprob = dot_nt(grad, values[kind])
+            inner = jnp.sum(prob * dprob, axis=-1, keepdims=True)
+            dscore = (prob * (dprob - inner)).astype(bf16)
+            dqs.append(jnp.dot(dscore, keys[kind], preferred_element_type=f32))
+            dks.append(dot_tn(dscore, stack_pairs(queries, kind)))
+            dvs.append(dot_tn(prob.astype(bf16), grad))
+            row += count
+        dkv = jnp.concatenate([unspread(dks) * SCALE, unspread(dvs)], axis=1)
+        dkvsend[layer] = dkv.astype(bf16).reshape(ZDEV, SPAN, 2 * KV_WIDTH)
+        exchange(
+            layer, 5, lambda peer: dkvsend.at[layer, peer], lambda spot: dkvrecv.at[layer, spot]
+        )()
+        dkv = gathered_sum(dkvsend.at[layer], dkvrecv.at[layer])
+        dqk = jnp.concatenate([join_pairs(dqs) * SCALE, dkv[:, :KV_WIDTH]], axis=1)
+        dqk = turn(dqk, cosine[...], sine_up[...], sine_down[...], -1.0)
+        dqkv = jnp.concatenate([dqk, dkv[:, KV_WIDTH:]], axis=1).astype(bf16)
+        rights[layer, :, :QKV] = dqkv
+        lefts[layer, :, :D] = n1s[layer]
+        lefts[layer, :, D:] = ctx[layer]
+        bias_term = jnp.sum(dqkv.astype(f32), axis=0, keepdims=True)
+        grad_one = dot_nt(dqkv, joint[layer, :, :QKV])
+        x = xs[layer].astype(f32)
+        scale = rms_scale(x)
+        scaled = grad_one * gain_one
+        inner = jnp.mean(scaled * x, axis=-1, keepdims=True)
+        dx = dhid + scale * (scaled - x * (scale * scale * inner))
+        gain_one_term = jnp.sum(grad_one * x * scale, axis=0, keepdims=True)
+        rounded = dx.astype(bf16).astype(f32)
+        dys[...] = rounded
+        igs[layer] = jnp.where(layer == 1, rounded, dx)
+        terms = jnp.concatenate(
+            [bias_term, gain_one_term, gain_two_term, jnp.zeros((1, 128), f32)], axis=1
+        )
+        for at in range(12):
+            vecs[layer, at : at + 1, :] = terms[:, 256 * at : 256 * (at + 1)]
+        vecs[layer, 12:16, :] = jnp.zeros((4, 256), f32)
+
+        @pl.when(layer == section_at)
+        def _():
+            for copy in staying(layer):
+                copy.start()
+
+        @pl.when(layer != section_at)
+        def _():
+            for copy in leaving(layer, section_at):
+                copy.start()
+
+        return carry
+
+    lax.fori_loop(0, 2, backward, 0)
+    for copy in staying(section_at):
+        copy.wait()
+    for copy in leaving(other, section_at):
+        copy.wait_send()
+    for copy in leaving(other, other):
+        copy.wait_recv()
+
+
+def run_layers(tokens, cotangent, mask, cosine, sine_up, sine_down, vectors, joint, wide, down):
+    vmem = pl.BlockSpec(memory_space=pltpu.VMEM)
+    anywhere = pl.BlockSpec(memory_space=pl.ANY)
+
+    def per_micro(shape, kind):
+        return jax.ShapeDtypeStruct((2,) + shape, kind)
+
+    def scratch(shape, kind=bf16, lead=2):
+        return pltpu.VMEM((lead,) + shape, kind)
+
+    return pl.pallas_call(
+        layers_kernel,
+        out_shape=(
+            per_micro((SPAN, D), bf16),
+            per_micro((SPAN, D), f32),
+            per_micro((ZDEV, SPAN, D), bf16),
+            per_micro((ROW, 2 * WIN), bf16),
+            per_micro((ROW, WIN), bf16),
+            per_micro((ZDEV, SPAN, D), bf16),
+            per_micro((SPAN, 2 * D), bf16),
+            per_micro((SPAN, QKV + D), bf16),
+            per_micro((16, 256), f32),
+        ),
+        in_specs=[vmem] * 7 + [anywhere] * 3,
+        out_specs=[vmem] * 9,
+        scratch_shapes=[
+            scratch((D, QKV + D)),
+            scratch((ZDEV, TILES_R, 16, 2 * WIN)),
+            scratch((WIN, D)),
+            scratch((SPAN, D), lead=3),
+            scratch((SPAN, D)),
+            scratch((SPAN, D)),
+            scratch((ZDEV, SPAN, 2 * KV_WIDTH)),
+            scratch((HEADS * SPAN, ROW), f32),
+            scratch((SPAN, D)),
+            scratch((SPAN, D), f32),
+            scratch((ZDEV, SPAN, D)),
+            scratch((2, ROW, WIN), f32),
+            scratch((ROW, WIN)),
+            scratch((ZDEV, SPAN, D)),
+            scratch((ZDEV, SPAN, D)),
+            pltpu.VMEM((SPAN, D), f32),
+            scratch((ZDEV, SPAN, D)),
+            scratch((ROW, 2 * WIN)),
+            pltpu.VMEM((ROW, D), f32),
+            scratch((ZDEV, SPAN, D)),
+            scratch((ZDEV, SPAN, D)),
+            scratch((ZDEV, SPAN, 2 * KV_WIDTH)),
+            scratch((ZDEV, SPAN, 2 * KV_WIDTH)),
+            scratch((SPAN, 2 * D)),
+            scratch((SPAN, QKV + D)),
+            scratch((16, 256), f32),
+            scratch((SPAN, D), f32),
+            pltpu.SemaphoreType.DMA((2, 6, 3)),
+            pltpu.SemaphoreType.DMA((2, 6, 3)),
+            pltpu.SemaphoreType.DMA((2, 3)),
+            pltpu.SemaphoreType.DMA((9,)),
+            pltpu.SemaphoreType.DMA((9,)),
+            pltpu.SemaphoreType.DMA((9,)),
+        ],
+        compiler_params=pltpu.CompilerParams(
+            collective_id=3, has_side_effects=True, vmem_limit_bytes=60 * 1024 * 1024
+        ),
+        name="layers",
+    )(tokens, cotangent, mask, cosine, sine_up, sine_down, vectors, joint, wide, down)
+
+
+def weights_kernel(
+    w_qkv, w_out, w_gate, w_up, w_down, vec,
+    joint, wide, down, vectors,
+    zeros, send_sems, recv_sems, local_sems,
+):
+    section_at = lax.axis_index("section")
+    group_at = lax.axis_index("group")
+    replica_at = lax.axis_index("replica")
+    x_at, y_at = replica_at // RING, lax.rem(replica_at, RING)
+    links = Links(send_sems, recv_sems)
+    sibling = {"section": 1 - section_at}
+
+    def along_x(spot):
+        return {"replica": spot * RING + y_at}
+
+    def along_y(spot):
+        return {"replica": x_at * RING + spot}
+
+    def along_z(spot):
+        return {"group": spot}
+
+    zeros[...] = jnp.zeros_like(zeros)
+    peers = [ring_spot(group_at, step) for step in (1, 2, 3)]
+    greet(
+        [
+            ring_spot(x_at, 1) * RING + y_at,
+            ring_spot(x_at, -1) * RING + y_at,
+            x_at * RING + ring_spot(y_at, 1),
+            x_at * RING + ring_spot(y_at, -1),
+        ],
+        peers,
+        [1 - section_at],
+    )
+    row_tile = pl.ds(pl.multiple_of(jnp.minimum(replica_at, TILES_R - 1) * 16, 16), 16)
+    slots = []
+    for which, source in enumerate((w_gate, w_up)):
+        target = wide.at[section_at, group_at, x_at, y_at, :, WIN * which : WIN * (which + 1)]
+        slots.append((source, target))
+
+    def window(source, spot):
+        start = pl.multiple_of((19 * spot) // 2 * 128, 128)
+        return source.at[row_tile, pl.ds(start, WIN)]
+
+    slot_sem = links.take(6)
+    for step, peer in enumerate(peers):
+        for which, (source, target) in enumerate(slots):
+            links.send(window(source, peer), target, slot_sem + 2 * step + which, along_z(peer))
+    vec_sem = links.take(4)
+    for step, peer in enumerate(peers):
+        links.send(vec, vectors.at[section_at, group_at], vec_sem + step, along_z(peer))
+    shift = lax.rem(group_at, 2) * 64
+    body = pl.ds(pl.multiple_of(shift, 64), BLOCK)
+    gap = pl.ds(pl.multiple_of(BLOCK - 19 * shift, 64), 64)
+    locals_ = []
+    for source, target in [
+        *[(window(source, group_at), target) for source, target in slots],
+        (w_qkv, joint.at[section_at, group_at, :, 0:QKV]),
+        (w_out, joint.at[section_at, group_at, :, QKV : QKV + D]),
+        (w_down, down.at[section_at, body]),
+        (zeros, down.at[0, gap]),
+        (zeros, down.at[1, gap]),
+        (vec, vectors.at[section_at, group_at]),
+    ]:
+        copy = pltpu.make_async_copy(source, target, local_sems.at[len(locals_)])
+        copy.start()
+        locals_.append(copy)
+    for at in (2, 3):
+        locals_[at].wait()
+
+    def joint_block(spot, half):
+        return joint.at[section_at, spot, pl.ds(112 * half, 112)]
+
+    joint_share = RingShare(links, group_at, along_z, joint_block, sibling)
+    joint_share.start()
+    down_sem = links.take(1)
+    down_view = down.at[section_at, body]
+    links.send(w_down, down_view, down_sem, sibling)
+    locals_[0].wait()
+    locals_[1].wait()
+
+    def arrived_slots(which):
+        for step, peer in enumerate(peers):
+            spot = ring_spot(group_at, -1 - step)
+            cols = pl.ds(WIN * which, WIN)
+            target = wide.at[section_at, spot, x_at, y_at, :, cols]
+            links.arrived(target, slot_sem + 2 * step + which, along_z(peer))
+
+    def sharers(which, x_first):
+        start = WIN * which
+
+        def small(spot, half):
+            cols = pl.ds(start + WIN // 2 * half, WIN // 2)
+            if x_first:
+                return wide.at[section_at, :, spot, y_at, :, cols]
+            return wide.at[section_at, :, x_at, spot, :, cols]
+
+        def big(spot, half):
+            span, cols = pl.ds(2 * half, 2), pl.ds(start, WIN)
+            if x_first:
+                return wide.at[section_at, :, span, spot, :, cols]
+            return wide.at[section_at, :, spot, span, :, cols]
+
+        one = (x_at, along_x) if x_first else (y_at, along_y)
+        two = (y_at, along_y) if x_first else (x_at, along_x)
+        return RingShare(links, *one, small), RingShare(links, *two, big, sibling)
+
+    gate_one, gate_two = sharers(0, False)
+    up_one, up_two = sharers(1, True)
+    arrived_slots(0)
+    gate_one.start()
+    arrived_slots(1)
+    up_one.start()
+    gate_one.middle()
+    up_one.middle()
+    gate_one.end()
+    gate_two.start()
+    up_one.end()
+    up_two.start()
+    joint_share.middle()
+    for step, peer in enumerate(peers):
+        spot = ring_spot(group_at, -1 - step)
+        links.arrived(vectors.at[section_at, spot], vec_sem + step, along_z(peer))
+    locals_[7].wait()
+    links.send(vectors.at[section_at], vectors.at[section_at], vec_sem + 3, sibling)
+    gate_two.middle()
+    up_two.middle()
+    joint_share.end()
+    gate_two.end()
+    up_two.end()
+    other = 1 - section_at
+    for at in (4, 5, 6):
+        locals_[at].wait()
+    links.arrived(down.at[other, body], down_sem, sibling)
+    links.arrived(vectors.at[other], vec_sem + 3, sibling)
+    joint_share.end_twin(lambda spot, half: joint.at[other, spot, pl.ds(112 * half, 112)])
+    for which, share in ((0, gate_two), (1, up_two)):
+        cols = pl.ds(WIN * which, WIN)
+        if which:
+            share.end_twin(lambda s, h: wide.at[other, :, pl.ds(2 * h, 2), s, :, cols])
+        else:
+            share.end_twin(lambda s, h: wide.at[other, :, s, pl.ds(2 * h, 2), :, cols])
+    links.finish()
+
+
+def share_weights(w_qkv, w_out, w_gate, w_up, w_down, vec):
+    anywhere = pl.BlockSpec(memory_space=pl.ANY)
+    sems = 6 + 4 + 1 + 3 * 14 + 2 * 6
+    return pl.pallas_call(
+        weights_kernel,
+        out_shape=(
+            jax.ShapeDtypeStruct((2, ZDEV, OWN, QKV + D), bf16),
+            jax.ShapeDtypeStruct((2, ZDEV, RING, RING, 16, 2 * WIN), bf16),
+            jax.ShapeDtypeStruct((2, WIN, D), bf16),
+            jax.ShapeDtypeStruct((2, ZDEV, 8, 128), f32),
+        ),
+        in_specs=[anywhere] * 6,
+        out_specs=[pl.BlockSpec(memory_space=pltpu.VMEM)] * 4,
+        scratch_shapes=[
+            pltpu.VMEM((64, D), bf16),
+            pltpu.SemaphoreType.DMA((sems,)),
+            pltpu.SemaphoreType.DMA((sems,)),
+            pltpu.SemaphoreType.DMA((8,)),
+        ],
+        compiler_params=pltpu.CompilerParams(
+            collective_id=2, has_side_effects=True, vmem_limit_bytes=58 * 1024 * 1024
+        ),
+        name="weights",
+    )(w_qkv, w_out, w_gate, w_up, w_down, vec)
 
 
 def on_device(
@@ -687,55 +1115,26 @@
 ):
     section_at = lax.axis_index("section")
     group_at = lax.axis_index("group")
-    first = section_at == 0
-    own_set = gather_weights(
-        w_qkv[0], b_qkv[0], w_out[0], w_gate[0], w_up[0], w_down[0], norm_attn[0], norm_ffn[0]
-    )
-    other_set = tuple(map(swap, own_set))
-
-    def unpack(members):
-        w_qo, w_gu, padded_down, vectors = members
-        vectors = vectors[0].astype(f32)
-        return (
-            w_qo,
-            w_gu,
-            padded_down,
-            vectors[:QKV],
-            vectors[QKV : QKV + D],
-            vectors[QKV + D :],
-        )
-
-    layer_sets = [
-        unpack([jnp.where(first, a, b) for a, b in zip(own_set, other_set)]),
-        unpack([jnp.where(first, b, a) for a, b in zip(own_set, other_set)]),
-    ]
-    own_tokens = lax.dynamic_index_in_dim(tokens, section_at, 0, keepdims=False)[0]
-    own_cotangent = lax.dynamic_index_in_dim(cotangent, section_at, 0, keepdims=False)[0]
+    vec = jnp.concatenate([b_qkv[0], norm_attn[0], norm_ffn[0]]).astype(f32)
+    vec = jnp.pad(vec, (0, 1024 - vec.shape[0])).reshape(8, 128)
+    joint, wide, down, vectors = share_weights(
+        w_qkv[0], w_out[0], w_gate[0], w_up[0], w_down[0], vec
+    )
+    vectors = vectors.reshape(2, ZDEV, 1024)
+    parts = (vectors[..., : QKV // 4], vectors[..., QKV // 4 : QKV // 4 + OWN])
+    parts = parts + (vectors[..., QKV // 4 + OWN : QKV // 4 + 2 * OWN],)
+    vectors = jnp.concatenate([part.reshape(2, 1, -1) for part in parts], axis=2)
     lengths = lax.dynamic_index_in_dim(doc_lengths, section_at, 0, keepdims=False)[0]
-    tables = doc_tables(lengths, group_at)
-    out_first, kept_first = layer_forward(own_tokens, layer_sets[0], tables)
-    out_second, kept_second = layer_forward(out_first, layer_sets[1], tables)
-    grad_second, pieces_second = layer_backward(
-        own_cotangent.astype(f32), kept_second, layer_sets[1], tables
-    )
-    grad_second = grad_second.astype(bf16)
-    grad_first, pieces_first = layer_backward(
-        grad_second.astype(f32), kept_first, layer_sets[0], tables
-    )
-    sent = [jnp.where(first, b, a) for a, b in zip(pieces_first, pieces_second)]
-    kept = [jnp.where(first, a, b) for a, b in zip(pieces_first, pieces_second)]
-    got = [swap(member) for member in sent]
-    token_pieces = jnp.concatenate([kept[0], got[0]], axis=0)
-    row_pieces = jnp.concatenate([kept[1], got[1]], axis=0)
-    grads = weight_grads(token_pieces, row_pieces, kept[2] + got[2])
-
-    def placed(lead, second):
-        mine = jnp.where(first, lead, second)
-        theirs = swap(jnp.where(first, second, lead))
-        return jnp.stack([jnp.where(first, mine, theirs), jnp.where(first, theirs, mine)])
-
-    acts = placed(out_first, out_second)
-    input_grads = placed(grad_first, grad_second.astype(f32))
+    acts, input_grads, *pieces = run_layers(
+        tokens[:, 0],
+        cotangent[:, 0],
+        *doc_tables(lengths, group_at),
+        vectors,
+        joint.reshape(2, D, QKV + D),
+        wide.reshape(2, ZDEV, REPL, 16, 2 * WIN),
+        down,
+    )
+    grads = weight_grads(*pieces)
     return (acts[None, :, None], input_grads[None, :, None]) + tuple(g[None] for g in grads)
 
 

time: 622 us -> 295 us (0.47); the launches traced: 611 us -> 295 us
  waiting for transfers between devices: 175 us -> 0 us
  Pallas kernels: 109 us -> 265 us
  blocking collectives: 90.9 us -> 0 us
  local copies, waits for them, and re-layouts: 89.1 us -> 13.2 us
  other arithmetic: 75 us -> 15.9 us
  matrix products: 53.8 us -> 0 us
  between operations: 15.9 us -> 0.78 us
    pallas_call x0 -> x2, Pallas kernels: none -> 160 us  [the longest x1 104 us: run_layers(): pl.pallas_call(layers_kernel, out_shape=(per_micro((SPAN, D), bf16), per_...]
    all_gather x2 -> x0, waiting for transfers between devices: 97.5 us -> none  [the longest x1 54.1 us: gather_weights(): joint = lax.all_gather(joint, ('group', 'replica'), axis=0, tiled=False)]
    all_gather x6 -> x0, blocking collectives: 78.1 us -> none  [the longest x2 27.2 us: layer_backward(): grad_mlp_all = lax.all_gather(grad_mlp, 'group', axis=0, tiled=True)]
    reduce_scatter x6 -> x0, waiting for transfers between devices: 73.2 us -> none  [the longest x2 31.9 us: layer_backward(): lax.psum_scatter(grad_kv_all.astype(bf16), 'group', scatter_dimension=0,...]
    dot_general x28 -> x0, matrix products: 53.8 us -> none  [the longest x8 25.3 us: dot_t(): return jnp.einsum('id,ed->ie', left, right, preferred_element_type=f32)]
    reshape x24 -> x4, local copies, waits for them, and re-layouts: 23.5 us -> 1.05 us  [the longest x1 0.77 us: on_device(): vectors = vectors.reshape(2, ZDEV, 1024)]
    select_n x6 -> x0, other arithmetic: 13.8 us -> none  [the longest x2 5.78 us: on_device(): kept = [jnp.where(first, a, b) for a, b in zip(pieces_first, pieces_second)]]
    unnamed x17 -> x4, other arithmetic: 16.5 us -> 2.82 us
  transfers between devices with their start and end apart: 17 -> 0, of which waited for: 11 -> 0; matrix products, arithmetic and copies ran while one was open for 20% -> 0% of each run, Pallas kernels for 0% -> 0%
where the time goes in v3:
time: 295 us
  Pallas kernels  265 us (90%)
  other arithmetic  15.9 us (5%)
  local copies, waits for them, and re-layouts  13.2 us (4%)
    pallas_call x1, Pallas kernels, share_grads(): pl.pallas_call(grads_kernel, out_shape=jax.ShapeDtypeStruct((RING, RING,...  105 us
    pallas_call x1, Pallas kernels, run_layers(): pl.pallas_call(layers_kernel, out_shape=(per_micro((SPAN, D), bf16), per_...  104 us
    pallas_call x1, Pallas kernels, share_weights(): pl.pallas_call(weights_kernel, out_shape=(jax.ShapeDtypeStruct((2, ZDEV,...  55.5 us
    convert_element_type x4, other arithmetic, rows_of(): return block.reshape(OWN, width).astype(f32)  6.66 us

profile of v3, /device:TPU:0, one launch (start us, length us, event | category | flops | bytes accessed | tf_op | source)
XLA Modules:
  0.0 294.7 jit_solution(10803728294053632537)
XLA Ops:
  0.6 0.7 fusion.10
  1.3 0.2 reduce-window.7
  1.5 0.7 bitcast_subtract_fusion
  2.4 0.2 multiply_sine_fusion
  2.6 0.8 pad_maximum_fusion.2
  3.5 0.7 fusion.1.mask
  4.2 0.7 reduce
  4.9 0.7 reduce.1
  5.6 0.7 reduce.2
  6.3 0.7 fusion.9.vec
  7.0 55.5 %weights.1 = (bf16[2,4,224,2048]{3,2,1,0:T(8,128)(2,1)}, bf16[2,4,4,4,16,2560]{5,4,3,2,1,0:T(8,128)(2,1)}, bf16[2,1280,896]{2,1,0:T(8,128)(2,1)}, f32[2,4,8,128]{3,2,1,0:T(8,128)}) custom-call(bf16[224,1152]{1,0:T(8,128)(2,1)} %bitcast.81, bf16[224,896]{1,0:T(8,128)(2,1)} %bitcast.83, bf16[224,4864]{1,0:T(8,128)(2,1)} %bitcast.73, ...), custom_call_target="tpu_custom_call" | custom-call | tf_op jit(solution)/shard_map/weights/pallas_call | solution.py:1090
  62.5 0.8 reshape.196
  63.7 0.6 pad_maximum_fusion.3.vectors
  64.3 104.3 %layers.1 = (bf16[2,64,896]{2,1,0:T(8,128)(2,1)}, f32[2,64,896]{2,1,0:T(8,128)}, bf16[2,4,64,896]{3,2,1,0:T(8,128)(2,1)}, bf16[2,256,2560]{2,1,0:T(8,128)(2,1)},...) custom-call(bf16[2,64,896]{2,1,0:T(8,128)(2,1)} %bitcast.84, ...), custom_call_target="tpu_custom_call" | custom-call | tf_op jit(solution)/shard_map/layers/pallas_call | solution.py:886
  168.6 105.1 %grads.1 = bf16[4,4,16,15232]{3,2,1,0:T(8,128)(2,1)} custom-call(bf16[512,896]{1,0:T(8,128)(2,1)} %bitcast.79, bf16[512,2560]{1,0:T(8,128)(2,1)} %bitcast.72, bf16[512,1280]{1,0:T(8,128)(2,1)} %bitcast.78, bf16[512,896]{1,0:T(8,128)(2,1)} %bitcast.80, bf16[2,64,1792]{2,1,0:T(8,128)(2,1)} %get-tuple-element.33.left_tokens, ...), custom_call_target="tpu_custom_call" | custom-call | tf_op jit(solution)/shard_map/grads/pallas_call | solution.py:465
  273.6 1.4 slice.48
  275.0 0.4 reshape.207
  275.6 1.3 slice.49
  276.8 0.5 reshape.208
  277.5 2.3 maximum_convert_fusion
  279.9 2.6 fusion.11
  282.4 2.3 bitcast_convert_fusion
  284.8 2.3 bitcast_convert_fusion.1
  287.1 1.1 slice.43
  288.2 1.0 bitcast_convert_fusion.2
  289.3 1.0 slice.45
  290.3 0.9 bitcast_convert_fusion.3
  291.2 0.7 convert_bitcast_fusion
  292.0 0.6 fusion.13
  292.7 0.6 broadcast_in_dim.29
  293.3 0.7 copy.38
  294.0 0.8 copy.39
  (20 shorter events, 1.0 us)
Async XLA Ops:
  287.1 6.2 %copy-start.1 = (bf16[2,64,896]{2,1,0:T(8,128)(2,1)S(1)}, bf16[2,64,896]{2,1,0:T(8,128)(2,1)}, u32[]{:S(2)}) copy-start(bf16[2,64,896]{2,1,0:T(8,128)(2,1)} %get-tuple-element.27) | copy-start | bytes 688132
  288.2 5.7 %copy-start = (f32[2,64,896]{2,1,0:T(8,128)S(1)}, f32[2,64,896]{2,1,0:T(8,128)}, u32[]{:S(2)}) copy-start(f32[2,64,896]{2,1,0:T(8,128)} %get-tuple-element.28) | copy-start | bytes 1376260

commit v4 on v3

--- a/solution.py
+++ b/solution.py
@@ -80,7 +80,7 @@
 
 class Links:
     def __init__(self, send_sems, recv_sems):
-        self.send_sems, self.recv_sems, self.used, self.started = send_sems, recv_sems, 0, []
+        self.send_sems, self.recv_sems, self.used, self.started = send_sems, recv_sems, 0, {}
 
     def take(self, count):
         first = self.used
@@ -100,103 +100,106 @@
     def send(self, source, target, sem_at, device):
         copy = self.copy(source, target, sem_at, device)
         copy.start()
-        self.started.append(copy)
+        self.started[sem_at] = lambda: copy
+
+    def send_block(self, block, spot, half, sem_at, device):
+        def again():
+            return self.copy(block(spot, half), block(spot, half), sem_at, device)
+
+        again().start()
+        self.started[sem_at] = again
 
     def arrived(self, target, sem_at, device):
         self.copy(target, target, sem_at, device).wait_recv()
 
     def finish(self):
-        for copy in self.started:
-            copy.wait_send()
-        self.started = []
+        for copy in self.started.values():
+            copy().wait_send()
+        self.started = {}
 
 
 class RingSum:
     def __init__(self, links, spot, device_at, block, first, second, left, right, add):
-        self.links, self.spot, self.block, self.add = links, spot, block, add
+        self.links, self.block, self.add = links, block, add
+        self.spots = [ring_spot(spot, steps) for steps in (0, 1, 2, -1)]
         self.right, self.left = device_at(ring_spot(spot, 1)), device_at(ring_spot(spot, -1))
         self.first, self.second, self.from_left, self.from_right = first, second, left, right
         self.sem = links.take(6)
 
     def start(self):
-        send, sem, spot = self.links.send, self.sem, self.spot
-        far = ring_spot(spot, 2)
-        send(self.block(far, 0), self.first, sem, self.right)
-        send(self.block(far, 1), self.second, sem + 1, self.left)
-        send(self.block(ring_spot(spot, 1), 1), self.from_left(1), sem + 2, self.right)
-        send(self.block(ring_spot(spot, -1), 0), self.from_right(0), sem + 3, self.left)
+        send, sem, spots = self.links.send, self.sem, self.spots
+        send(self.block(spots[2], 0), self.first, sem, self.right)
+        send(self.block(spots[2], 1), self.second, sem + 1, self.left)
+        send(self.block(spots[1], 1), self.from_left(1), sem + 2, self.right)
+        send(self.block(spots[-1], 0), self.from_right(0), sem + 3, self.left)
 
     def middle(self):
-        links, sem, spot = self.links, self.sem, self.spot
+        links, sem, spots = self.links, self.sem, self.spots
         links.arrived(self.first, sem, self.right)
-        onward = self.block(ring_spot(spot, 1), 0)
+        onward = self.block(spots[1], 0)
         self.add(onward, onward, self.first)
         links.send(onward, self.from_left(0), sem + 4, self.right)
         links.arrived(self.second, sem + 1, self.left)
-        onward = self.block(ring_spot(spot, -1), 1)
+        onward = self.block(spots[-1], 1)
         self.add(onward, onward, self.second)
         links.send(onward, self.from_right(1), sem + 5, self.left)
 
     def end(self, result):
-        links, sem, spot = self.links, self.sem, self.spot
+        links, sem, spots = self.links, self.sem, self.spots
         links.arrived(self.from_left(1), sem + 2, self.right)
         links.arrived(self.from_right(0), sem + 3, self.left)
         links.arrived(self.from_left(0), sem + 4, self.right)
         links.arrived(self.from_right(1), sem + 5, self.left)
         for half in (0, 1):
             self.add(
-                result(half), self.block(spot, half), self.from_left(half), self.from_right(half)
+                result(half), self.block(spots[0], half), self.from_left(half), self.from_right(half)
             )
 
 
 class RingShare:
     def __init__(self, links, spot, device_at, block, sibling=None):
-        self.links, self.spot, self.block, self.sibling = links, spot, block, sibling
-        self.right, self.left = device_at(ring_spot(spot, 1)), device_at(ring_spot(spot, -1))
+        self.links, self.block, self.sibling = links, block, sibling
+        self.spots = [ring_spot(spot, steps) for steps in (0, 1, 2, -1)]
+        self.right, self.left = device_at(self.spots[1]), device_at(self.spots[-1])
         self.sem = links.take(6)
         self.twin = links.take(8) if sibling else 0
 
+    def send(self, steps, half, at, device):
+        self.links.send_block(self.block, self.spots[steps], half, self.sem + at, device)
+
     def pass_on(self, steps, half):
         if self.sibling:
-            view = self.block(ring_spot(self.spot, steps), half)
-            self.links.send(view, view, self.twin + 2 * (steps % RING) + half, self.sibling)
+            sem = self.twin + 2 * (steps % RING) + half
+            self.links.send_block(self.block, self.spots[steps], half, sem, self.sibling)
+
+    def arrived(self, steps, half, at, device, onward=None):
+        self.links.arrived(self.block(self.spots[steps], half), self.sem + at, device)
+        if onward:
+            self.send(steps, half, *onward)
+        self.pass_on(steps, half)
 
     def start(self):
-        send, sem = self.links.send, self.sem
-        low, high = self.block(self.spot, 0), self.block(self.spot, 1)
-        send(low, low, sem, self.right)
-        send(high, high, sem + 2, self.left)
-        send(high, high, sem + 1, self.right)
-        send(low, low, sem + 3, self.left)
+        self.send(0, 0, 0, self.right)
+        self.send(0, 1, 2, self.left)
+        self.send(0, 1, 1, self.right)
+        self.send(0, 0, 3, self.left)
         self.pass_on(0, 0)
         self.pass_on(0, 1)
 
     def middle(self):
-        links, sem, spot = self.links, self.sem, self.spot
-        low = self.block(ring_spot(spot, -1), 0)
-        links.arrived(low, sem, self.right)
-        links.send(low, low, sem + 4, self.right)
-        self.pass_on(-1, 0)
-        high = self.block(ring_spot(spot, 1), 1)
-        links.arrived(high, sem + 2, self.left)
-        links.send(high, high, sem + 5, self.left)
-        self.pass_on(1, 1)
+        self.arrived(-1, 0, 0, self.right, (4, self.right))
+        self.arrived(1, 1, 2, self.left, (5, self.left))
 
     def end(self):
-        links, sem, spot = self.links, self.sem, self.spot
-        for steps, half, at, device in (
-            (-1, 1, 1, self.right),
-            (1, 0, 3, self.left),
-            (2, 0, 4, self.right),
-            (2, 1, 5, self.left),
-        ):
-            links.arrived(self.block(ring_spot(spot, steps), half), sem + at, device)
-            self.pass_on(steps, half)
+        self.arrived(-1, 1, 1, self.right)
+        self.arrived(1, 0, 3, self.left)
+        self.arrived(2, 0, 4, self.right)
+        self.arrived(2, 1, 5, self.left)
 
     def end_twin(self, twin_block):
         for steps in range(RING):
             for half in (0, 1):
-                view = twin_block(ring_spot(self.spot, steps), half)
+                view = twin_block(self.spots[steps], half)
                 self.links.arrived(view, self.twin + 2 * steps + half, self.sibling)
 
 
@@ -492,6 +495,43 @@
     )(n2, dgu, act, dmlp, lefts, rights, vecs)
 
 
+def widen_kernel(block, rest, gate, up, qkv, out, down):
+    at = pl.program_id(0)
+    for target, start, width in (
+        (gate, 0, FF), (up, FF, FF), (qkv, QO_AT, QKV), (out, QO_AT + QKV, D),
+    ):
+        target[...] = block[0, :, start : start + width].astype(f32)
+    for inner in range(3):
+        rows = pl.ds(pl.multiple_of((3 * at + inner) * 16, 16), 16)
+        start = DOWN_AT + D * inner
+        down[rows, :] = block[0, :, start : start + D].astype(f32)
+    for tile in range(34):
+
+        @pl.when(at == tile // 3)
+        def _():
+            rows = pl.ds((3 * TILES_R + tile) * 16, 16)
+            start = D * (tile % 17)
+            down[rows, :] = rest[tile // 17, :, start : start + D].astype(f32)
+
+
+def widen(shared):
+    rows = [FF, FF, QKV, D]
+    return pl.pallas_call(
+        widen_kernel,
+        grid=(TILES_R,),
+        out_shape=[jax.ShapeDtypeStruct((OWN, width), f32) for width in rows]
+        + [jax.ShapeDtypeStruct((BLOCK, D), f32)],
+        in_specs=[
+            pl.BlockSpec((1, 16, COLS), lambda at: (at, 0, 0)),
+            pl.BlockSpec((2, 16, COLS), lambda at: (TILES_R // 2, 0, 0)),
+        ],
+        out_specs=[pl.BlockSpec((16, width), lambda at: (at, 0)) for width in rows]
+        + [pl.BlockSpec((BLOCK, D), lambda at: (0, 0))],
+        compiler_params=pltpu.CompilerParams(vmem_limit_bytes=40 * 1024 * 1024),
+        name="widen",
+    )(shared, shared)
+
+
 def weight_grads(n2, dgu, act, dmlp, lefts, rights, vecs):
     group_at = lax.axis_index("group")
     shared = share_grads(
@@ -504,30 +544,18 @@
         vecs,
     )
     shared = shared.reshape(REPL, 16, COLS)
-
-    def rows_of(start, width):
-        block = shared[:TILES_R, :, start : start + width]
-        return block.reshape(OWN, width).astype(f32)
-
-    lead = shared[:TILES_R, :, DOWN_AT : DOWN_AT + 3 * D].reshape(TILES_R, 16, 3, D)
-    rest = shared[TILES_R:].reshape(2, 16, 17, D)
-    grad_down = jnp.concatenate(
-        [
-            jnp.transpose(lead, (0, 2, 1, 3)).reshape(-1, D),
-            jnp.transpose(rest, (0, 2, 1, 3)).reshape(-1, D),
-        ]
-    ).astype(f32)
+    grad_gate, grad_up, grad_qkv, grad_out, grad_down = widen(shared)
     vec = shared[0, :, VEC_AT:].reshape(16 * 256).astype(f32)
 
     def own_part(start, width):
         return lax.dynamic_slice_in_dim(vec, start + group_at * width, width, 0)
 
     return (
-        rows_of(QO_AT, QKV),
+        grad_qkv,
         own_part(0, QKV // ZDEV),
-        rows_of(QO_AT + QKV, D),
-        rows_of(0, FF),
-        rows_of(FF, FF),
+        grad_out,
+        grad_gate,
+        grad_up,
         grad_down,
         own_part(QKV, OWN),
         own_part(QKV + D, OWN),
@@ -595,29 +623,200 @@
 
 
 def layers_kernel(
-    tokens, cotangent, mask, cosine, sine_up, sine_down, vectors, joint_hbm, wide_hbm, down_hbm,
+    tokens, cotangent, mask, cosine, sine_up, sine_down, vec,
+    w_qkv, w_out, w_gate, w_up, w_down,
     acts, grads_in, out_n2, out_dgu, out_act, out_dmlp, out_left, out_right, out_vec,
-    joint, wide, down, xs, n1s, qs, kvs, probs, ctx, hid, n2s, gus, act, ysend, yrecv,
+    joint, wide, down, vectors, zeros,
+    xs, n1s, qs, kvs, probs, ctx, hid, n2s, gus, act, ysend, yrecv,
     dys, dmlp, dgu, dn2, dsend, drecv, dkvsend, dkvrecv, lefts, rights, vecs, igs,
-    send_sems, recv_sems, load_sems, away_send, away_recv, stay_sems,
+    send_sems, recv_sems, away_send, away_recv, stay_sems, ring_send, ring_recv, local_sems,
 ):
     section_at = lax.axis_index("section")
     group_at = lax.axis_index("group")
+    replica_at = lax.axis_index("replica")
+    x_at, y_at = replica_at // RING, lax.rem(replica_at, RING)
     other = 1 - section_at
+    sibling = {"section": other}
+    links = Links(ring_send, ring_recv)
+
+    def along_x(spot):
+        return {"replica": spot * RING + y_at}
+
+    def along_y(spot):
+        return {"replica": x_at * RING + spot}
+
+    def along_z(spot):
+        return {"group": spot}
+
+    zeros[...] = jnp.zeros_like(zeros)
     peers = [ring_spot(group_at, step) for step in (1, 2, 3)]
-    greet([], peers, [other])
-
-    def load(layer, which):
-        source, target = [
-            (joint_hbm.at[layer], joint.at[layer]),
-            (wide_hbm.at[layer, :, pl.ds(0, TILES_R)], wide.at[layer]),
-            (down_hbm.at[layer], down.at[layer]),
-        ][which]
-        return pltpu.make_async_copy(source, target, load_sems.at[layer, which])
-
-    for layer in (0, 1):
-        for which in range(3):
-            load(layer, which).start()
+    sources = [ring_spot(group_at, -step) for step in (1, 2, 3)]
+    greet(
+        [
+            ring_spot(x_at, 1) * RING + y_at,
+            ring_spot(x_at, -1) * RING + y_at,
+            x_at * RING + ring_spot(y_at, 1),
+            x_at * RING + ring_spot(y_at, -1),
+        ],
+        peers,
+        [other],
+    )
+    row_tile = pl.ds(pl.multiple_of(jnp.minimum(replica_at, TILES_R - 1) * 16, 16), 16)
+    slots = []
+    for which, source in enumerate((w_gate, w_up)):
+        target = wide.at[section_at, group_at, x_at, y_at, :, WIN * which : WIN * (which + 1)]
+        slots.append((source, target))
+
+    def window(source, spot):
+        start = pl.multiple_of((19 * spot) // 2 * 128, 128)
+        return source.at[row_tile, pl.ds(start, WIN)]
+
+    slot_sem = links.take(6)
+    for step, peer in enumerate(peers):
+        for which, (source, target) in enumerate(slots):
+            links.send(window(source, peer), target, slot_sem + 2 * step + which, along_z(peer))
+    vec_sem = links.take(4)
+    for step, peer in enumerate(peers):
+        links.send(vec, vectors.at[section_at, group_at], vec_sem + step, along_z(peer))
+    shift = lax.rem(group_at, 2) * 64
+    body = pl.ds(pl.multiple_of(shift, 64), BLOCK)
+    gap = pl.ds(pl.multiple_of(BLOCK - 19 * shift, 64), 64)
+    locals_ = []
+    for source, target in [
+        *[(window(source, group_at), target) for source, target in slots],
+        (w_qkv, joint.at[section_at, group_at, :, 0:QKV]),
+        (w_out, joint.at[section_at, group_at, :, QKV : QKV + D]),
+        (w_down, down.at[section_at, body]),
+        (zeros, down.at[0, gap]),
+        (zeros, down.at[1, gap]),
+        (vec, vectors.at[section_at, group_at]),
+    ]:
+        copy = pltpu.make_async_copy(source, target, local_sems.at[len(locals_)])
+        copy.start()
+        locals_.append(copy)
+    down_sem = links.take(1)
+    links.send(w_down, down.at[section_at, body], down_sem, sibling)
+
+    def joint_block(spot, half):
+        return joint.at[section_at, spot, pl.ds(112 * half, 112)]
+
+    def joint_twin(spot, half):
+        return joint.at[other, spot, pl.ds(112 * half, 112)]
+
+    joint_share = RingShare(links, group_at, along_z, joint_block, sibling)
+
+    def sharers(which, x_first):
+        start = WIN * which
+
+        def small(spot, half):
+            cols = pl.ds(start + WIN // 2 * half, WIN // 2)
+            if x_first:
+                return wide.at[section_at, :, spot, y_at, :, cols]
+            return wide.at[section_at, :, x_at, spot, :, cols]
+
+        def big(spot, half, layer=section_at):
+            span, cols = pl.ds(2 * half, 2), pl.ds(start, WIN)
+            if x_first:
+                return wide.at[layer, :, span, spot, :, cols]
+            return wide.at[layer, :, spot, span, :, cols]
+
+        one = (x_at, along_x) if x_first else (y_at, along_y)
+        two = (y_at, along_y) if x_first else (x_at, along_x)
+        stage_two = RingShare(links, *two, big, sibling)
+        return RingShare(links, *one, small), stage_two, lambda spot, half: big(spot, half, other)
+
+    gate_one, gate_two, gate_twin = sharers(0, False)
+    up_one, up_two, up_twin = sharers(1, True)
+
+    @pl.when(section_at == 0)
+    def _():
+        locals_[2].wait()
+        locals_[3].wait()
+        joint_share.start()
+
+    for which, share in ((0, gate_one), (1, up_one)):
+        locals_[which].wait()
+        for step, spot in enumerate(sources):
+            cols = pl.ds(WIN * which, WIN)
+            target = wide.at[section_at, spot, x_at, y_at, :, cols]
+            links.arrived(target, slot_sem + 2 * step + which, along_z(peers[step]))
+        share.start()
+    gate_one.middle()
+    up_one.middle()
+    gate_one.end()
+    up_one.end()
+
+    @pl.when(section_at == 0)
+    def _():
+        gate_two.start()
+        up_two.start()
+
+    locals_[7].wait()
+    for step, spot in enumerate(sources):
+        links.arrived(vectors.at[section_at, spot], vec_sem + step, along_z(peers[step]))
+    links.send(vectors.at[section_at], vectors.at[section_at], vec_sem + 3, sibling)
+
+    @pl.when(section_at == 0)
+    def _():
+        joint_share.middle()
+        gate_two.middle()
+        up_two.middle()
+        joint_share.end()
+
+    @pl.when(section_at == 1)
+    def _():
+        locals_[2].wait()
+        locals_[3].wait()
+        joint_share.end_twin(joint_twin)
+        joint_share.start()
+
+    links.arrived(vectors.at[other], vec_sem + 3, sibling)
+    for at in (4, 5, 6):
+        locals_[at].wait()
+
+    def while_keys_travel():
+        @pl.when(section_at == 0)
+        def _():
+            gate_two.end()
+            up_two.end()
+
+        @pl.when(section_at == 1)
+        def _():
+            gate_two.start()
+            up_two.start()
+            joint_share.middle()
+
+    def while_rows_travel():
+        @pl.when(section_at == 1)
+        def _():
+            gate_two.middle()
+            up_two.middle()
+            gate_two.end_twin(gate_twin)
+            up_two.end_twin(up_twin)
+
+        links.arrived(down.at[other, body], down_sem, sibling)
+
+    def while_sums_travel():
+        @pl.when(section_at == 1)
+        def _():
+            joint_share.end()
+            gate_two.end()
+            up_two.end()
+
+    def late_weights(at):
+        @pl.when(section_at == 0)
+        def _():
+            if at == 0:
+                joint_share.end_twin(joint_twin)
+            else:
+                gate_two.end_twin(gate_twin)
+                up_two.end_twin(up_twin)
+
+    def vector_row(layer):
+        total = vectors[layer, 0]
+        for z in range(1, ZDEV):
+            total = total + vectors[layer, z]
+        return jnp.concatenate([total[at : at + 1] for at in range(8)], axis=1)
 
     def exchange(layer, which, source, target):
         copies = []
@@ -650,8 +849,11 @@
         return finish
 
     def wide_cols(layer, start):
-        block = wide[layer, :, :, :, pl.ds(pl.multiple_of(start, 128), TILE)]
-        return block.reshape(D, TILE)
+        block = wide[layer, :, :, :, :, pl.ds(pl.multiple_of(start, 128), TILE)]
+        return block.reshape(ZDEV, REPL, 16, TILE)[:, :TILES_R].reshape(D, TILE)
+
+    def joint_cols(layer, start, stop):
+        return joint[layer, :, :, start:stop].reshape(D, stop - start)
 
     def gathered_sum(own, got):
         total = own[group_at].astype(f32)
@@ -665,15 +867,17 @@
     xs[0] = tokens[section_at]
     bias_at, gain_at, gain_two_at = (0, QKV), (QKV, QKV + D), (QKV + D, QKV + 2 * D)
 
-    def forward(layer, carry):
+    def forward(layer):
         x = xs[layer].astype(f32)
-        gain_one = vectors[layer, :, gain_at[0] : gain_at[1]]
-        gain_two = vectors[layer, :, gain_two_at[0] : gain_two_at[1]]
+        row = vector_row(layer)
+        gain_one = row[:, gain_at[0] : gain_at[1]]
+        gain_two = row[:, gain_two_at[0] : gain_two_at[1]]
         n1 = (x * rms_scale(x) * gain_one).astype(bf16)
         n1s[layer] = n1
-        load(layer, 0).wait()
-        qkv = jnp.dot(n1, joint[layer, :, :QKV], preferred_element_type=f32)
-        qkv = qkv + vectors[layer, :, bias_at[0] : bias_at[1]]
+        if layer == 1:
+            late_weights(0)
+        qkv = jnp.dot(n1, joint_cols(layer, 0, QKV), preferred_element_type=f32)
+        qkv = qkv + row[:, bias_at[0] : bias_at[1]]
         turned = turn(
             qkv[:, : D + KV_WIDTH], cosine[...], sine_up[...], sine_down[...], 1.0
         ).astype(bf16)
@@ -681,12 +885,15 @@
         kvs[layer, group_at] = jnp.concatenate(
             [turned[:, D:], qkv[:, D + KV_WIDTH :].astype(bf16)], axis=1
         )
-        exchange(
+        done = exchange(
             layer, 0, lambda peer: kvs.at[layer, group_at], lambda spot: kvs.at[layer, spot]
-        )()
+        )
+        if layer == 0:
+            while_keys_travel()
+        done()
         kv = kvs[layer].reshape(ROW, 2 * KV_WIDTH)
         keys, values = spread(kv[:, :KV_WIDTH]), spread(kv[:, KV_WIDTH:])
-        outs, row = [], 0
+        outs, at_row = [], 0
         for kind, (pairs, _) in enumerate(KINDS):
             count = SPAN * len(pairs)
             scores = dot_nt(stack_pairs(turned, kind), keys[kind]) * SCALE
@@ -694,18 +901,21 @@
             top = jnp.max(scores, axis=-1, keepdims=True)
             raised = jnp.exp(scores - top)
             prob = raised * (1.0 / jnp.sum(raised, axis=-1, keepdims=True))
-            probs[layer, row : row + count] = prob
+            probs[layer, at_row : at_row + count] = prob
             outs.append(jnp.dot(prob.astype(bf16), values[kind], preferred_element_type=f32))
-            row += count
+            at_row += count
         context = join_pairs(outs).astype(bf16)
         ctx[layer] = context
-        hidden = x + jnp.dot(context, joint[layer, :, QKV:], preferred_element_type=f32)
+        hidden = x + jnp.dot(context, joint_cols(layer, QKV, QKV + D), preferred_element_type=f32)
         hid[layer] = hidden
         n2s[layer, group_at] = (hidden * rms_scale(hidden) * gain_two).astype(bf16)
         done = exchange(
             layer, 1, lambda peer: n2s.at[layer, group_at], lambda spot: n2s.at[layer, spot]
         )
-        load(layer, 1).wait()
+        if layer == 0:
+            while_rows_travel()
+        else:
+            late_weights(1)
         done()
 
         def columns(tile, carry):
@@ -721,17 +931,24 @@
             return carry
 
         lax.fori_loop(0, WIN // TILE, columns, 0)
-        load(layer, 2).wait()
         partial = jnp.dot(act[layer], down[layer], preferred_element_type=f32)
         ysend[layer] = partial.astype(bf16).reshape(ZDEV, SPAN, D)
-        exchange(
+        done = exchange(
             layer, 2, lambda peer: ysend.at[layer, peer], lambda spot: yrecv.at[layer, spot]
-        )()
+        )
+        if layer == 0:
+            while_sums_travel()
+        done()
         mlp = gathered_sum(ysend.at[layer], yrecv.at[layer])
         xs[layer + 1] = (hidden + mlp).astype(bf16)
-        return carry
-
-    lax.fori_loop(0, 2, forward, 0)
+
+    forward(0)
+    dmlp[1, group_at] = cotangent[section_at]
+    grads_done = exchange(
+        1, 3, lambda peer: dmlp.at[1, group_at], lambda spot: dmlp.at[1, spot]
+    )
+    forward(1)
+    grads_done()
     dys[...] = cotangent[section_at].astype(f32)
 
     def hand_over(layer):
@@ -766,15 +983,16 @@
             for at, (source, target) in enumerate(hand_over(layer))
         ]
 
-    def backward(turn_at, carry):
-        layer = 1 - turn_at
-        gain_one = vectors[layer, :, gain_at[0] : gain_at[1]]
-        gain_two = vectors[layer, :, gain_two_at[0] : gain_two_at[1]]
+    def backward(layer):
+        row = vector_row(layer)
+        gain_one = row[:, gain_at[0] : gain_at[1]]
+        gain_two = row[:, gain_two_at[0] : gain_two_at[1]]
         dy = dys[...]
-        dmlp[layer, group_at] = dy.astype(bf16)
-        exchange(
-            layer, 3, lambda peer: dmlp.at[layer, group_at], lambda spot: dmlp.at[layer, spot]
-        )()
+        if layer == 0:
+            dmlp[layer, group_at] = dy.astype(bf16)
+            exchange(
+                layer, 3, lambda peer: dmlp.at[layer, group_at], lambda spot: dmlp.at[layer, spot]
+            )()
         dn2[...] = jnp.zeros_like(dn2)
 
         def columns(tile, carry):
@@ -806,14 +1024,14 @@
         gain_two_term = jnp.sum(grad_two * hidden * scale, axis=0, keepdims=True)
         dt = dhid.astype(bf16)
         rights[layer, :, QKV:] = dt
-        do = dot_nt(dt, joint[layer, :, QKV:]).astype(bf16)
+        do = dot_nt(dt, joint_cols(layer, QKV, QKV + D)).astype(bf16)
         kv = kvs[layer].reshape(ROW, 2 * KV_WIDTH)
         keys, values = spread(kv[:, :KV_WIDTH]), spread(kv[:, KV_WIDTH:])
         queries = qs[layer]
-        dqs, dks, dvs, row = [], [], [], 0
+        dqs, dks, dvs, at_row = [], [], [], 0
         for kind, (pairs, _) in enumerate(KINDS):
             count = SPAN * len(pairs)
-            prob = probs[layer, row : row + count]
+            prob = probs[layer, at_row : at_row + count]
             grad = stack_pairs(do, kind)
             dprob = dot_nt(grad, values[kind])
             inner = jnp.sum(prob * dprob, axis=-1, keepdims=True)
@@ -821,7 +1039,7 @@
             dqs.append(jnp.dot(dscore, keys[kind], preferred_element_type=f32))
             dks.append(dot_tn(dscore, stack_pairs(queries, kind)))
             dvs.append(dot_tn(prob.astype(bf16), grad))
-            row += count
+            at_row += count
         dkv = jnp.concatenate([unspread(dks) * SCALE, unspread(dvs)], axis=1)
         dkvsend[layer] = dkv.astype(bf16).reshape(ZDEV, SPAN, 2 * KV_WIDTH)
         exchange(
@@ -835,7 +1053,7 @@
         lefts[layer, :, :D] = n1s[layer]
         lefts[layer, :, D:] = ctx[layer]
         bias_term = jnp.sum(dqkv.astype(f32), axis=0, keepdims=True)
-        grad_one = dot_nt(dqkv, joint[layer, :, :QKV])
+        grad_one = dot_nt(dqkv, joint_cols(layer, 0, QKV))
         x = xs[layer].astype(f32)
         scale = rms_scale(x)
         scaled = grad_one * gain_one
@@ -844,7 +1062,7 @@
         gain_one_term = jnp.sum(grad_one * x * scale, axis=0, keepdims=True)
         rounded = dx.astype(bf16).astype(f32)
         dys[...] = rounded
-        igs[layer] = jnp.where(layer == 1, rounded, dx)
+        igs[layer] = rounded if layer == 1 else dx
         terms = jnp.concatenate(
             [bias_term, gain_one_term, gain_two_term, jnp.zeros((1, 128), f32)], axis=1
         )
@@ -862,23 +1080,25 @@
             for copy in leaving(layer, section_at):
                 copy.start()
 
-        return carry
-
-    lax.fori_loop(0, 2, backward, 0)
+    backward(1)
+    backward(0)
     for copy in staying(section_at):
         copy.wait()
     for copy in leaving(other, section_at):
         copy.wait_send()
     for copy in leaving(other, other):
         copy.wait_recv()
-
-
-def run_layers(tokens, cotangent, mask, cosine, sine_up, sine_down, vectors, joint, wide, down):
+    links.finish()
+
+
+def run_layers(tokens, cotangent, mask, cosine, sine_up, sine_down, vec, *weights):
     vmem = pl.BlockSpec(memory_space=pltpu.VMEM)
     anywhere = pl.BlockSpec(memory_space=pl.ANY)
 
     def per_micro(shape, kind):
         return jax.ShapeDtypeStruct((2,) + shape, kind)
+
+    sems = 6 + 4 + 1 + 3 * 14 + 2 * 6
 
     def scratch(shape, kind=bf16, lead=2):
         return pltpu.VMEM((lead,) + shape, kind)
@@ -896,12 +1116,14 @@
             per_micro((SPAN, QKV + D), bf16),
             per_micro((16, 256), f32),
         ),
-        in_specs=[vmem] * 7 + [anywhere] * 3,
+        in_specs=[vmem] * 7 + [anywhere] * 5,
         out_specs=[vmem] * 9,
         scratch_shapes=[
-            scratch((D, QKV + D)),
-            scratch((ZDEV, TILES_R, 16, 2 * WIN)),
+            scratch((ZDEV, OWN, QKV + D)),
+            scratch((ZDEV, RING, RING, 16, 2 * WIN)),
             scratch((WIN, D)),
+            scratch((ZDEV, 8, 384), f32),
+            pltpu.VMEM((64, D), bf16),
             scratch((SPAN, D), lead=3),
             scratch((SPAN, D)),
             scratch((SPAN, D)),
@@ -928,186 +1150,18 @@
             scratch((SPAN, D), f32),
             pltpu.SemaphoreType.DMA((2, 6, 3)),
             pltpu.SemaphoreType.DMA((2, 6, 3)),
-            pltpu.SemaphoreType.DMA((2, 3)),
             pltpu.SemaphoreType.DMA((9,)),
             pltpu.SemaphoreType.DMA((9,)),
             pltpu.SemaphoreType.DMA((9,)),
+            pltpu.SemaphoreType.DMA((sems,)),
+            pltpu.SemaphoreType.DMA((sems,)),
+            pltpu.SemaphoreType.DMA((8,)),
         ],
         compiler_params=pltpu.CompilerParams(
             collective_id=3, has_side_effects=True, vmem_limit_bytes=60 * 1024 * 1024
         ),
         name="layers",
-    )(tokens, cotangent, mask, cosine, sine_up, sine_down, vectors, joint, wide, down)
-
-
-def weights_kernel(
-    w_qkv, w_out, w_gate, w_up, w_down, vec,
-    joint, wide, down, vectors,
-    zeros, send_sems, recv_sems, local_sems,
-):
-    section_at = lax.axis_index("section")
-    group_at = lax.axis_index("group")
-    replica_at = lax.axis_index("replica")
-    x_at, y_at = replica_at // RING, lax.rem(replica_at, RING)
-    links = Links(send_sems, recv_sems)
-    sibling = {"section": 1 - section_at}
-
-    def along_x(spot):
-        return {"replica": spot * RING + y_at}
-
-    def along_y(spot):
-        return {"replica": x_at * RING + spot}
-
-    def along_z(spot):
-        return {"group": spot}
-
-    zeros[...] = jnp.zeros_like(zeros)
-    peers = [ring_spot(group_at, step) for step in (1, 2, 3)]
-    greet(
-        [
-            ring_spot(x_at, 1) * RING + y_at,
-            ring_spot(x_at, -1) * RING + y_at,
-            x_at * RING + ring_spot(y_at, 1),
-            x_at * RING + ring_spot(y_at, -1),
-        ],
-        peers,
-        [1 - section_at],
-    )
-    row_tile = pl.ds(pl.multiple_of(jnp.minimum(replica_at, TILES_R - 1) * 16, 16), 16)
-    slots = []
-    for which, source in enumerate((w_gate, w_up)):
-        target = wide.at[section_at, group_at, x_at, y_at, :, WIN * which : WIN * (which + 1)]
-        slots.append((source, target))
-
-    def window(source, spot):
-        start = pl.multiple_of((19 * spot) // 2 * 128, 128)
-        return source.at[row_tile, pl.ds(start, WIN)]
-
-    slot_sem = links.take(6)
-    for step, peer in enumerate(peers):
-        for which, (source, target) in enumerate(slots):
-            links.send(window(source, peer), target, slot_sem + 2 * step + which, along_z(peer))
-    vec_sem = links.take(4)
-    for step, peer in enumerate(peers):
-        links.send(vec, vectors.at[section_at, group_at], vec_sem + step, along_z(peer))
-    shift = lax.rem(group_at, 2) * 64
-    body = pl.ds(pl.multiple_of(shift, 64), BLOCK)
-    gap = pl.ds(pl.multiple_of(BLOCK - 19 * shift, 64), 64)
-    locals_ = []
-    for source, target in [
-        *[(window(source, group_at), target) for source, target in slots],
-        (w_qkv, joint.at[section_at, group_at, :, 0:QKV]),
-        (w_out, joint.at[section_at, group_at, :, QKV : QKV + D]),
-        (w_down, down.at[section_at, body]),
-        (zeros, down.at[0, gap]),
-        (zeros, down.at[1, gap]),
-        (vec, vectors.at[section_at, group_at]),
-    ]:
-        copy = pltpu.make_async_copy(source, target, local_sems.at[len(locals_)])
-        copy.start()
-        locals_.append(copy)
-    for at in (2, 3):
-        locals_[at].wait()
-
-    def joint_block(spot, half):
-        return joint.at[section_at, spot, pl.ds(112 * half, 112)]
-
-    joint_share = RingShare(links, group_at, along_z, joint_block, sibling)
-    joint_share.start()
-    down_sem = links.take(1)
-    down_view = down.at[section_at, body]
-    links.send(w_down, down_view, down_sem, sibling)
-    locals_[0].wait()
-    locals_[1].wait()
-
-    def arrived_slots(which):
-        for step, peer in enumerate(peers):
-            spot = ring_spot(group_at, -1 - step)
-            cols = pl.ds(WIN * which, WIN)
-            target = wide.at[section_at, spot, x_at, y_at, :, cols]
-            links.arrived(target, slot_sem + 2 * step + which, along_z(peer))
-
-    def sharers(which, x_first):
-        start = WIN * which
-
-        def small(spot, half):
-            cols = pl.ds(start + WIN // 2 * half, WIN // 2)
-            if x_first:
-                return wide.at[section_at, :, spot, y_at, :, cols]
-            return wide.at[section_at, :, x_at, spot, :, cols]
-
-        def big(spot, half):
-            span, cols = pl.ds(2 * half, 2), pl.ds(start, WIN)
-            if x_first:
-                return wide.at[section_at, :, span, spot, :, cols]
-            return wide.at[section_at, :, spot, span, :, cols]
-
-        one = (x_at, along_x) if x_first else (y_at, along_y)
-        two = (y_at, along_y) if x_first else (x_at, along_x)
-        return RingShare(links, *one, small), RingShare(links, *two, big, sibling)
-
-    gate_one, gate_two = sharers(0, False)
-    up_one, up_two = sharers(1, True)
-    arrived_slots(0)
-    gate_one.start()
-    arrived_slots(1)
-    up_one.start()
-    gate_one.middle()
-    up_one.middle()
-    gate_one.end()
-    gate_two.start()
-    up_one.end()
-    up_two.start()
-    joint_share.middle()
-    for step, peer in enumerate(peers):
-        spot = ring_spot(group_at, -1 - step)
-        links.arrived(vectors.at[section_at, spot], vec_sem + step, along_z(peer))
-    locals_[7].wait()
-    links.send(vectors.at[section_at], vectors.at[section_at], vec_sem + 3, sibling)
-    gate_two.middle()
-    up_two.middle()
-    joint_share.end()
-    gate_two.end()
-    up_two.end()
-    other = 1 - section_at
-    for at in (4, 5, 6):
-        locals_[at].wait()
-    links.arrived(down.at[other, body], down_sem, sibling)
-    links.arrived(vectors.at[other], vec_sem + 3, sibling)
-    joint_share.end_twin(lambda spot, half: joint.at[other, spot, pl.ds(112 * half, 112)])
-    for which, share in ((0, gate_two), (1, up_two)):
-        cols = pl.ds(WIN * which, WIN)
-        if which:
-            share.end_twin(lambda s, h: wide.at[other, :, pl.ds(2 * h, 2), s, :, cols])
-        else:
-            share.end_twin(lambda s, h: wide.at[other, :, s, pl.ds(2 * h, 2), :, cols])
-    links.finish()
-
-
-def share_weights(w_qkv, w_out, w_gate, w_up, w_down, vec):
-    anywhere = pl.BlockSpec(memory_space=pl.ANY)
-    sems = 6 + 4 + 1 + 3 * 14 + 2 * 6
-    return pl.pallas_call(
-        weights_kernel,
-        out_shape=(
-            jax.ShapeDtypeStruct((2, ZDEV, OWN, QKV + D), bf16),
-            jax.ShapeDtypeStruct((2, ZDEV, RING, RING, 16, 2 * WIN), bf16),
-            jax.ShapeDtypeStruct((2, WIN, D), bf16),
-            jax.ShapeDtypeStruct((2, ZDEV, 8, 128), f32),
-        ),
-        in_specs=[anywhere] * 6,
-        out_specs=[pl.BlockSpec(memory_space=pltpu.VMEM)] * 4,
-        scratch_shapes=[
-            pltpu.VMEM((64, D), bf16),
-            pltpu.SemaphoreType.DMA((sems,)),
-            pltpu.SemaphoreType.DMA((sems,)),
-            pltpu.SemaphoreType.DMA((8,)),
-        ],
-        compiler_params=pltpu.CompilerParams(
-            collective_id=2, has_side_effects=True, vmem_limit_bytes=58 * 1024 * 1024
-        ),
-        name="weights",
-    )(w_qkv, w_out, w_gate, w_up, w_down, vec)
+    )(tokens, cotangent, mask, cosine, sine_up, sine_down, vec, *weights)
 
 
 def on_device(
@@ -1115,24 +1169,23 @@
 ):
     section_at = lax.axis_index("section")
     group_at = lax.axis_index("group")
-    vec = jnp.concatenate([b_qkv[0], norm_attn[0], norm_ffn[0]]).astype(f32)
-    vec = jnp.pad(vec, (0, 1024 - vec.shape[0])).reshape(8, 128)
-    joint, wide, down, vectors = share_weights(
-        w_qkv[0], w_out[0], w_gate[0], w_up[0], w_down[0], vec
-    )
-    vectors = vectors.reshape(2, ZDEV, 1024)
-    parts = (vectors[..., : QKV // 4], vectors[..., QKV // 4 : QKV // 4 + OWN])
-    parts = parts + (vectors[..., QKV // 4 + OWN : QKV // 4 + 2 * OWN],)
-    vectors = jnp.concatenate([part.reshape(2, 1, -1) for part in parts], axis=2)
+    vec = jnp.zeros((8 * 384,), f32)
+    for member, start in ((b_qkv, 0), (norm_attn, QKV), (norm_ffn, QKV + D)):
+        width = member.shape[1]
+        vec = lax.dynamic_update_slice(
+            vec, member[0].astype(f32), (start + width * group_at,)
+        )
     lengths = lax.dynamic_index_in_dim(doc_lengths, section_at, 0, keepdims=False)[0]
     acts, input_grads, *pieces = run_layers(
         tokens[:, 0],
         cotangent[:, 0],
         *doc_tables(lengths, group_at),
-        vectors,
-        joint.reshape(2, D, QKV + D),
-        wide.reshape(2, ZDEV, REPL, 16, 2 * WIN),
-        down,
+        vec.reshape(8, 384),
+        w_qkv[0],
+        w_out[0],
+        w_gate[0],
+        w_up[0],
+        w_down[0],
     )
     grads = weight_grads(*pieces)
     return (acts[None, :, None], input_grads[None, :, None]) + tuple(g[None] for g in grads)

time: 295 us -> 283 us (0.959)
  other arithmetic: 15.9 us -> 5.57 us
  local copies, waits for them, and re-layouts: 13.2 us -> 8.08 us
  Pallas kernels: 265 us -> 268 us
    pallas_call x1, Pallas kernels: 55.5 us -> 8.52 us  [widen(): pl.pallas_call(widen_kernel, grid=(TILES_R,), out_shape=[jax.ShapeDtypeSt...]
    pallas_call x1, Pallas kernels: 104 us -> 151 us  [run_layers(): pl.pallas_call(layers_kernel, out_shape=(per_micro((SPAN, D), bf16), per_...]
    slice x7 -> x0, local copies, waits for them, and re-layouts: 7.41 us -> none  [the longest x3 4.7 us: rows_of(): block = shared[:TILES_R, :, start:start + width]]
    convert_element_type x5 -> x3, other arithmetic: 9.01 us -> 2.07 us  [on_device(): member[0].astype(f32)]
    pallas_call x1, Pallas kernels: 105 us -> 109 us  [share_grads(): pl.pallas_call(grads_kernel, out_shape=jax.ShapeDtypeStruct((RING, RING,...]
    unnamed x7 -> x9, local copies, waits for them, and re-layouts: 1.48 us -> 4.69 us
where the time goes in v4:
time: 283 us; the launch traced here: 282 us
  Pallas kernels  268 us (95%)
  local copies, waits for them, and re-layouts  8.08 us (3%)
  other arithmetic  5.57 us (2%)
    pallas_call x1, Pallas kernels, run_layers(): pl.pallas_call(layers_kernel, out_shape=(per_micro((SPAN, D), bf16), per_...  151 us
    pallas_call x1, Pallas kernels, share_grads(): pl.pallas_call(grads_kernel, out_shape=jax.ShapeDtypeStruct((RING, RING,...  109 us
    pallas_call x1, Pallas kernels, widen(): pl.pallas_call(widen_kernel, grid=(TILES_R,), out_shape=[jax.ShapeDtypeSt...  8.52 us

profile of v4, /device:TPU:0, one launch (start us, length us, event | category | flops | bytes accessed | tf_op | source)
XLA Modules:
  0.0 282.5 jit_solution(10007641710180650534)
XLA Ops:
  0.7 0.7 fusion.3
  1.3 0.2 reduce-window.7
  1.5 0.7 bitcast_subtract_fusion
  2.1 0.1 convert_reduce_fusion
  2.2 0.1 select_reduce_fusion
  2.3 0.1 dynamic_slice.23
  2.4 0.7 convert_element_type.45
  3.1 0.7 convert_element_type.46
  3.8 0.1 subtract_convert_fusion
  3.9 0.7 convert_reduce_fusion.1
  4.6 0.3 dynamic_update_slice.9
  4.9 0.3 dynamic_update_slice.10
  5.1 0.2 dynamic_update_slice.11
  5.3 0.6 reshape.89.vec
  5.9 0.7 fusion.1.mask
  6.6 0.2 multiply_sine_fusion
  6.9 0.8 pad_maximum_fusion.2
  7.6 150.8 %layers.1 = (bf16[2,64,896]{2,1,0:T(8,128)(2,1)}, f32[2,64,896]{2,1,0:T(8,128)}, bf16[2,4,64,896]{3,2,1,0:T(8,128)(2,1)}, bf16[2,256,2560]{2,1,0:T(8,128)(2,1)},...) custom-call(bf16[2,64,896]{2,1,0:T(8,128)(2,1)} %bitcast.50, ...), custom_call_target="tpu_custom_call" | custom-call | tf_op jit(solution)/shard_map/layers/pallas_call | solution.py:1106
  158.4 108.9 %grads.1 = bf16[4,4,16,15232]{3,2,1,0:T(8,128)(2,1)} custom-call(bf16[512,896]{1,0:T(8,128)(2,1)} %bitcast.44, bf16[512,2560]{1,0:T(8,128)(2,1)} %bitcast.39, bf16[512,1280]{1,0:T(8,128)(2,1)} %bitcast.43, bf16[512,896]{1,0:T(8,128)(2,1)} %bitcast.45, bf16[2,64,1792]{2,1,0:T(8,128)(2,1)} %get-tuple-element.30.left_tokens, ...), custom_call_target="tpu_custom_call" | custom-call | tf_op jit(solution)/shard_map/grads/pallas_call | solution.py:468
  267.3 0.7 convert_bitcast_fusion
  268.0 0.6 fusion.4
  268.6 0.1 dynamic_slice.26
  268.7 0.6 broadcast_in_dim.66
  269.3 0.0 copy-start
  269.3 3.2 %copy-done = bf16[4,4,16,15232]{3,2,1,0:T(8,128)(2,1)S(1)} copy-done((bf16[4,4,16,15232]{3,2,1,0:T(8,128)(2,1)S(1)}, bf16[4,4,16,15232]{3,2,1,0:T(8,128)(2,1)}, u32[]{:S(2)}) %copy-start) | copy-done | bytes 7798808
  272.5 0.0 copy-start.2
  272.5 0.0 copy-start.1
  272.5 8.5 %widen.1 = (f32[224,4864]{1,0:T(8,128)}, f32[224,4864]{1,0:T(8,128)}, f32[224,1152]{1,0:T(8,128)}, f32[224,896]{1,0:T(8,128)}, f32[1216,896]{1,0:T(8,128)}) custom-call(bf16[16,16,15232]{2,1,0:T(8,128)(2,1)S(1)} %bitcast.37, bf16[16,16,15232]{2,1,0:T(8,128)(2,1)S(1)} %bitcast.38), custom_call_target="tpu_custom_call" | custom-call | tf_op jit(solution)/shard_map/widen/pallas_call | solution.py:519
  281.0 0.0 copy-done.2
  281.0 0.7 copy.31
  281.7 0.0 copy-done.1
  281.7 0.8 copy.32
  (5 shorter events, 0.0 us)
Async XLA Ops:
  269.3 3.2 %copy-start = (bf16[4,4,16,15232]{3,2,1,0:T(8,128)(2,1)S(1)}, bf16[4,4,16,15232]{3,2,1,0:T(8,128)(2,1)}, u32[]{:S(2)}) copy-start(bf16[4,4,16,15232]{3,2,1,0:T(8,128)(2,1)} %grads.1) | copy-start | bytes 23396356
  272.5 8.5 %copy-start.2 = (bf16[2,64,896]{2,1,0:T(8,128)(2,1)S(1)}, bf16[2,64,896]{2,1,0:T(8,128)(2,1)}, u32[]{:S(2)}) copy-start(bf16[2,64,896]{2,1,0:T(8,128)(2,1)} %get-tuple-element.24) | copy-start | bytes 688132
  272.5 9.2 %copy-start.1 = (f32[2,64,896]{2,1,0:T(8,128)S(1)}, f32[2,64,896]{2,1,0:T(8,128)}, u32[]{:S(2)}) copy-start(f32[2,64,896]{2,1,0:T(8,128)} %get-tuple-element.25) | copy-start | bytes 1376260

commit v5 on v4

--- a/solution.py
+++ b/solution.py
@@ -1,3 +1,5 @@
+import math
+
 import jax
 import jax.numpy as jnp
 from jax import lax
@@ -33,30 +35,6 @@
     return lax.rsqrt(jnp.mean(values * values, axis=-1, keepdims=True) + eps)
 
 
-def doc_tables(doc_lens, group_at):
-    doc_ends = jnp.cumsum(doc_lens)
-    doc_starts = doc_ends - doc_lens
-    row_spots = jnp.arange(ROW, dtype=jnp.int32)
-    segment = jnp.sum((doc_ends[None, :] <= row_spots[:, None]).astype(jnp.int32), axis=1)
-    doc_pick = segment[:, None] == jnp.arange(doc_lens.shape[0], dtype=jnp.int32)[None, :]
-    doc_begin = jnp.sum(jnp.where(doc_pick, doc_starts[None, :], 0), axis=1)
-    first_row = group_at * SPAN
-    own_segment = lax.dynamic_slice_in_dim(segment, first_row, SPAN)
-    own_spots = lax.dynamic_slice_in_dim(row_spots, first_row, SPAN)
-    own_begin = lax.dynamic_slice_in_dim(doc_begin, first_row, SPAN)
-    allowed = (own_segment[:, None] == segment[None, :]) & (
-        row_spots[None, :] <= own_spots[:, None]
-    )
-    inv_freqs = rope_base ** (-jnp.arange(0, HEAD_DIM, 2, dtype=f32) / HEAD_DIM)
-    angles = (own_spots - own_begin).astype(f32)[:, None] * inv_freqs[None, :]
-    cosine, sine = jnp.cos(angles), jnp.sin(angles)
-    blank = jnp.zeros_like(sine)
-    cosine = jnp.concatenate([cosine] * 4, axis=1)
-    sine_up = jnp.concatenate([-sine, blank] * 2, axis=1)
-    sine_down = jnp.concatenate([blank, sine] * 2, axis=1)
-    return (allowed.astype(f32), cosine, sine_up, sine_down)
-
-
 MESH = pl.DeviceIdType.MESH
 TILES_R = OWN // 16
 COLS = 15232
@@ -225,7 +203,7 @@
 
 def grads_kernel(
     n2_rows, dgu, act_rows, dmlp, left_tokens, right_tokens, vecs,
-    shared, n2t, act, left_rows, right_rows, vec, part, own, zbuf, left_all, right_all, vec_all,
+    shared, n2t, act, left_rows, vec, part, own, zbuf, left_all, right_all, vec_all,
     a_first, a_second, a_left, a_right, a_sum, a_first2, a_second2, a_left2, a_right2,
     b_first, b_second, b_left, b_right, b_sum, b_first2, b_second2, b_left2, b_right2,
     c_first, c_second, c_left, c_right, c_sum, c_first2, c_second2, c_left2, c_right2,
@@ -252,40 +230,98 @@
         ],
         peers,
     )
-    right_rows[...] = right_tokens[...].reshape(2 * SPAN, QKV + D)
+    right_all[group_at] = right_tokens[...].reshape(2 * SPAN, QKV + D)
+    rights_share = RingShare(
+        links,
+        group_at,
+        lambda spot: {"group": spot},
+        lambda spot, half: right_all.at[spot, pl.ds(SPAN * half, SPAN)],
+    )
+    rights_share.start()
     vec[...] = vecs[0] + vecs[1]
     tall = left_tokens[...].reshape(2 * SPAN, 2 * D).T
     for z in range(ZDEV):
         left_rows[z, :OWN] = tall[OWN * z : OWN * (z + 1)]
         left_rows[z, OWN:] = tall[D + OWN * z : D + OWN * (z + 1)]
-    tok_sem = links.take(9)
+    tok_sem = links.take(6)
     for step, peer in enumerate(peers):
         for at, (source, target) in enumerate(
             [
                 (left_rows.at[peer], left_all.at[group_at]),
-                (right_rows, right_all.at[group_at]),
                 (vec, vec_all.at[group_at]),
             ]
         ):
-            links.send(source, target, tok_sem + 3 * step + at, {"group": peer})
+            links.send(source, target, tok_sem + 2 * step + at, {"group": peer})
     left_all[group_at] = left_rows[group_at]
-    right_all[group_at] = right_rows[...]
     vec_all[group_at] = vec[...]
 
     n2t[...] = n2_rows[...].T
+
+    def gate_up(first, count):
+        def columns(tile, carry):
+            at = pl.multiple_of(tile * 256, 256)
+            block = jnp.dot(
+                n2t[OWN * first : OWN * (first + count)],
+                dgu[:, pl.ds(at, 256)],
+                preferred_element_type=f32,
+            ).astype(bf16)
+            block = block.reshape(count, TILES_R, 16, 256)
+            for z in range(count):
+                where = pl.multiple_of(tile * 256 + (first + z) * 2 * WIN, 128)
+                for r in range(TILES_R):
+                    part[r // RING, r % RING, :, pl.ds(where, 256)] = block[z, r]
+            return carry
+
+        lax.fori_loop(0, 2 * WIN // 256, columns, 0)
+
     act[...] = act_rows[...].T
-
-    def gate_up(tile, carry):
-        at = pl.multiple_of(tile * 256, 256)
-        block = jnp.dot(n2t[...], dgu[:, pl.ds(at, 256)], preferred_element_type=f32).astype(bf16)
-        block = block.reshape(ZDEV, TILES_R, 16, 256)
-        for z in range(ZDEV):
-            where = pl.multiple_of(tile * 256 + z * 2 * WIN, 128)
-            for r in range(TILES_R):
-                part[r // RING, r % RING, :, pl.ds(where, 256)] = block[z, r]
-        return carry
-
-    lax.fori_loop(0, 2 * WIN // 256, gate_up, 0)
+    def summers(cols, x_first, bufs):
+        first, second, left, right, total, first2, second2, left2, right2 = bufs
+        start, stop = cols
+
+        def big(spot, half):
+            span = pl.ds(2 * half, 2)
+            if x_first:
+                return part.at[spot, span, :, start:stop]
+            return part.at[span, spot, :, start:stop]
+
+        cuts = halves(0, stop - start)
+
+        def small(spot, half):
+            return total.at[spot, :, cuts[half][0] : cuts[half][1]]
+
+        def pair(buf):
+            return lambda half: buf.at[pl.ds(2 * half, 2)]
+
+        def cut(buf):
+            return lambda half: buf.at[:, cuts[half][0] : cuts[half][1]]
+
+        one = (x_at, along_x) if x_first else (y_at, along_y)
+        two = (y_at, along_y) if x_first else (x_at, along_x)
+        stage_one = RingSum(
+            links, *one, big, first, second, pair(left), pair(right), add_into
+        )
+        stage_two = RingSum(
+            links, *two, small, first2, second2, cut(left2), cut(right2), add_into
+        )
+
+        def result(half):
+            return own.at[:, start + cuts[half][0] : start + cuts[half][1]]
+
+        return stage_one, stage_two, pair(total), result
+
+    a_one, a_two, a_mid, a_result = summers(
+        PART_A, True,
+        (a_first, a_second, a_left, a_right, a_sum, a_first2, a_second2, a_left2, a_right2),
+    )
+    b_one, b_two, b_mid, b_result = summers(
+        PART_B, False,
+        (b_first, b_second, b_left, b_right, b_sum, b_first2, b_second2, b_left2, b_right2),
+    )
+    c_one, c_two, c_mid, c_result = summers(
+        PART_C, False,
+        (c_first, c_second, c_left, c_right, c_sum, c_first2, c_second2, c_left2, c_right2),
+    )
     shift = lax.rem(group_at, 2) * 64
     for quarter in range(4):
         rows = pl.ds(pl.multiple_of(shift + 304 * quarter, 16), 304)
@@ -298,62 +334,18 @@
             else:
                 r, at = TILES_R + (tile - 3 * TILES_R) // 17, D * ((tile - 3 * TILES_R) % 17)
             part[r // RING, r % RING, :, at : at + D] = block[inner]
-
-    def summers(cols, x_first, bufs):
-        first, second, left, right, total, first2, second2, left2, right2 = bufs
-        start, stop = cols
-
-        def big(spot, half):
-            span = pl.ds(2 * half, 2)
-            if x_first:
-                return part.at[spot, span, :, start:stop]
-            return part.at[span, spot, :, start:stop]
-
-        cuts = halves(0, stop - start)
-
-        def small(spot, half):
-            return total.at[spot, :, cuts[half][0] : cuts[half][1]]
-
-        def pair(buf):
-            return lambda half: buf.at[pl.ds(2 * half, 2)]
-
-        def cut(buf):
-            return lambda half: buf.at[:, cuts[half][0] : cuts[half][1]]
-
-        one = (x_at, along_x) if x_first else (y_at, along_y)
-        two = (y_at, along_y) if x_first else (x_at, along_x)
-        stage_one = RingSum(
-            links, *one, big, first, second, pair(left), pair(right), add_into
-        )
-        stage_two = RingSum(
-            links, *two, small, first2, second2, cut(left2), cut(right2), add_into
-        )
-
-        def result(half):
-            return own.at[:, start + cuts[half][0] : start + cuts[half][1]]
-
-        return stage_one, stage_two, pair(total), result
-
-    a_one, a_two, a_mid, a_result = summers(
-        PART_A, True,
-        (a_first, a_second, a_left, a_right, a_sum, a_first2, a_second2, a_left2, a_right2),
-    )
-    b_one, b_two, b_mid, b_result = summers(
-        PART_B, False,
-        (b_first, b_second, b_left, b_right, b_sum, b_first2, b_second2, b_left2, b_right2),
-    )
-    c_one, c_two, c_mid, c_result = summers(
-        PART_C, False,
-        (c_first, c_second, c_left, c_right, c_sum, c_first2, c_second2, c_left2, c_right2),
-    )
+    rights_share.middle()
+    gate_up(0, 3)
     a_one.start()
+    gate_up(3, 1)
     b_one.start()
     a_one.middle()
     b_one.middle()
     for step, peer in enumerate(peers):
         source = ring_spot(group_at, -1 - step)
-        for at, target in enumerate((left_all, right_all, vec_all)):
-            links.arrived(target.at[source], tok_sem + 3 * step + at, {"group": peer})
+        for at, target in enumerate((left_all, vec_all)):
+            links.arrived(target.at[source], tok_sem + 2 * step + at, {"group": peer})
+    rights_share.end()
     for width, col, row in ((QKV, 0, 0), (D, QKV, OWN)):
         total = jnp.dot(
             left_all[0, row : row + OWN], right_all[0, :, col : col + width],
@@ -464,7 +456,7 @@
         return [pltpu.VMEM(shape, bf16) for shape in shapes]
 
     vmem = pl.BlockSpec(memory_space=pltpu.VMEM)
-    sems = 9 + 3 + 6 * 6 + 4 * 6
+    sems = 6 + 6 + 3 + 6 * 6 + 4 * 6
     return pl.pallas_call(
         grads_kernel,
         out_shape=jax.ShapeDtypeStruct((RING, RING, 16, COLS), bf16),
@@ -474,7 +466,6 @@
             pltpu.VMEM((D, 2 * ROW), bf16),
             pltpu.VMEM((WIN, 2 * ROW), bf16),
             pltpu.VMEM((ZDEV, 2 * OWN, 2 * SPAN), bf16),
-            pltpu.VMEM((2 * SPAN, QKV + D), bf16),
             pltpu.VMEM((16, 256), f32),
             pltpu.VMEM((RING, RING, 16, COLS), bf16),
             pltpu.VMEM((16, COLS), bf16),
@@ -497,17 +488,19 @@
 
 def widen_kernel(block, rest, gate, up, qkv, out, down):
     at = pl.program_id(0)
-    for target, start, width in (
-        (gate, 0, FF), (up, FF, FF), (qkv, QO_AT, QKV), (out, QO_AT + QKV, D),
-    ):
-        target[...] = block[0, :, start : start + width].astype(f32)
-    for inner in range(3):
-        rows = pl.ds(pl.multiple_of((3 * at + inner) * 16, 16), 16)
-        start = DOWN_AT + D * inner
-        down[rows, :] = block[0, :, start : start + D].astype(f32)
+    for inner in range(2):
+        rows = pl.ds(16 * inner, 16)
+        for target, start, width in (
+            (gate, 0, FF), (up, FF, FF), (qkv, QO_AT, QKV), (out, QO_AT + QKV, D),
+        ):
+            target[rows, :] = block[inner, :, start : start + width].astype(f32)
+        for place in range(3):
+            tile = pl.multiple_of((6 * at + 3 * inner + place) * 16, 16)
+            start = DOWN_AT + D * place
+            down[pl.ds(tile, 16), :] = block[inner, :, start : start + D].astype(f32)
     for tile in range(34):
 
-        @pl.when(at == tile // 3)
+        @pl.when(at == tile // 5)
         def _():
             rows = pl.ds((3 * TILES_R + tile) * 16, 16)
             start = D * (tile % 17)
@@ -518,14 +511,14 @@
     rows = [FF, FF, QKV, D]
     return pl.pallas_call(
         widen_kernel,
-        grid=(TILES_R,),
+        grid=(TILES_R // 2,),
         out_shape=[jax.ShapeDtypeStruct((OWN, width), f32) for width in rows]
         + [jax.ShapeDtypeStruct((BLOCK, D), f32)],
         in_specs=[
-            pl.BlockSpec((1, 16, COLS), lambda at: (at, 0, 0)),
+            pl.BlockSpec((2, 16, COLS), lambda at: (at, 0, 0)),
             pl.BlockSpec((2, 16, COLS), lambda at: (TILES_R // 2, 0, 0)),
         ],
-        out_specs=[pl.BlockSpec((16, width), lambda at: (at, 0)) for width in rows]
+        out_specs=[pl.BlockSpec((32, width), lambda at: (at, 0)) for width in rows]
         + [pl.BlockSpec((BLOCK, D), lambda at: (0, 0))],
         compiler_params=pltpu.CompilerParams(vmem_limit_bytes=40 * 1024 * 1024),
         name="widen",
@@ -623,12 +616,13 @@
 
 
 def layers_kernel(
-    tokens, cotangent, mask, cosine, sine_up, sine_down, vec,
+    tokens, cotangent, lengths, vec,
     w_qkv, w_out, w_gate, w_up, w_down,
     acts, grads_in, out_n2, out_dgu, out_act, out_dmlp, out_left, out_right, out_vec,
-    joint, wide, down, vectors, zeros,
-    xs, n1s, qs, kvs, probs, ctx, hid, n2s, gus, act, ysend, yrecv,
-    dys, dmlp, dgu, dn2, dsend, drecv, dkvsend, dkvrecv, lefts, rights, vecs, igs,
+    joint, wide, down, vectors, zeros, mask, cosine, sine_up, sine_down,
+    xs, n1s, qs, kvs, probs, ctx, hid, n2s, gus, act, ysend,
+    sum_first, sum_second, sum_left, sum_right, row_total,
+    dys, dmlp, dgu, dn2, dsend, dkvsend, dkvrecv, lefts, rights, vecs, igs,
     send_sems, recv_sems, away_send, away_recv, stay_sems, ring_send, ring_recv, local_sems,
 ):
     section_at = lax.axis_index("section")
@@ -751,6 +745,28 @@
         gate_two.start()
         up_two.start()
 
+    def starts(spots):
+        begin, end = jnp.zeros_like(spots), 0
+        for doc in range(lengths.shape[2]):
+            length = lengths[section_at, 0, doc]
+            end = end + length
+            begin = begin + jnp.where(spots >= end, length, 0)
+        return begin
+
+    own_spots = lax.broadcasted_iota(jnp.int32, (SPAN, ROW), 0) + group_at * SPAN
+    row_spots = lax.broadcasted_iota(jnp.int32, (SPAN, ROW), 1)
+    own_begin = starts(own_spots)
+    allowed_now = (own_begin == starts(row_spots)) & (row_spots <= own_spots)
+    mask[...] = jnp.where(allowed_now, 1.0, 0.0).astype(f32)
+    lane = lax.broadcasted_iota(jnp.int32, (SPAN, 128), 1)
+    turn_at = lax.rem(lane, HEAD_DIM // 2).astype(f32)
+    freqs = jnp.exp(turn_at * (-2.0 / HEAD_DIM * math.log(rope_base)))
+    angles = (own_spots - own_begin)[:, :128].astype(f32) * freqs
+    sine = jnp.sin(angles)
+    cosine[...] = jnp.cos(angles)
+    first_half = lax.rem(lane, HEAD_DIM) < HEAD_DIM // 2
+    sine_up[...] = jnp.where(first_half, -sine, 0.0)
+    sine_down[...] = jnp.where(first_half, 0.0, sine)
     locals_[7].wait()
     for step, spot in enumerate(sources):
         links.arrived(vectors.at[section_at, spot], vec_sem + step, along_z(peers[step]))
@@ -768,7 +784,6 @@
         locals_[2].wait()
         locals_[3].wait()
         joint_share.end_twin(joint_twin)
-        joint_share.start()
 
     links.arrived(vectors.at[other], vec_sem + 3, sibling)
     for at in (4, 5, 6):
@@ -784,13 +799,14 @@
         def _():
             gate_two.start()
             up_two.start()
-            joint_share.middle()
+            joint_share.start()
 
     def while_rows_travel():
         @pl.when(section_at == 1)
         def _():
             gate_two.middle()
             up_two.middle()
+            joint_share.middle()
             gate_two.end_twin(gate_twin)
             up_two.end_twin(up_twin)
 
@@ -866,6 +882,23 @@
 
     xs[0] = tokens[section_at]
     bias_at, gain_at, gain_two_at = (0, QKV), (QKV, QKV + D), (QKV + D, QKV + 2 * D)
+
+    def row_share(rows):
+        return RingShare(
+            links, group_at, along_z, lambda spot, half: rows.at[spot, pl.ds(32 * half, 32)]
+        )
+
+    def row_sum(rows, use):
+        def pair(buf):
+            return lambda half: buf.at[use, pl.ds(32 * half, 32)]
+
+        return RingSum(
+            links, group_at, along_z, lambda spot, half: rows.at[spot, pl.ds(32 * half, 32)],
+            sum_first.at[use], sum_second.at[use], pair(sum_left), pair(sum_right), add_into,
+        )
+
+    def sum_half(half):
+        return row_total.at[pl.ds(32 * half, 32)]
 
     def forward(layer):
         x = xs[layer].astype(f32)
@@ -890,6 +923,8 @@
         )
         if layer == 0:
             while_keys_travel()
+        else:
+            grads_share.middle()
         done()
         kv = kvs[layer].reshape(ROW, 2 * KV_WIDTH)
         keys, values = spread(kv[:, :KV_WIDTH]), spread(kv[:, KV_WIDTH:])
@@ -909,14 +944,14 @@
         hidden = x + jnp.dot(context, joint_cols(layer, QKV, QKV + D), preferred_element_type=f32)
         hid[layer] = hidden
         n2s[layer, group_at] = (hidden * rms_scale(hidden) * gain_two).astype(bf16)
-        done = exchange(
-            layer, 1, lambda peer: n2s.at[layer, group_at], lambda spot: n2s.at[layer, spot]
-        )
+        share = row_share(n2s.at[layer])
+        share.start()
+        share.middle()
         if layer == 0:
             while_rows_travel()
         else:
             late_weights(1)
-        done()
+        share.end()
 
         def columns(tile, carry):
             at = tile * TILE
@@ -933,22 +968,20 @@
         lax.fori_loop(0, WIN // TILE, columns, 0)
         partial = jnp.dot(act[layer], down[layer], preferred_element_type=f32)
         ysend[layer] = partial.astype(bf16).reshape(ZDEV, SPAN, D)
-        done = exchange(
-            layer, 2, lambda peer: ysend.at[layer, peer], lambda spot: yrecv.at[layer, spot]
-        )
+        adder = row_sum(ysend.at[layer], layer)
+        adder.start()
+        adder.middle()
         if layer == 0:
             while_sums_travel()
-        done()
-        mlp = gathered_sum(ysend.at[layer], yrecv.at[layer])
-        xs[layer + 1] = (hidden + mlp).astype(bf16)
+        adder.end(sum_half)
+        xs[layer + 1] = (hidden + row_total[...]).astype(bf16)
 
     forward(0)
     dmlp[1, group_at] = cotangent[section_at]
-    grads_done = exchange(
-        1, 3, lambda peer: dmlp.at[1, group_at], lambda spot: dmlp.at[1, spot]
-    )
+    grads_share = row_share(dmlp.at[1])
+    grads_share.start()
     forward(1)
-    grads_done()
+    grads_share.end()
     dys[...] = cotangent[section_at].astype(f32)
 
     def hand_over(layer):
@@ -990,9 +1023,10 @@
         dy = dys[...]
         if layer == 0:
             dmlp[layer, group_at] = dy.astype(bf16)
-            exchange(
-                layer, 3, lambda peer: dmlp.at[layer, group_at], lambda spot: dmlp.at[layer, spot]
-            )()
+            share = row_share(dmlp.at[layer])
+            share.start()
+            share.middle()
+            share.end()
         dn2[...] = jnp.zeros_like(dn2)
 
         def columns(tile, carry):
@@ -1012,10 +1046,11 @@
 
         lax.fori_loop(0, WIN // TILE, columns, 0)
         dsend[layer] = dn2[...].astype(bf16).reshape(ZDEV, SPAN, D)
-        exchange(
-            layer, 4, lambda peer: dsend.at[layer, peer], lambda spot: drecv.at[layer, spot]
-        )()
-        grad_two = gathered_sum(dsend.at[layer], drecv.at[layer])
+        adder = row_sum(dsend.at[layer], 2 + layer)
+        adder.start()
+        adder.middle()
+        adder.end(sum_half)
+        grad_two = row_total[...]
         hidden = hid[layer]
         scale = rms_scale(hidden)
         scaled = grad_two * gain_two
@@ -1091,14 +1126,14 @@
     links.finish()
 
 
-def run_layers(tokens, cotangent, mask, cosine, sine_up, sine_down, vec, *weights):
+def run_layers(tokens, cotangent, lengths, vec, *weights):
     vmem = pl.BlockSpec(memory_space=pltpu.VMEM)
     anywhere = pl.BlockSpec(memory_space=pl.ANY)
 
     def per_micro(shape, kind):
         return jax.ShapeDtypeStruct((2,) + shape, kind)
 
-    sems = 6 + 4 + 1 + 3 * 14 + 2 * 6
+    sems = 6 + 4 + 1 + 3 * 14 + 2 * 6 + 8 * 6
 
     def scratch(shape, kind=bf16, lead=2):
         return pltpu.VMEM((lead,) + shape, kind)
@@ -1116,7 +1151,7 @@
             per_micro((SPAN, QKV + D), bf16),
             per_micro((16, 256), f32),
         ),
-        in_specs=[vmem] * 7 + [anywhere] * 5,
+        in_specs=[vmem, vmem, pl.BlockSpec(memory_space=pltpu.SMEM), vmem] + [anywhere] * 5,
         out_specs=[vmem] * 9,
         scratch_shapes=[
             scratch((ZDEV, OWN, QKV + D)),
@@ -1124,6 +1159,10 @@
             scratch((WIN, D)),
             scratch((ZDEV, 8, 384), f32),
             pltpu.VMEM((64, D), bf16),
+            pltpu.VMEM((SPAN, ROW), f32),
+            pltpu.VMEM((SPAN, 128), f32),
+            pltpu.VMEM((SPAN, 128), f32),
+            pltpu.VMEM((SPAN, 128), f32),
             scratch((SPAN, D), lead=3),
             scratch((SPAN, D)),
             scratch((SPAN, D)),
@@ -1135,12 +1174,15 @@
             scratch((2, ROW, WIN), f32),
             scratch((ROW, WIN)),
             scratch((ZDEV, SPAN, D)),
-            scratch((ZDEV, SPAN, D)),
+            scratch((SPAN // 2, D), lead=4),
+            scratch((SPAN // 2, D), lead=4),
+            scratch((SPAN, D), lead=4),
+            scratch((SPAN, D), lead=4),
+            pltpu.VMEM((SPAN, D), f32),
             pltpu.VMEM((SPAN, D), f32),
             scratch((ZDEV, SPAN, D)),
             scratch((ROW, 2 * WIN)),
             pltpu.VMEM((ROW, D), f32),
-            scratch((ZDEV, SPAN, D)),
             scratch((ZDEV, SPAN, D)),
             scratch((ZDEV, SPAN, 2 * KV_WIDTH)),
             scratch((ZDEV, SPAN, 2 * KV_WIDTH)),
@@ -1161,13 +1203,12 @@
             collective_id=3, has_side_effects=True, vmem_limit_bytes=60 * 1024 * 1024
         ),
         name="layers",
-    )(tokens, cotangent, mask, cosine, sine_up, sine_down, vec, *weights)
+    )(tokens, cotangent, lengths, vec, *weights)
 
 
 def on_device(
     tokens, cotangent, doc_lengths, w_qkv, b_qkv, w_out, w_gate, w_up, w_down, norm_attn, norm_ffn
 ):
-    section_at = lax.axis_index("section")
     group_at = lax.axis_index("group")
     vec = jnp.zeros((8 * 384,), f32)
     for member, start in ((b_qkv, 0), (norm_attn, QKV), (norm_ffn, QKV + D)):
@@ -1175,11 +1216,10 @@
         vec = lax.dynamic_update_slice(
             vec, member[0].astype(f32), (start + width * group_at,)
         )
-    lengths = lax.dynamic_index_in_dim(doc_lengths, section_at, 0, keepdims=False)[0]
     acts, input_grads, *pieces = run_layers(
         tokens[:, 0],
         cotangent[:, 0],
-        *doc_tables(lengths, group_at),
+        doc_lengths,
         vec.reshape(8, 384),
         w_qkv[0],
         w_out[0],

time: 283 us -> 264 us (0.933)
  Pallas kernels: 268 us -> 253 us
    pallas_call x1, Pallas kernels: 151 us -> 142 us  [run_layers(): pl.pallas_call(layers_kernel, out_shape=(per_micro((SPAN, D), bf16), per_...]
    pallas_call x1, Pallas kernels: 109 us -> 104 us  [share_grads(): pl.pallas_call(grads_kernel, out_shape=jax.ShapeDtypeStruct((RING, RING,...]
where the time goes in v5:
time: 264 us
  Pallas kernels  253 us (96%)
  local copies, waits for them, and re-layouts  7.35 us (3%)
  other arithmetic  2.76 us (1%)
    pallas_call x1, Pallas kernels, run_layers(): pl.pallas_call(layers_kernel, out_shape=(per_micro((SPAN, D), bf16), per_...  142 us
    pallas_call x1, Pallas kernels, share_grads(): pl.pallas_call(grads_kernel, out_shape=jax.ShapeDtypeStruct((RING, RING,...  104 us
    pallas_call x1, Pallas kernels, widen(): pl.pallas_call(widen_kernel, grid=(TILES_R // 2,), out_shape=[jax.ShapeDt...  6.51 us

profile of v5, /device:TPU:0, one launch (start us, length us, event | category | flops | bytes accessed | tf_op | source)
XLA Modules:
  0.0 263.9 jit_solution(3632247358443227049)
XLA Ops:
  0.6 0.7 convert_element_type.33
  1.3 0.7 convert_element_type.34
  2.0 0.7 convert_reduce_fusion
  2.7 0.3 dynamic_update_slice.9
  3.0 0.3 dynamic_update_slice.10
  3.3 0.2 dynamic_update_slice.11
  3.5 0.6 reshape.46.vec
  4.1 142.4 %layers.1 = (bf16[2,64,896]{2,1,0:T(8,128)(2,1)}, f32[2,64,896]{2,1,0:T(8,128)}, bf16[2,4,64,896]{3,2,1,0:T(8,128)(2,1)}, bf16[2,256,2560]{2,1,0:T(8,128)(2,1)},...) custom-call(bf16[2,64,896]{2,1,0:T(8,128)(2,1)} %bitcast.44, ...), custom_call_target="tpu_custom_call" | custom-call | tf_op jit(solution)/shard_map/layers/pallas_call | solution.py:1141
  146.5 104.2 %grads.1 = bf16[4,4,16,15232]{3,2,1,0:T(8,128)(2,1)} custom-call(bf16[512,896]{1,0:T(8,128)(2,1)} %bitcast.38, bf16[512,2560]{1,0:T(8,128)(2,1)} %bitcast.33, bf16[512,1280]{1,0:T(8,128)(2,1)} %bitcast.37, bf16[512,896]{1,0:T(8,128)(2,1)} %bitcast.39, bf16[2,64,1792]{2,1,0:T(8,128)(2,1)} %get-tuple-element.30.left_tokens, ...), custom_call_target="tpu_custom_call" | custom-call | tf_op jit(solution)/shard_map/grads/pallas_call | solution.py:460
  250.7 0.7 convert_bitcast_fusion
  251.4 0.6 fusion
  252.1 0.1 dynamic_slice.9
  252.1 0.6 broadcast_in_dim.37
  252.7 0.0 copy-start
  252.7 3.2 %copy-done = bf16[4,4,16,15232]{3,2,1,0:T(8,128)(2,1)S(1)} copy-done((bf16[4,4,16,15232]{3,2,1,0:T(8,128)(2,1)S(1)}, bf16[4,4,16,15232]{3,2,1,0:T(8,128)(2,1)}, u32[]{:S(2)}) %copy-start) | copy-done | bytes 7798808
  255.9 0.0 copy-start.2
  255.9 0.0 copy-start.1
  255.9 6.5 %widen.1 = (f32[224,4864]{1,0:T(8,128)}, f32[224,4864]{1,0:T(8,128)}, f32[224,1152]{1,0:T(8,128)}, f32[224,896]{1,0:T(8,128)}, f32[1216,896]{1,0:T(8,128)}) custom-call(bf16[16,16,15232]{2,1,0:T(8,128)(2,1)S(1)} %bitcast.31, bf16[16,16,15232]{2,1,0:T(8,128)(2,1)S(1)} %bitcast.32), custom_call_target="tpu_custom_call" | custom-call | tf_op jit(solution)/shard_map/widen/pallas_call | solution.py:512
  262.4 0.0 copy-done.2
  262.4 0.7 copy.29
  263.1 0.0 copy-done.1
  263.1 0.8 copy.30
  (2 shorter events, 0.0 us)
Async XLA Ops:
  252.7 3.2 %copy-start = (bf16[4,4,16,15232]{3,2,1,0:T(8,128)(2,1)S(1)}, bf16[4,4,16,15232]{3,2,1,0:T(8,128)(2,1)}, u32[]{:S(2)}) copy-start(bf16[4,4,16,15232]{3,2,1,0:T(8,128)(2,1)} %grads.1) | copy-start | bytes 23396356
  255.9 6.5 %copy-start.2 = (bf16[2,64,896]{2,1,0:T(8,128)(2,1)S(1)}, bf16[2,64,896]{2,1,0:T(8,128)(2,1)}, u32[]{:S(2)}) copy-start(bf16[2,64,896]{2,1,0:T(8,128)(2,1)} %get-tuple-element.24) | copy-start | bytes 688132
  255.9 7.2 %copy-start.1 = (f32[2,64,896]{2,1,0:T(8,128)S(1)}, f32[2,64,896]{2,1,0:T(8,128)}, u32[]{:S(2)}) copy-start(f32[2,64,896]{2,1,0:T(8,128)} %get-tuple-element.25) | copy-start | bytes 1376260

commit v6 on v5

--- a/solution.py
+++ b/solution.py
@@ -1049,6 +1049,8 @@
         adder = row_sum(dsend.at[layer], 2 + layer)
         adder.start()
         adder.middle()
+        kv = kvs[layer].reshape(ROW, 2 * KV_WIDTH)
+        keys, values = spread(kv[:, :KV_WIDTH]), spread(kv[:, KV_WIDTH:])
         adder.end(sum_half)
         grad_two = row_total[...]
         hidden = hid[layer]
@@ -1060,10 +1062,8 @@
         dt = dhid.astype(bf16)
         rights[layer, :, QKV:] = dt
         do = dot_nt(dt, joint_cols(layer, QKV, QKV + D)).astype(bf16)
-        kv = kvs[layer].reshape(ROW, 2 * KV_WIDTH)
-        keys, values = spread(kv[:, :KV_WIDTH]), spread(kv[:, KV_WIDTH:])
         queries = qs[layer]
-        dqs, dks, dvs, at_row = [], [], [], 0
+        dscores, dks, dvs, at_row = [], [], [], 0
         for kind, (pairs, _) in enumerate(KINDS):
             count = SPAN * len(pairs)
             prob = probs[layer, at_row : at_row + count]
@@ -1071,24 +1071,34 @@
             dprob = dot_nt(grad, values[kind])
             inner = jnp.sum(prob * dprob, axis=-1, keepdims=True)
             dscore = (prob * (dprob - inner)).astype(bf16)
-            dqs.append(jnp.dot(dscore, keys[kind], preferred_element_type=f32))
+            dscores.append(dscore)
             dks.append(dot_tn(dscore, stack_pairs(queries, kind)))
             dvs.append(dot_tn(prob.astype(bf16), grad))
             at_row += count
         dkv = jnp.concatenate([unspread(dks) * SCALE, unspread(dvs)], axis=1)
         dkvsend[layer] = dkv.astype(bf16).reshape(ZDEV, SPAN, 2 * KV_WIDTH)
-        exchange(
+        done = exchange(
             layer, 5, lambda peer: dkvsend.at[layer, peer], lambda spot: dkvrecv.at[layer, spot]
-        )()
-        dkv = gathered_sum(dkvsend.at[layer], dkvrecv.at[layer])
-        dqk = jnp.concatenate([join_pairs(dqs) * SCALE, dkv[:, :KV_WIDTH]], axis=1)
-        dqk = turn(dqk, cosine[...], sine_up[...], sine_down[...], -1.0)
-        dqkv = jnp.concatenate([dqk, dkv[:, KV_WIDTH:]], axis=1).astype(bf16)
-        rights[layer, :, :QKV] = dqkv
+        )
+        dqs = [
+            jnp.dot(dscore, member, preferred_element_type=f32)
+            for dscore, member in zip(dscores, keys)
+        ]
+        dq = turn(join_pairs(dqs) * SCALE, cosine[...], sine_up[...], sine_down[...], -1.0)
+        dq = dq.astype(bf16)
+        rights[layer, :, :D] = dq
         lefts[layer, :, :D] = n1s[layer]
         lefts[layer, :, D:] = ctx[layer]
-        bias_term = jnp.sum(dqkv.astype(f32), axis=0, keepdims=True)
-        grad_one = dot_nt(dqkv, joint_cols(layer, 0, QKV))
+        grad_one = dot_nt(dq, joint_cols(layer, 0, D))
+        done()
+        dkv = gathered_sum(dkvsend.at[layer], dkvrecv.at[layer])
+        dk = turn(dkv[:, :KV_WIDTH], cosine[...], sine_up[...], sine_down[...], -1.0)
+        dkv = jnp.concatenate([dk, dkv[:, KV_WIDTH:]], axis=1).astype(bf16)
+        rights[layer, :, D:QKV] = dkv
+        grad_one = grad_one + dot_nt(dkv, joint_cols(layer, D, QKV))
+        bias_term = jnp.concatenate(
+            [jnp.sum(part.astype(f32), axis=0, keepdims=True) for part in (dq, dkv)], axis=1
+        )
         x = xs[layer].astype(f32)
         scale = rms_scale(x)
         scaled = grad_one * gain_one

time: 264 us -> 264 us (level)
  no operation moved by 1% of the time
where the time goes in v6:
time: 264 us
  Pallas kernels  253 us (96%)
  local copies, waits for them, and re-layouts  7.35 us (3%)
  other arithmetic  2.76 us (1%)
    pallas_call x1, Pallas kernels, run_layers(): pl.pallas_call(layers_kernel, out_shape=(per_micro((SPAN, D), bf16), per_...  142 us
    pallas_call x1, Pallas kernels, share_grads(): pl.pallas_call(grads_kernel, out_shape=jax.ShapeDtypeStruct((RING, RING,...  104 us
    pallas_call x1, Pallas kernels, widen(): pl.pallas_call(widen_kernel, grid=(TILES_R // 2,), out_shape=[jax.ShapeDt...  6.51 us

profile of v6, /device:TPU:0, one launch (start us, length us, event | category | flops | bytes accessed | tf_op | source)
XLA Modules:
  0.0 263.8 jit_solution(680017381140079993)
XLA Ops:
  0.6 0.7 convert_element_type.33
  1.3 0.7 convert_element_type.34
  2.0 0.7 convert_reduce_fusion
  2.7 0.3 dynamic_update_slice.9
  3.0 0.3 dynamic_update_slice.10
  3.3 0.2 dynamic_update_slice.11
  3.5 0.6 reshape.46.vec
  4.1 142.3 %layers.1 = (bf16[2,64,896]{2,1,0:T(8,128)(2,1)}, f32[2,64,896]{2,1,0:T(8,128)}, bf16[2,4,64,896]{3,2,1,0:T(8,128)(2,1)}, bf16[2,256,2560]{2,1,0:T(8,128)(2,1)},...) custom-call(bf16[2,64,896]{2,1,0:T(8,128)(2,1)} %bitcast.44, ...), custom_call_target="tpu_custom_call" | custom-call | tf_op jit(solution)/shard_map/layers/pallas_call | solution.py:1151
  146.4 104.2 %grads.1 = bf16[4,4,16,15232]{3,2,1,0:T(8,128)(2,1)} custom-call(bf16[512,896]{1,0:T(8,128)(2,1)} %bitcast.38, bf16[512,2560]{1,0:T(8,128)(2,1)} %bitcast.33, bf16[512,1280]{1,0:T(8,128)(2,1)} %bitcast.37, bf16[512,896]{1,0:T(8,128)(2,1)} %bitcast.39, bf16[2,64,1792]{2,1,0:T(8,128)(2,1)} %get-tuple-element.30.left_tokens, ...), custom_call_target="tpu_custom_call" | custom-call | tf_op jit(solution)/shard_map/grads/pallas_call | solution.py:460
  250.6 0.7 convert_bitcast_fusion
  251.3 0.6 fusion
  251.9 0.1 dynamic_slice.9
  252.0 0.6 broadcast_in_dim.37
  252.6 0.0 copy-start
  252.6 3.2 %copy-done = bf16[4,4,16,15232]{3,2,1,0:T(8,128)(2,1)S(1)} copy-done((bf16[4,4,16,15232]{3,2,1,0:T(8,128)(2,1)S(1)}, bf16[4,4,16,15232]{3,2,1,0:T(8,128)(2,1)}, u32[]{:S(2)}) %copy-start) | copy-done | bytes 7798808
  255.8 0.0 copy-start.2
  255.8 0.0 copy-start.1
  255.8 6.5 %widen.1 = (f32[224,4864]{1,0:T(8,128)}, f32[224,4864]{1,0:T(8,128)}, f32[224,1152]{1,0:T(8,128)}, f32[224,896]{1,0:T(8,128)}, f32[1216,896]{1,0:T(8,128)}) custom-call(bf16[16,16,15232]{2,1,0:T(8,128)(2,1)S(1)} %bitcast.31, bf16[16,16,15232]{2,1,0:T(8,128)(2,1)S(1)} %bitcast.32), custom_call_target="tpu_custom_call" | custom-call | tf_op jit(solution)/shard_map/widen/pallas_call | solution.py:512
  262.3 0.0 copy-done.2
  262.3 0.7 copy.29
  263.0 0.0 copy-done.1
  263.0 0.8 copy.30
  (2 shorter events, 0.0 us)
Async XLA Ops:
  252.6 3.2 %copy-start = (bf16[4,4,16,15232]{3,2,1,0:T(8,128)(2,1)S(1)}, bf16[4,4,16,15232]{3,2,1,0:T(8,128)(2,1)}, u32[]{:S(2)}) copy-start(bf16[4,4,16,15232]{3,2,1,0:T(8,128)(2,1)} %grads.1) | copy-start | bytes 23396356
  255.8 6.5 %copy-start.2 = (bf16[2,64,896]{2,1,0:T(8,128)(2,1)S(1)}, bf16[2,64,896]{2,1,0:T(8,128)(2,1)}, u32[]{:S(2)}) copy-start(bf16[2,64,896]{2,1,0:T(8,128)(2,1)} %get-tuple-element.24) | copy-start | bytes 688132
  255.8 7.2 %copy-start.1 = (f32[2,64,896]{2,1,0:T(8,128)S(1)}, f32[2,64,896]{2,1,0:T(8,128)}, u32[]{:S(2)}) copy-start(f32[2,64,896]{2,1,0:T(8,128)} %get-tuple-element.25) | copy-start | bytes 1376260
